TPU v7x, 32 devices: a whole 2x2x4 slice. The times are simulated.
32 devices in a mesh: row: 16 (over z, y, core), col: 2 (over x).
Axes of the slice: x: 2, y: 2, z: 4, core: 2. Of those that a mesh axis runs over, the one named last changes fastest.
Arguments:
- velocity: float32 [3, 16, 1024, 1024], P(None, None, 'row', 'col'), may hold values from -6 to 6
- dy_op: bfloat16 [1024, 1024], replicated, may hold values from -0.1875 to 0.1875
- dz_op: bfloat16 [1024, 1024], replicated, may hold values from -0.1875 to 0.1875
- node_force: float32 [3, 256], P(None, ('row', 'col')), may hold values from -6 to 6
- node_cell: int32 [3, 256], P(None, ('row', 'col')), may hold values from 0 to 1023, as said below
Outputs:
- tendency: float32 [3, 16, 1024, 1024], P(None, None, 'row', 'col')
Inputs may be any that keep to these rules, and one draw needn't show every extreme that they name: `node_cell`: the nodes of the block held by device (r, c) of the mesh have their z coordinate in the c-th of the 2 equal ranges of z; x lies below 16, y below 1024.
All inputs are finite; a program needn't handle non-finite values.
Results may differ from a plain program's by a relative error of at most 0.0029.
Values sent between devices are 32-bit elements; how exact they have to be, the bound alone decides.
No kernel may reach another device: no remote copies, remote signals or barrier semaphores. Data moves between devices by JAX's collectives and lax.ppermute only.
A program may use at most 384 MiB of HBM per device.

v0:
```python
import jax
import jax.numpy as jnp
from jax import lax
from jax.sharding import PartitionSpec as P


def y_terms(pencil_slab, dy_op):
    transport_array = pencil_slab[1]
    result_list = []
    for comp in range(3):
        rounded = pencil_slab[comp].astype(jnp.bfloat16)
        gradient_in_y = jnp.einsum(
            "ab,xbz->xaz", dy_op, rounded, preferred_element_type=jnp.float32
        )
        result_list.append(-(transport_array * gradient_in_y))
    return jnp.stack(result_list)


def z_terms(pencil_slab, dz_op):
    transport_array = pencil_slab[2]
    result_list = []
    for comp in range(3):
        rounded = pencil_slab[comp].astype(jnp.bfloat16)
        gradient_in_z = jnp.einsum(
            "xyb,ab->xya", rounded, dz_op, preferred_element_type=jnp.float32
        )
        result_list.append(-(transport_array * gradient_in_z))
    return jnp.stack(result_list)


def per_device(velocity, dy_op, dz_op, node_force, node_cell):
    lines_y = lax.all_to_all(velocity, "row", split_axis=1, concat_axis=2, tiled=True)
    along_y = y_terms(lines_y, dy_op)
    summed = along_y + lax.all_to_all(
        z_terms(lax.all_to_all(lines_y, "col", split_axis=2, concat_axis=3, tiled=True), dz_op),
        "col",
        split_axis=3,
        concat_axis=2,
        tiled=True,
    )
    tendency = lax.all_to_all(summed, "row", split_axis=2, concat_axis=1, tiled=True)
    forces, node_cells = (
        lax.all_gather(node_force, "row", axis=1, tiled=True),
        lax.all_gather(node_cell, "row", axis=1, tiled=True),
    )
    y_direction_width = tendency.shape[2]
    width_z = tendency.shape[3]
    row_pos = lax.axis_index("row")
    col_pos = lax.axis_index("col")
    local_y = node_cells[1] - row_pos * y_direction_width
    local_z = node_cells[2] - col_pos * width_z
    owned_node = (
        (local_y >= 0) & (local_y < y_direction_width) & (local_z >= 0) & (local_z < width_z)
    )
    flat_index = jnp.where(
        owned_node, (node_cells[0] * y_direction_width + local_y) * width_z + local_z, 0
    ).astype(jnp.int32)
    pushed = jnp.where(owned_node[None], forces, jnp.float32(0.0))
    flat_out = tendency.reshape(3, -1).at[:, flat_index].add(pushed)
    return flat_out.reshape(tendency.shape)


def solution(mesh):
    return jax.shard_map(
        per_device,
        mesh=mesh,
        in_specs=(
            P(None, None, "row", "col"),
            P(),
            P(),
            P(None, ("row", "col")),
            P(None, ("row", "col")),
        ),
        out_specs=P(None, None, "row", "col"),
        check_vma=False,
    )
```

profile of v0, /device:TPU:8, one launch (start us, length us, event | category | flops | bytes accessed | tf_op | source)
XLA Modules:
  0.0 609.1 jit_solution(5789272677871844165)
XLA Ops:
  0.0 0.0 copy-start
  0.0 3.6 copy.59
  3.6 143.3 %all_to_all.54 = f32[3,16,64,512]{3,2,0,1:T(8,128)S(1)} all-to-all(f32[3,16,64,512]{3,2,0,1:T(8,128)S(1)} %copy.59), channel_id=1, replica_groups=mesh['row'=16,'col'=2] {'row'}, dimensions={1} | all-to-all | bytes 12582912 | tf_op jit(solution)/shard_map/all_to_all | solution.py:32
  147.0 0.0 copy-start.2
  147.0 1.2 copy.60
  148.2 2.0 copy-done.2
  150.2 0.0 copy-start.3
  150.2 14.2 %copy.65 = f32[3,1,1024,512]{3,1,0,2:T(1,128)S(1)} copy(f32[3,1,1024,512]{3,2,0,1:T(8,128)S(1)} %bitcast.90) | data formatting | bytes 12582912 | tf_op jit(solution)/shard_map/all_to_all | solution.py:32
  164.4 0.0 copy-done.3
  164.4 73.8 %all_to_all.55 = f32[3,1,1024,512]{3,1,0,2:T(1,128)S(1)} all-to-all(f32[3,1,1024,512]{3,1,0,2:T(1,128)S(1)} %copy.65), channel_id=1, replica_groups=mesh['row'=16,'col'=2] {'col'}, dimensions={2} | all-to-all | bytes 12582912 | tf_op jit(solution)/shard_map/all_to_all | solution.py:35
  238.2 0.8 copy.66
  239.1 1.5 slice.52
  240.6 0.4 convert.9
  241.0 1.2 fusion.9
  242.2 2.3 copy.68
  244.5 3.2 copy.67
  247.7 0.5 copy.77
  248.2 0.0 copy-start.5
  248.2 0.0 copy-done
  248.2 0.0 copy-start.8
  248.2 2.6 negate_bitcast_fusion
  250.9 0.0 copy-done.5
  250.9 0.0 copy-done.8
  250.9 2.6 negate_bitcast_fusion.2
  253.5 1.3 copy.69
  254.8 0.0 copy-start.6
  254.8 0.0 copy-start.7
  254.8 3.4 negate_bitcast_fusion.1
  258.2 0.0 copy-done.6
  258.2 0.0 copy-done.7
  258.2 3.3 pad_maximum_fusion
  261.5 16.1 %copy.70 = f32[3,1,512,1024]{2,1,0,3:T(1,128)} copy(f32[3,1,512,1024]{3,2,1,0:T(8,128)} %pad_maximum_fusion) | data formatting | bytes 12582912 | tf_op jit(solution)/shard_map/stack | solution.py:28
  277.6 6.3 %all-to-all-start.2 = ((f32[3,1,512,1024]{2,1,0,3:T(1,128)}), f32[3,1,512,1024]{2,1,0,3:T(1,128)}, u32[]{:S(2)}, u32[]{:S(2)}) async-start(f32[3,1,512,1024]{2,1,0,3:T(1,128)} %copy.70), calls=%async_computation.2 | async-start | bytes 12582912 | tf_op jit(solution)/shard_map/all_to_all | solution.py:34
  283.8 1.7 slice.67
  285.6 1.8 slice.49
  287.4 2.0 copy.61
  289.4 3.3 convert.8
  292.7 0.0 copy-start.4
  292.7 0.0 copy-start.11
  292.7 0.2 fusion.8
  292.9 1.4 copy-done.4
  294.3 0.6 copy-done.11
  294.9 1.3 fusion.1
  296.2 2.7 fusion.3
  298.9 2.7 fusion.5
  301.6 52.4 %all-to-all-done.2 = f32[3,1,512,1024]{2,1,0,3:T(1,128)} async-done(((f32[3,1,512,1024]{2,1,0,3:T(1,128)}), f32[3,1,512,1024]{2,1,0,3:T(1,128)}, u32[]{:S(2)}, u32[]{:S(2)}) %all-to-all-start.2) | async-done | bytes 6291488 | tf_op jit(solution)/shard_map/all_to_all | solution.py:34
  353.9 6.3 %copy.71 = f32[3,1,512,1024]{2,3,0,1:T(8,128)} copy(f32[3,1,512,1024]{2,1,0,3:T(1,128)} %all-to-all-done.2) | data formatting | bytes 12582912 | tf_op jit(solution)/shard_map/all_to_all | solution.py:34
  360.3 10.3 %copy.72 = f32[3,1,2,512,512]{3,2,4,0,1:T(2,128)} copy(f32[3,1,2,512,512]{3,4,2,0,1:T(8,128)} %bitcast.95) | data formatting | bytes 12582912 | tf_op jit(solution)/shard_map/all_to_all | solution.py:34
  370.6 9.2 %all_to_all.48 = f32[3,1,1024,512]{2,3,1,0:T(8,128)} reshape(f32[3,1,2,512,512]{3,2,4,0,1:T(2,128)} %copy.72) | data formatting | bytes 12582912 | tf_op jit(solution)/shard_map/all_to_all | solution.py:34
  379.7 6.6 %maximum_add_fusion = f32[3,1,1024,512]{2,3,1,0:T(8,128)} fusion(f32[3,1,1024,512]{2,3,1,0:T(8,128)} %all_to_all.48, f32[1,1,1024,512]{2,3,1,0:T(8,128)S(1)} %fusion.1, f32[1,1,1024,512]{2,3,1,0:T(8,128)} %fusion.3, f32[1,1,1024,512]{2,3,1,0:T(8,128)} %fusion.5), kind=kLoop, calls=%fused_computation.1 | loop fusion | flops 4718592 | bytes 18874368 | tf_op jit(solution)/shard_map/add | solution.py:34
  386.4 16.0 %copy.73 = f32[3,1,1024,512]{3,1,0,2:T(1,128)} copy(f32[3,1,1024,512]{2,3,1,0:T(8,128)} %maximum_add_fusion) | data formatting | bytes 12582912 | tf_op jit(solution)/shard_map/add | solution.py:34
  402.3 4.9 all-to-all-start.3
  407.3 0.0 copy-done.9
  407.3 147.6 %all-gather.1 = f32[16,8,3]{1,2,0:T(4,128)S(1)} all-gather(f32[1,8,3]{1,2,0:T(4,128)S(1)} %bitcast.108), channel_id=1, replica_groups=mesh['row'=16,'col'=2] {'row'}, dimensions={0}, use_global_device_ids=true | all-gather | bytes 1632 | tf_op jit(solution)/shard_map/all_gather | solution.py:43
  554.8 0.1 reshape.248
  554.9 0.0 copy-done.10
  554.9 16.8 %all-gather = s32[16,8,3]{1,2,0:T(4,128)S(1)} all-gather(s32[1,8,3]{1,2,0:T(4,128)S(1)} %bitcast.109), channel_id=1, replica_groups=mesh['row'=16,'col'=2] {'row'}, dimensions={0}, use_global_device_ids=true | all-gather | bytes 1632 | tf_op jit(solution)/shard_map/all_gather | solution.py:44
  571.8 0.1 reshape.246
  571.9 0.0 all-to-all-done.3
  571.9 3.7 copy.81
  575.6 7.5 %copy.78 = f32[1,3,1024,512]{3,1,2,0:T(4,128)} copy(f32[1,3,1024,512]{3,2,1,0:T(8,128)S(1)} %bitcast.96) | data formatting | bytes 12582912
  583.1 17.7 %scatter_fusion = f32[3,524288]{1,0:T(4,128)} fusion(f32[3,524288]{1,0:T(4,128)} %bitcast.91, s32[128]{0:T(128)S(1)} %get-tuple-element.5, f32[128,3]{0,1:T(4,128)S(1)} %broadcast_select_fusion), kind=kCustom, calls=%fused_computation | custom fusion | flops 384 | bytes 5120 | tf_op jit(solution)/shard_map/scatter-add | solution.py:59
  600.8 8.3 %copy.79 = f32[1,3,1024,512]{3,2,1,0:T(8,128)} copy(f32[1,3,1024,512]{3,1,2,0:T(4,128)} %bitcast.92) | data formatting | bytes 12582912
  609.1 0.0 copy-done.1
  (7 shorter events, 0.0 us)
Async XLA Ops:
  0.0 248.2 %copy-start = (bf16[1024,1024]{1,0:T(8,128)(2,1)S(1)}, bf16[1024,1024]{1,0:T(8,128)(2,1)}, u32[]{:S(2)}) copy-start(bf16[1024,1024]{1,0:T(8,128)(2,1)} %param.7) | copy-start | bytes 6291460
  147.0 3.2 copy-start.2
  150.2 14.2 %copy-start.3 = (f32[3,16,64,512]{3,2,1,0:T(8,128)}, f32[3,16,64,512]{3,2,1,0:T(8,128)S(1)}, u32[]{:S(2)}) copy-start(f32[3,16,64,512]{3,2,1,0:T(8,128)S(1)} %copy.60) | copy-start | bytes 18874372
  248.2 2.7 copy-start.5
  248.2 2.7 copy-start.8
  254.8 3.4 copy-start.6
  254.8 3.4 copy-start.7
  277.6 76.4 %all-to-all-start.2 = ((f32[3,1,512,1024]{2,1,0,3:T(1,128)}), f32[3,1,512,1024]{2,1,0,3:T(1,128)}, u32[]{:S(2)}, u32[]{:S(2)}) async-start(f32[3,1,512,1024]{2,1,0,3:T(1,128)} %copy.70), calls=%async_computation.2 | async-start | bytes 12582912 | tf_op jit(solution)/shard_map/all_to_all | solution.py:34
  292.7 1.6 copy-start.4
  292.7 2.2 copy-start.11
  402.3 4.9 copy-start.9
  402.3 152.6 %copy-start.10 = (s32[3,8]{1,0:T(4,128)S(1)}, s32[3,8]{1,0:T(4,128)}, u32[]{:S(2)}) copy-start(s32[3,8]{1,0:T(4,128)} %param.9) | copy-start | bytes 292
  402.3 169.6 %all-to-all-start.3 = ((f32[3,1,1024,512]{3,1,0,2:T(1,128)}), f32[3,1,1024,512]{3,1,0,2:T(1,128)}, u32[]{:S(2)}, u32[]{:S(2)}) async-start(f32[3,1,1024,512]{3,1,0,2:T(1,128)} %copy.73), calls=%async_computation.3 | async-start | bytes 12582912 | tf_op jit(solution)/shard_map/all_to_all | solution.py:41
  600.8 8.3 %copy-start.1 = (bf16[1024,1024]{1,0:T(8,128)(2,1)S(1)}, bf16[1024,1024]{1,0:T(8,128)(2,1)}, u32[]{:S(2)}) copy-start(bf16[1024,1024]{1,0:T(8,128)(2,1)} %param.7) | copy-start | bytes 6291460
where the time goes:
time: 615 us; the launch traced here: 609 us
  blocking collectives  382 us (62%)
  local copies, waits for them, and re-layouts  117 us (19%)
  waiting for transfers between devices  52.4 us (9%)
  other arithmetic  31.3 us (5%)
  matrix products  15.3 us (2%)
  starting transfers between devices  11.2 us (2%)
    all_gather x1, blocking collectives, per_device(): lax.all_gather(node_force, 'row', axis=1, tiled=True)  148 us
    all_to_all x1, blocking collectives, per_device(): lax.all_to_all(velocity, 'row', split_axis=1, concat_axis=2, tiled=True)  143 us
    all_to_all x1, blocking collectives, per_device(): lax.all_to_all(lines_y, 'col', split_axis=2, concat_axis=3, tiled=True)  73.8 us
    all_to_all x1, waiting for transfers between devices, per_device(): lax.all_to_all(z_terms(lax.all_to_all(lines_y, 'col', split_axis=2, conca...  52.4 us
    all_to_all x3, local copies, waits for them, and re-layouts, per_device(): lax.all_to_all(z_terms(lax.all_to_all(lines_y, 'col', split_axis=2, conca...  25.8 us
    unnamed x30, local copies, waits for them, and re-layouts  24.2 us
    scatter-add x1, other arithmetic, per_device(): flat_out = tendency.reshape(3, -1).at[:, flat_index].add(pushed)  17.7 us
    all_gather x1, blocking collectives, per_device(): lax.all_gather(node_cell, 'row', axis=1, tiled=True)  16.8 us
  transfers between devices with their start and end apart: 2, of which 1 were waited for; matrix products, arithmetic and copies ran while one was open for 3% of the time, Pallas kernels for 0%

commit v1 on v0

v1 whole, which is shorter than its diff:
```python
import functools

import jax
import jax.numpy as jnp
from jax import lax
from jax.experimental import pallas as pl
from jax.experimental.pallas import tpu as pltpu
from jax.sharding import PartitionSpec as P

VMEM = 60 << 20
CHUNKS = ((0, 2), (2, 1))
SHARES = (6, 2, 4)
NODE_STEPS = (2, 2)


def y_kernel(op_ref, lines_ref, grad_ref):
    shape = lines_ref.shape
    lines = lines_ref[...].reshape(shape[0] * shape[3], shape[4]).astype(jnp.bfloat16)
    grad = jnp.dot(op_ref[...], lines, preferred_element_type=jnp.float32)
    grad_ref[...] = grad.reshape(shape)


def y_gradient(op, lines):
    rows, comps, planes, height, width = lines.shape
    tile = min(width, 256)
    block = pl.BlockSpec((rows, 1, 1, height, tile), lambda c, p, j: (0, c, p, 0, j))
    flops = 2 * op.shape[0] * op.shape[1] * comps * planes * width
    return pl.pallas_call(
        y_kernel,
        grid=(comps, planes, width // tile),
        in_specs=[pl.BlockSpec(op.shape, lambda c, p, j: (0, 0)), block],
        out_specs=block,
        out_shape=jax.ShapeDtypeStruct(lines.shape, jnp.float32),
        compiler_params=pltpu.CompilerParams(vmem_limit_bytes=VMEM),
        cost_estimate=pl.CostEstimate(
            flops=flops, bytes_accessed=8 * lines.size + 2 * op.size, transcendentals=0
        ),
        name="y_gradient",
    )(op, lines)


def in_place(kernel, out, shape, name, grid, args, specs, out_spec, flops, size):
    kept = [] if out is None else [out]
    return pl.pallas_call(
        kernel,
        grid=grid,
        in_specs=specs + [pl.BlockSpec(memory_space=pl.ANY)] * len(kept),
        out_specs=out_spec,
        out_shape=jax.ShapeDtypeStruct(shape, jnp.float32),
        input_output_aliases={len(specs): 0} if kept else {},
        compiler_params=pltpu.CompilerParams(vmem_limit_bytes=VMEM),
        cost_estimate=pl.CostEstimate(flops=flops, bytes_accessed=size, transcendentals=0),
        name=name,
    )(*args, *kept)


def z_kernel(n_blocks, carrier_ref, *refs):
    field_refs, op_refs, out_ref = refs[:n_blocks], refs[n_blocks : 2 * n_blocks], refs[-1]
    planes, height, width = out_ref.shape
    grad = None
    for field_ref, op_ref in zip(field_refs, op_refs):
        field = field_ref[...].reshape(planes * height, width).astype(jnp.bfloat16)
        part = lax.dot_general(
            field, op_ref[...], (((1,), (1,)), ((), ())), preferred_element_type=jnp.float32
        )
        grad = part if grad is None else grad + part
    out_ref[...] = -(carrier_ref[...] * grad.reshape(out_ref.shape))


def z_terms(out, flat, planes, start, others, ops):
    count, height, width = others[0].shape if others else flat.shape
    tile = 4
    first, cycle, carried = start // tile, planes // tile, 2 * planes // tile
    here = pl.BlockSpec((tile, height, width), lambda i: (first + i, 0, 0))
    carrier = pl.BlockSpec((tile, height, width), lambda i: (carried + (first + i) % cycle, 0, 0))
    field = pl.BlockSpec((tile, height, width), lambda i: (i, 0, 0))
    op = pl.BlockSpec((width, width), lambda i: (0, 0))
    size = count * height * width
    return in_place(
        functools.partial(z_kernel, 1 + len(others)),
        out,
        flat.shape,
        "z_terms",
        (count // tile,),
        [flat, flat, *others, *ops],
        [carrier, here] + [field] * len(others) + [op] * len(ops),
        here,
        2 * size * width * len(ops),
        4 * size * (2 + len(ops)),
    )


def node_kernel(planes, node_ref, force_ref, base_ref, out_ref):
    tile, height, width = out_ref.shape
    out_ref[...] = base_ref[...]
    lane = lax.broadcasted_iota(jnp.int32, (1, width), 1)
    start = pl.program_id(0) * tile
    comp, begin = start // planes, start % planes

    def add_node(n, _):
        x, y, z = node_ref[0, n] - begin, node_ref[1, n], node_ref[2, n]

        @pl.when((x >= 0) & (x < tile) & (y >= 0) & (y < height) & (z >= 0) & (z < width))
        def _():
            row = out_ref[x, pl.ds(y, 1), :]
            out_ref[x, pl.ds(y, 1), :] = row + jnp.where(lane == z, force_ref[comp, n], 0.0)

        return 0

    lax.fori_loop(0, node_ref.shape[1], add_node, 0)


def add_nodes(out, planes, nodes, forces):
    total, height, width = out.shape
    tile = planes // 2
    block = pl.BlockSpec((tile, height, width), lambda i: (i, 0, 0))
    smem = pl.BlockSpec(memory_space=pltpu.SMEM)
    return pl.pallas_call(
        functools.partial(node_kernel, planes),
        grid=(total // tile,),
        in_specs=[smem, smem, block],
        out_specs=block,
        out_shape=jax.ShapeDtypeStruct(out.shape, jnp.float32),
        input_output_aliases={2: 0},
        compiler_params=pltpu.CompilerParams(vmem_limit_bytes=VMEM),
        cost_estimate=pl.CostEstimate(flops=out.size, bytes_accessed=8 * out.size, transcendentals=0),
        name="add_nodes",
    )(nodes, forces, out)


def combine_kernel(base_ref, carrier_ref, grad_ref, out_ref):
    out_ref[...] = base_ref[...] - carrier_ref[...] * grad_ref[:, 0]


def combine(out, flat, planes, grad, start):
    total, height, width = out.shape
    comps = grad.shape[1]
    tile = planes // 4
    per = planes // tile
    first = start * per
    here = pl.BlockSpec((tile, height, width), lambda c, i: (first + c * per + i, 0, 0))
    carrier = pl.BlockSpec((tile, height, width), lambda c, i: (per + i, 0, 0))
    return pl.pallas_call(
        combine_kernel,
        grid=(comps, per),
        in_specs=[here, carrier, pl.BlockSpec((tile, 1, height, width), lambda c, i: (i, c, 0, 0))],
        out_specs=here,
        out_shape=jax.ShapeDtypeStruct(out.shape, jnp.float32),
        input_output_aliases={0: 0},
        compiler_params=pltpu.CompilerParams(vmem_limit_bytes=VMEM),
        cost_estimate=pl.CostEstimate(
            flops=2 * grad.size, bytes_accessed=16 * grad.size, transcendentals=0
        ),
        name="combine",
    )(out, flat, grad)


def solution(mesh):
    n_row, n_col = mesh.shape["row"], mesh.shape["col"]

    def exchange(block):
        return lax.all_to_all(block, "row", split_axis=0, concat_axis=0, tiled=True)

    def per_device(velocity, dy_op, dz_op, node_force, node_cell):
        comps, planes, height, width = velocity.shape
        row_pos, col_pos = lax.axis_index("row"), lax.axis_index("col")
        total = comps * planes
        n_chunks = len(CHUNKS)
        n_phases = 2 * n_chunks

        def gather_step(known, step):
            moved = lax.ppermute(known, "row", [(i, i ^ step) for i in range(n_row)])
            return jnp.concatenate([known, moved], axis=1)

        def chunk_of(velocity, k):
            first, count = CHUNKS[k]
            block = velocity[first : first + count].swapaxes(0, 1)
            return block.reshape(n_row, planes // n_row, count, height, width).swapaxes(1, 2)

        def piece_of(velocity, k):
            unit = total // sum(SHARES)
            begin, end = unit * sum(SHARES[:k]), unit * sum(SHARES[: k + 1])
            return velocity.reshape(total, height, width)[begin:end]

        own_rows = lax.dynamic_slice_in_dim(dz_op, col_pos * width, width, 0)
        ops = [
            lax.dynamic_slice_in_dim(own_rows, (col_pos + s) % n_col * width, width, 1)
            for s in range(n_col)
        ]
        known = jnp.concatenate([node_force, node_cell.astype(jnp.float32)])
        steps = [1 << k for k in range(n_row.bit_length() - 1)][::-1]

        chunks = [chunk_of(velocity, 0)]
        pieces = [piece_of(velocity, 0)]
        grads = [None] * n_chunks
        out, start = None, 0
        for phase in range(n_phases):
            moved = exchange(chunks[phase])
            others = None
            if phase < len(SHARES):
                others = [
                    lax.ppermute(pieces[phase], "col", [(i, (i - s) % n_col) for i in range(n_col)])
                    for s in range(1, n_col)
                ]
            if phase < len(NODE_STEPS):
                last = phase == len(NODE_STEPS) - 1
                for _ in range(len(steps) if last else NODE_STEPS[phase]):
                    known = gather_step(known, steps.pop(0))
            if phase + 1 < n_chunks:
                chunks.append(chunk_of(velocity, phase + 1))
            if phase + 1 < len(SHARES):
                pieces.append(piece_of(velocity, phase + 1))
            if 1 <= phase <= n_chunks:
                chunks.append(y_gradient(dy_op, arrived))
            if phase > 0 and start < total:
                flat = velocity.reshape(total, height, width)
                out = z_terms(out, flat, planes, start, arriving, ops)
                start += arriving[0].shape[0]
            if phase == n_phases - 1:
                break
            arrived, arriving = moved, others
            if phase >= n_chunks:
                grads[phase - n_chunks] = moved
            state = velocity, chunks, pieces, arrived, arriving, grads, out, known
            state = lax.optimization_barrier(state)
            velocity, chunks, pieces, arrived, arriving, grads, out, known = state
        grads[-1] = moved
        flat = velocity.reshape(total, height, width)
        origin = jnp.stack([0 * row_pos, row_pos * height, col_pos * width])
        cells = known[comps:].astype(jnp.int32) - origin[:, None].astype(jnp.int32)
        out = add_nodes(out, planes, cells, known[:comps])
        for (first, count), grad in zip(CHUNKS, grads):
            grad = grad.swapaxes(1, 2).reshape(planes, count, height, width)
            out = combine(out, flat, planes, grad, first)
        return out.reshape(velocity.shape)

    return jax.shard_map(
        per_device,
        mesh=mesh,
        in_specs=(
            P(None, None, "row", "col"),
            P(),
            P(),
            P(None, ("row", "col")),
            P(None, ("row", "col")),
        ),
        out_specs=P(None, None, "row", "col"),
        check_vma=False,
    )
```

time: 615 us -> 319 us (0.52)
  blocking collectives: 382 us -> 0 us
  waiting for transfers between devices: 52.4 us -> 199 us
  local copies, waits for them, and re-layouts: 117 us -> 18.2 us
  Pallas kernels: 0 us -> 60.9 us
  other arithmetic: 31.3 us -> 1.05 us
  starting transfers between devices: 11.2 us -> 36.8 us
  matrix products: 15.3 us -> 0 us
    all_to_all x2 -> x0, blocking collectives: 217 us -> none  [the longest x1 143 us: per_device(): lax.all_to_all(velocity, 'row', split_axis=1, concat_axis=2, tiled=True)]
    all_gather x2 -> x0, blocking collectives: 164 us -> none  [the longest x1 148 us: per_device(): lax.all_gather(node_force, 'row', axis=1, tiled=True)]
    ppermute x0 -> x7, waiting for transfers between devices: none -> 124 us  [the longest x4 84.6 us: gather_step(): moved = lax.ppermute(known, 'row', [(i, i ^ step) for i in range(n_row)])]
    pallas_call x0 -> x8, Pallas kernels: none -> 60.9 us  [the longest x1 19.1 us: add_nodes(): pl.pallas_call(functools.partial(node_kernel, planes), grid=(total // til...]
    all_to_all x7 -> x0, local copies, waits for them, and re-layouts: 45.7 us -> none  [the longest x3 25.8 us: per_device(): lax.all_to_all(z_terms(lax.all_to_all(lines_y, 'col', split_axis=2, conca...]
    all_to_all x2 -> x4, waiting for transfers between devices: 52.4 us -> 74.6 us  [exchange(): return lax.all_to_all(block, 'row', split_axis=0, concat_axis=0, tiled=True)]
    unnamed x30 -> x12, local copies, waits for them, and re-layouts: 24.2 us -> 2.66 us
    scatter-add x1 -> x0, other arithmetic: 17.7 us -> none  [per_device(): flat_out = tendency.reshape(3, -1).at[:, flat_index].add(pushed)]
  transfers between devices with their start and end apart: 2 -> 11, of which waited for: 1 -> 6; matrix products, arithmetic and copies ran while one was open for 3% -> 4% of each run, Pallas kernels for 0% -> 18%
where the time goes in v1:
time: 319 us; the launch traced here: 316 us
  waiting for transfers between devices  199 us (62%)
  Pallas kernels  60.9 us (19%)
  starting transfers between devices  36.8 us (12%)
  local copies, waits for them, and re-layouts  18.2 us (6%)
    ppermute x4, waiting for transfers between devices, gather_step(): moved = lax.ppermute(known, 'row', [(i, i ^ step) for i in range(n_row)])  84.6 us
    all_to_all x4, waiting for transfers between devices, exchange(): return lax.all_to_all(block, 'row', split_axis=0, concat_axis=0, tiled=True)  74.6 us
    ppermute x3, waiting for transfers between devices, per_device(): lax.ppermute(pieces[phase], 'col', [(i, (i - s) % n_col) for i in range(n...  39.5 us
    all_to_all x4, starting transfers between devices, exchange(): return lax.all_to_all(block, 'row', split_axis=0, concat_axis=0, tiled=True)  25 us
    pallas_call x1, Pallas kernels, add_nodes(): pl.pallas_call(functools.partial(node_kernel, planes), grid=(total // til...  19.1 us
    pallas_call x3, Pallas kernels, in_place(): pl.pallas_call(kernel, grid=grid, in_specs=specs + [pl.BlockSpec(memory_s...  17.7 us
    pallas_call x2, Pallas kernels, combine(): pl.pallas_call(combine_kernel, grid=(comps, per), in_specs=[here, carrier...  13 us
    pallas_call x2, Pallas kernels, y_gradient(): pl.pallas_call(y_kernel, grid=(comps, planes, width // tile), in_specs=[p...  11.2 us
  transfers between devices with their start and end apart: 11, of which 6 were waited for; matrix products, arithmetic and copies ran while one was open for 4% of the time, Pallas kernels for 18%

profile of v1, /device:TPU:8, one launch (start us, length us, event | category | flops | bytes accessed | tf_op | source)
XLA Modules:
  0.0 315.8 jit_solution(5982150767717941775)
XLA Ops:
  0.0 4.9 %copy_bitcast_fusion = f32[16,2,1,64,512]{4,3,2,1,0:T(8,128)} fusion(f32[3,16,64,512]{3,2,1,0:T(8,128)} %param.5), kind=kLoop, calls=%fused_computation | loop fusion | bytes 8388608 | tf_op jit(solution)/shard_map/transpose;reshape | solution.py:178
  4.9 0.0 copy-start.5
  4.9 6.4 %all-to-all-start = ((f32[16,2,1,64,512]{4,3,2,1,0:T(8,128)}), f32[16,2,1,64,512]{4,3,2,1,0:T(8,128)}, u32[]{:S(2)}, u32[]{:S(2)}) async-start(f32[16,2,1,64,512]{4,3,2,1,0:T(8,128)} %copy_bitcast_fusion), calls=%async_computation | async-start | bytes 8388608 | tf_op jit(solution)/shard_map/all_to_all | solution.py:162
  11.3 0.0 copy-start.4
  11.4 0.0 copy-start
  11.4 2.4 slice.32
  13.7 1.6 collective-permute-start
  15.3 0.0 copy-done.5
  15.3 0.0 copy-done.4
  15.3 2.4 collective-permute-start.1
  17.7 84.6 %collective-permute-done.1 = f32[6,8]{1,0:T(8,128)S(1)} collective-permute-done((f32[6,8]{1,0:T(8,128)S(1)}, f32[6,8]{1,0:T(8,128)S(1)}, u32[]{:S(2)}, u32[]{:S(2)}) %collective-permute-start.1) | collective-permute-done | bytes 224 | tf_op jit(solution)/shard_map/ppermute | solution.py:172
  102.3 0.1 pad_maximum_fusion.1
  102.4 3.4 %collective-permute-start.2 = (f32[6,16]{1,0:T(8,128)S(1)}, f32[6,16]{1,0:T(8,128)S(1)}, u32[]{:S(2)}, u32[]{:S(2)}) collective-permute-start(f32[6,16]{1,0:T(8,128)S(1)} %pad_maximum_fusion.1), channel_id=1, source_target_pairs={{0,8},{2,10},{4,12},{6,14},{8,0},{10,2},{12,4},{14,6},{16,24},{18,... | collective-permute-start | bytes 1160 | tf_op jit(solution)/shard_map/ppermute | solution.py:172
  105.8 0.0 copy-done
  105.8 1.5 slice_bitcast_fusion.1
  107.2 0.1 slice.33
  107.3 0.0 collective-permute-done.2
  107.3 0.1 pad_maximum_fusion.2
  107.4 0.0 collective-permute-done.refs_1_
  107.4 0.0 all-to-all-done.lines_ref
  107.4 5.6 %all-to-all-start.1 = ((f32[16,1,1,64,512]{4,3,2,1,0:T(8,128)}), f32[16,1,1,64,512]{4,3,2,1,0:T(8,128)S(1)}, u32[]{:S(2)}, u32[]{:S(2)}) async-start(f32[16,1,1,64,512]{4,3,2,1,0:T(8,128)} %slice_bitcast_fusion.1), calls=%async_computation.1 | async-start | bytes 4194304 | tf_op jit(solution)/shard_map/all_to_all | solution.py:162
  113.0 1.5 collective-permute-start.3
  114.5 2.8 fusion
  117.3 1.5 collective-permute-start.4
  118.8 3.3 %slice_bitcast_fusion = f32[16,64,512]{2,1,0:T(8,128)} fusion(f32[3,16,64,512]{3,2,1,0:T(8,128)} %param.5), kind=kLoop, calls=%fused_computation.1 | loop fusion | bytes 4194304 | tf_op jit(solution)/shard_map/slice | solution.py:183
  122.1 6.8 %y_gradient.2 = f32[16,2,1,64,512]{4,3,2,1,0:T(8,128)} custom-call(bf16[1024,1024]{1,0:T(8,128)(2,1)} %op_ref.3, f32[16,2,1,64,512]{4,3,2,1,0:T(8,128)} %all-to-all-done.lines_ref), custom_call_target="tpu_custom_call" | custom-call | flops 2147483648 | bytes 10485760 | tf_op jit(solution)/shard_map/y_gradient/pallas_call | solution.py:28
  128.9 0.0 collective-permute-done.4
  128.9 0.1 pad_maximum_fusion.3
  128.9 0.0 collective-permute-start.5
  129.0 8.1 %z_terms.3.refs_4_ = f32[48,64,512]{2,1,0:T(8,128)} custom-call(f32[48,64,512]{2,1,0:T(8,128)} %bitcast.19, f32[48,64,512]{2,1,0:T(8,128)} %bitcast.20, f32[24,64,512]{2,1,0:T(8,128)} %collective-permute-done.refs_1_, bf16[512,512]{1,0:T(8,128)(2,1)} %get-tuple-element.44.refs_2_, bf16[512,512]{1,0:T(8,128)(2,1)} %get-tuple-element.43.refs_3_), custom_call_target="tpu_custom_call" | custom-call | flops 1610612736 | bytes 12582912 | tf_op jit(solution)/shard_map/z_terms/pallas_call | solution.py:44
  137.1 0.0 collective-permute-done.5
  137.1 0.1 pad_maximum_fusion.4
  137.2 1.1 collective-permute-done.3.refs_1_
  138.3 20.6 %all-to-all-done.1.lines_ref = f32[16,1,1,64,512]{4,3,2,1,0:T(8,128)S(1)} async-done(((f32[16,1,1,64,512]{4,3,2,1,0:T(8,128)}), f32[16,1,1,64,512]{4,3,2,1,0:T(8,128)S(1)}, u32[]{:S(2)}, u32[]{:S(2)}) %all-to-all-start.1) | async-done | bytes 2097184 | tf_op jit(solution)/shard_map/all_to_all | solution.py:162
  158.9 0.0 copy-start.1
  158.9 1.3 copy-done.1
  160.2 6.4 %all-to-all-start.2 = ((f32[16,2,1,64,512]{4,3,1,2,0:T(8,128)}), f32[16,2,1,64,512]{4,3,1,2,0:T(8,128)}, u32[]{:S(2)}, u32[]{:S(2)}) async-start(f32[16,2,1,64,512]{4,3,1,2,0:T(8,128)} %bitcast.28), calls=%async_computation.2 | async-start | bytes 8388608 | tf_op jit(solution)/shard_map/all_to_all | solution.py:162
  166.6 1.5 collective-permute-start.6
  168.1 3.6 %z_terms.4.refs_4_ = f32[48,64,512]{2,1,0:T(8,128)} custom-call(f32[48,64,512]{2,1,0:T(8,128)} %bitcast.21, f32[48,64,512]{2,1,0:T(8,128)} %bitcast.22, f32[8,64,512]{2,1,0:T(8,128)} %collective-permute-done.3.refs_1_, bf16[512,512]{1,0:T(8,128)(2,1)} %get-tuple-element.44.refs_2_, ...), custom_call_target="tpu_custom_call", output_to_operand_aliasing={{}: (5, {})} | custom-call | flops 536870912 | bytes 4194304 | tf_op jit(solution)/shard_map/z_terms/pallas_call | solution.py:44
  171.8 4.4 %y_gradient.3 = f32[16,1,1,64,512]{4,3,2,1,0:T(8,128)} custom-call(bf16[1024,1024]{1,0:T(8,128)(2,1)} %op_ref.3, f32[16,1,1,64,512]{4,3,2,1,0:T(8,128)} %copy-done.1), custom_call_target="tpu_custom_call" | custom-call | flops 1073741824 | bytes 6291456 | tf_op jit(solution)/shard_map/y_gradient/pallas_call | solution.py:28
  176.1 38.4 %collective-permute-done.6.refs_1_ = f32[16,64,512]{2,1,0:T(8,128)S(1)} collective-permute-done((f32[16,64,512]{2,1,0:T(8,128)}, f32[16,64,512]{2,1,0:T(8,128)S(1)}, u32[]{:S(2)}, u32[]{:S(2)}) %collective-permute-start.6) | collective-permute-done | bytes 2097184 | tf_op jit(solution)/shard_map/ppermute | solution.py:202
  214.5 0.0 copy-start.3
  214.5 42.9 %all-to-all-done.2 = f32[16,2,1,64,512]{4,3,1,2,0:T(8,128)} async-done(((f32[16,2,1,64,512]{4,3,1,2,0:T(8,128)}), f32[16,2,1,64,512]{4,3,1,2,0:T(8,128)}, u32[]{:S(2)}, u32[]{:S(2)}) %all-to-all-start.2) | async-done | bytes 4194336 | tf_op jit(solution)/shard_map/all_to_all | solution.py:162
  257.5 0.0 copy-done.3
  257.5 6.6 %all-to-all-start.3 = ((f32[16,1,1,64,512]{4,3,2,1,0:T(8,128)}), f32[16,1,1,64,512]{4,3,2,1,0:T(8,128)S(1)}, u32[]{:S(2)}, u32[]{:S(2)}) async-start(f32[16,1,1,64,512]{4,3,2,1,0:T(8,128)} %y_gradient.3), calls=%async_computation.3 | async-start | bytes 4194304 | tf_op jit(solution)/shard_map/all_to_all | solution.py:162
  264.0 0.1 pad_add_fusion
  264.1 0.6 slice.31.force_ref
  264.7 5.9 %z_terms.5.base_ref = f32[48,64,512]{2,1,0:T(8,128)} custom-call(f32[48,64,512]{2,1,0:T(8,128)} %bitcast.23, f32[48,64,512]{2,1,0:T(8,128)} %bitcast.24, f32[16,64,512]{2,1,0:T(8,128)} %copy-done.3, bf16[512,512]{1,0:T(8,128)(2,1)} %get-tuple-element.44.refs_2_, bf16[512,512]{1,0:T(8,128)(2,1)} %get-tuple-element.43.refs_3_, ...), custom_call_target="tpu_custom_call", output_to_operand_aliasing={{}: (5, {})} | custom-call | flops 1073741824 | bytes 8388608 | tf_op jit(solution)/shard_map/z_terms/pallas_call | solution.py:44
  270.6 0.7 convert_subtract_fusion.node_ref
  271.2 19.1 %add_nodes.1.base_ref = f32[48,64,512]{2,1,0:T(8,128)} custom-call(s32[3,128]{1,0:T(4,128)} %convert_subtract_fusion.node_ref, f32[3,128]{1,0:T(4,128)} %slice.31.force_ref, f32[48,64,512]{2,1,0:T(8,128)} %z_terms.5.base_ref), custom_call_target="tpu_custom_call", output_to_operand_aliasing={{}: (2, {})} | custom-call | flops 1572864 | bytes 12582912 | tf_op jit(solution)/shard_map/add_nodes/pallas_call | solution.py:118
  290.3 8.4 %combine.2.base_ref = f32[48,64,512]{2,1,0:T(8,128)} custom-call(f32[48,64,512]{2,1,0:T(8,128)} %add_nodes.1.base_ref, f32[48,64,512]{2,1,0:T(8,128)} %bitcast.25, f32[16,2,64,512]{3,2,1,0:T(8,128)} %bitcast.12.grad_ref), custom_call_target="tpu_custom_call", output_to_operand_aliasing={{}: (0, {})} | custom-call | flops 2097152 | bytes 16777216 | tf_op jit(solution)/shard_map/combine/pallas_call | solution.py:143
  298.7 11.2 %all-to-all-done.3 = f32[16,1,1,64,512]{4,3,2,1,0:T(8,128)S(1)} async-done(((f32[16,1,1,64,512]{4,3,2,1,0:T(8,128)}), f32[16,1,1,64,512]{4,3,2,1,0:T(8,128)S(1)}, u32[]{:S(2)}, u32[]{:S(2)}) %all-to-all-start.3) | async-done | bytes 2097184 | tf_op jit(solution)/shard_map/all_to_all | solution.py:162
  309.9 0.0 copy-start.2
  309.9 1.3 copy-done.2
  311.2 4.6 %combine.3 = f32[48,64,512]{2,1,0:T(8,128)} custom-call(f32[48,64,512]{2,1,0:T(8,128)} %combine.2.base_ref, f32[48,64,512]{2,1,0:T(8,128)} %bitcast.26, f32[16,1,64,512]{3,2,1,0:T(8,128)} %bitcast.29), custom_call_target="tpu_custom_call", output_to_operand_aliasing={{}: (0, {})} | custom-call | flops 1048576 | bytes 8388608 | tf_op jit(solution)/shard_map/combine/pallas_call | solution.py:143
  (2 shorter events, 0.0 us)
Async XLA Ops:
  4.9 10.4 %copy-start.5 = (s32[3,8]{1,0:T(4,128)S(1)}, s32[3,8]{1,0:T(4,128)}, u32[]{:S(2)}) copy-start(s32[3,8]{1,0:T(4,128)} %param.9) | copy-start | bytes 292
  4.9 102.5 %all-to-all-start = ((f32[16,2,1,64,512]{4,3,2,1,0:T(8,128)}), f32[16,2,1,64,512]{4,3,2,1,0:T(8,128)}, u32[]{:S(2)}, u32[]{:S(2)}) async-start(f32[16,2,1,64,512]{4,3,2,1,0:T(8,128)} %copy_bitcast_fusion), calls=%async_computation | async-start | bytes 8388608 | tf_op jit(solution)/shard_map/all_to_all | solution.py:162
  11.3 3.9 %copy-start.4 = (f32[3,8]{1,0:T(4,128)S(1)}, f32[3,8]{1,0:T(4,128)}, u32[]{:S(2)}) copy-start(f32[3,8]{1,0:T(4,128)} %param.8) | copy-start | bytes 292
  11.4 94.4 %copy-start = (f32[3,16,64,512]{3,2,1,0:T(8,128)S(1)}, f32[3,16,64,512]{3,2,1,0:T(8,128)}, u32[]{:S(2)}) copy-start(f32[3,16,64,512]{3,2,1,0:T(8,128)} %param.5) | copy-start | bytes 18874372
  13.7 93.7 %collective-permute-start = (f32[24,64,512]{2,1,0:T(8,128)S(1)}, f32[24,64,512]{2,1,0:T(8,128)}, u32[]{:S(2)}, u32[]{:S(2)}) collective-permute-start(f32[24,64,512]{2,1,0:T(8,128)S(1)} %slice.32), channel_id=1, source_target_pairs={{0,1},{1,0},{2,3},{3,2},{4,5},{5,4},{6,7},{7,6},{8,9},{9,8},{10,11... | collective-permute-start | bytes 9437192 | tf_op jit(solution)/shard_map/ppermute | solution.py:202
  15.3 87.0 %collective-permute-start.1 = (f32[6,8]{1,0:T(8,128)S(1)}, f32[6,8]{1,0:T(8,128)S(1)}, u32[]{:S(2)}, u32[]{:S(2)}) collective-permute-start(f32[6,8]{1,0:T(8,128)S(1)} %pad_maximum_fusion), channel_id=1, source_target_pairs={{0,16},{2,18},{4,20},{6,22},{8,24},{10,26},{12,28},{14,30},{16,0},... | collective-permute-start | bytes 584 | tf_op jit(solution)/shard_map/ppermute | solution.py:172
  102.4 5.0 %collective-permute-start.2 = (f32[6,16]{1,0:T(8,128)S(1)}, f32[6,16]{1,0:T(8,128)S(1)}, u32[]{:S(2)}, u32[]{:S(2)}) collective-permute-start(f32[6,16]{1,0:T(8,128)S(1)} %pad_maximum_fusion.1), channel_id=1, source_target_pairs={{0,8},{2,10},{4,12},{6,14},{8,0},{10,2},{12,4},{14,6},{16,24},{18,... | collective-permute-start | bytes 1160 | tf_op jit(solution)/shard_map/ppermute | solution.py:172
  107.4 51.5 %all-to-all-start.1 = ((f32[16,1,1,64,512]{4,3,2,1,0:T(8,128)}), f32[16,1,1,64,512]{4,3,2,1,0:T(8,128)S(1)}, u32[]{:S(2)}, u32[]{:S(2)}) async-start(f32[16,1,1,64,512]{4,3,2,1,0:T(8,128)} %slice_bitcast_fusion.1), calls=%async_computation.1 | async-start | bytes 4194304 | tf_op jit(solution)/shard_map/all_to_all | solution.py:162
  113.0 25.3 %collective-permute-start.3 = (f32[8,64,512]{2,1,0:T(8,128)S(1)}, f32[8,64,512]{2,1,0:T(8,128)}, u32[]{:S(2)}, u32[]{:S(2)}) collective-permute-start(f32[8,64,512]{2,1,0:T(8,128)S(1)} %slice.33), channel_id=1, source_target_pairs={{0,1},{1,0},{2,3},{3,2},{4,5},{5,4},{6,7},{7,6},{8,9},{9,8},{10,11... | collective-permute-start | bytes 3145736 | tf_op jit(solution)/shard_map/ppermute | solution.py:202
  117.3 11.5 %collective-permute-start.4 = (f32[6,32]{1,0:T(8,128)S(1)}, f32[6,32]{1,0:T(8,128)S(1)}, u32[]{:S(2)}, u32[]{:S(2)}) collective-permute-start(f32[6,32]{1,0:T(8,128)S(1)} %pad_maximum_fusion.2), channel_id=1, source_target_pairs={{0,4},{2,6},{4,0},{6,2},{8,12},{10,14},{12,8},{14,10},{16,20},{18,... | collective-permute-start | bytes 2312 | tf_op jit(solution)/shard_map/ppermute | solution.py:172
  128.9 8.2 %collective-permute-start.5 = (f32[6,64]{1,0:T(8,128)S(1)}, f32[6,64]{1,0:T(8,128)S(1)}, u32[]{:S(2)}, u32[]{:S(2)}) collective-permute-start(f32[6,64]{1,0:T(8,128)S(1)} %pad_maximum_fusion.3), channel_id=1, source_target_pairs={{0,2},{2,0},{4,6},{6,4},{8,10},{10,8},{12,14},{14,12},{16,18},{18,... | collective-permute-start | bytes 4616 | tf_op jit(solution)/shard_map/ppermute | solution.py:172
  158.9 1.3 copy-start.1
  160.2 97.3 %all-to-all-start.2 = ((f32[16,2,1,64,512]{4,3,1,2,0:T(8,128)}), f32[16,2,1,64,512]{4,3,1,2,0:T(8,128)}, u32[]{:S(2)}, u32[]{:S(2)}) async-start(f32[16,2,1,64,512]{4,3,1,2,0:T(8,128)} %bitcast.28), calls=%async_computation.2 | async-start | bytes 8388608 | tf_op jit(solution)/shard_map/all_to_all | solution.py:162
  166.6 47.9 %collective-permute-start.6 = (f32[16,64,512]{2,1,0:T(8,128)}, f32[16,64,512]{2,1,0:T(8,128)S(1)}, u32[]{:S(2)}, u32[]{:S(2)}) collective-permute-start(f32[16,64,512]{2,1,0:T(8,128)} %slice_bitcast_fusion), channel_id=1, source_target_pairs={{0,1},{1,0},{2,3},{3,2},{4,5},{5,4},{6,7},{7,6},{8,9},{9,8},{10,11... | collective-permute-start | bytes 6291464 | tf_op jit(solution)/shard_map/ppermute | solution.py:202
  214.5 42.9 %copy-start.3 = (f32[16,64,512]{2,1,0:T(8,128)}, f32[16,64,512]{2,1,0:T(8,128)S(1)}, u32[]{:S(2)}) copy-start(f32[16,64,512]{2,1,0:T(8,128)S(1)} %collective-permute-done.6.refs_1_) | copy-start | bytes 6291460
  257.5 52.4 %all-to-all-start.3 = ((f32[16,1,1,64,512]{4,3,2,1,0:T(8,128)}), f32[16,1,1,64,512]{4,3,2,1,0:T(8,128)S(1)}, u32[]{:S(2)}, u32[]{:S(2)}) async-start(f32[16,1,1,64,512]{4,3,2,1,0:T(8,128)} %y_gradient.3), calls=%async_computation.3 | async-start | bytes 4194304 | tf_op jit(solution)/shard_map/all_to_all | solution.py:162
  309.9 1.3 copy-start.2

commit v2 on v1

--- a/solution.py
+++ b/solution.py
@@ -8,9 +8,7 @@
 from jax.sharding import PartitionSpec as P
 
 VMEM = 60 << 20
-CHUNKS = ((0, 2), (2, 1))
-SHARES = (6, 2, 4)
-NODE_STEPS = (2, 2)
+GROUP = 4
 
 
 def y_kernel(op_ref, lines_ref, grad_ref):
@@ -112,7 +110,7 @@
 
 def add_nodes(out, planes, nodes, forces):
     total, height, width = out.shape
-    tile = planes // 2
+    tile = planes
     block = pl.BlockSpec((tile, height, width), lambda i: (i, 0, 0))
     smem = pl.BlockSpec(memory_space=pltpu.SMEM)
     return pl.pallas_call(
@@ -155,83 +153,186 @@
     )(out, flat, grad)
 
 
+def place_kernel(height, each, far, place_ref, op_ref, *refs):
+    line_refs, grad_refs, lines, grad = refs[:far], refs[far:-2], refs[-2], refs[-1]
+    near = len(grad_refs)
+    part = height // 8
+    tile = lines.shape[1]
+
+    def rows(s, t):
+        start = ((place_ref[0] ^ s) * near + (place_ref[1] ^ t)) * height
+        return pl.ds(pl.multiple_of(start, height), height)
+
+    for p in range(each):
+        for s in range(far):
+            for t in range(near):
+                block = line_refs[s][pl.ds((t * each + p) * part, part)]
+                lines[rows(s, t), :] = block.reshape(height, tile).astype(jnp.bfloat16)
+        grad[...] = jnp.dot(op_ref[...], lines[...], preferred_element_type=jnp.float32)
+        for s in range(far):
+            for t in range(near):
+                block = grad[rows(s, t), :].reshape(part, 8, tile)
+                grad_refs[t][pl.ds((s * each + p) * part, part)] = block
+
+
+def placed_gradient(place, op, lines, height, each):
+    far = len(lines)
+    count, _, width = lines[0].shape
+    near = (count - 1) * 8 // (each * height)
+    tile = min(width, 256)
+    block = pl.BlockSpec((count - 1, 8, tile), lambda j, _: (0, 0, j))
+    out_count = far * each * height // 8
+    out_block = pl.BlockSpec((out_count, 8, tile), lambda j, _: (0, 0, j))
+    size = far * (count - 1) * 8 * width
+    return pl.pallas_call(
+        functools.partial(place_kernel, height, each, far),
+        grid_spec=pltpu.PrefetchScalarGridSpec(
+            num_scalar_prefetch=1,
+            grid=(width // tile,),
+            in_specs=[pl.BlockSpec(op.shape, lambda j, _: (0, 0))] + [block] * far,
+            out_specs=[out_block] * near,
+            scratch_shapes=[
+                pltpu.VMEM((op.shape[0], tile), jnp.bfloat16),
+                pltpu.VMEM((op.shape[0], tile), jnp.float32),
+            ],
+        ),
+        out_shape=[jax.ShapeDtypeStruct((out_count, 8, width), jnp.float32)] * near,
+        compiler_params=pltpu.CompilerParams(vmem_limit_bytes=VMEM),
+        cost_estimate=pl.CostEstimate(
+            flops=2 * op.shape[0] * size, bytes_accessed=8 * size + 2 * op.size, transcendentals=0
+        ),
+        name="placed_gradient",
+    )(place, op, *lines)
+
+
+def placed_kernel(each, place_ref, base_ref, carrier_ref, grad_ref, out_ref):
+    for t in range(grad_ref.shape[0]):
+        here = pl.ds((place_ref[1] ^ t) * each, each)
+        out_ref[here] = base_ref[here] - carrier_ref[here] * grad_ref[t]
+
+
+def placed_combine(place, out, flat, grad, planes, comp, s):
+    near, each, height, width = grad.shape
+    far = planes // (near * each)
+    tile = min(width, 256)
+
+    def spec(first):
+        return pl.BlockSpec(
+            (near * each, height, tile), lambda j, at: (first * far + (at[0] ^ s), 0, j)
+        )
+
+    return pl.pallas_call(
+        functools.partial(placed_kernel, each),
+        grid_spec=pltpu.PrefetchScalarGridSpec(
+            num_scalar_prefetch=1,
+            grid=(width // tile,),
+            in_specs=[
+                spec(comp),
+                spec(1),
+                pl.BlockSpec((near, each, height, tile), lambda j, at: (0, 0, 0, j)),
+            ],
+            out_specs=spec(comp),
+        ),
+        out_shape=jax.ShapeDtypeStruct(out.shape, jnp.float32),
+        input_output_aliases={1: 0},
+        compiler_params=pltpu.CompilerParams(vmem_limit_bytes=VMEM),
+        cost_estimate=pl.CostEstimate(
+            flops=2 * grad.size, bytes_accessed=16 * grad.size, transcendentals=0
+        ),
+        name="placed_combine",
+    )(place, out, flat, grad)
+
+
+def after(value, *others):
+    return lax.optimization_barrier((value, others))[0]
+
+
 def solution(mesh):
     n_row, n_col = mesh.shape["row"], mesh.shape["col"]
+    near = GROUP
+    far = n_row // near
+    shifts = list(range(2, far)) + [1]
 
     def exchange(block):
         return lax.all_to_all(block, "row", split_axis=0, concat_axis=0, tiled=True)
+
+    def swap(block, distance):
+        return lax.ppermute(block, "row", [(i, i ^ distance) for i in range(n_row)])
 
     def per_device(velocity, dy_op, dz_op, node_force, node_cell):
         comps, planes, height, width = velocity.shape
         row_pos, col_pos = lax.axis_index("row"), lax.axis_index("col")
-        total = comps * planes
-        n_chunks = len(CHUNKS)
-        n_phases = 2 * n_chunks
-
-        def gather_step(known, step):
-            moved = lax.ppermute(known, "row", [(i, i ^ step) for i in range(n_row)])
-            return jnp.concatenate([known, moved], axis=1)
-
-        def chunk_of(velocity, k):
-            first, count = CHUNKS[k]
-            block = velocity[first : first + count].swapaxes(0, 1)
-            return block.reshape(n_row, planes // n_row, count, height, width).swapaxes(1, 2)
-
-        def piece_of(velocity, k):
-            unit = total // sum(SHARES)
-            begin, end = unit * sum(SHARES[:k]), unit * sum(SHARES[: k + 1])
-            return velocity.reshape(total, height, width)[begin:end]
+        total, each = comps * planes, planes // n_row
+        far_pos, near_pos = row_pos // near, row_pos % near
+        place = jnp.stack([far_pos, near_pos]).astype(jnp.int32)
+        bulk = comps - 1
+        eights = each * height // 8
+        per_node = node_force.shape[1]
 
         own_rows = lax.dynamic_slice_in_dim(dz_op, col_pos * width, width, 0)
         ops = [
             lax.dynamic_slice_in_dim(own_rows, (col_pos + s) % n_col * width, width, 1)
             for s in range(n_col)
         ]
-        known = jnp.concatenate([node_force, node_cell.astype(jnp.float32)])
-        steps = [1 << k for k in range(n_row.bit_length() - 1)][::-1]
-
-        chunks = [chunk_of(velocity, 0)]
-        pieces = [piece_of(velocity, 0)]
-        grads = [None] * n_chunks
-        out, start = None, 0
-        for phase in range(n_phases):
-            moved = exchange(chunks[phase])
-            others = None
-            if phase < len(SHARES):
-                others = [
-                    lax.ppermute(pieces[phase], "col", [(i, (i - s) % n_col) for i in range(n_col)])
-                    for s in range(1, n_col)
-                ]
-            if phase < len(NODE_STEPS):
-                last = phase == len(NODE_STEPS) - 1
-                for _ in range(len(steps) if last else NODE_STEPS[phase]):
-                    known = gather_step(known, steps.pop(0))
-            if phase + 1 < n_chunks:
-                chunks.append(chunk_of(velocity, phase + 1))
-            if phase + 1 < len(SHARES):
-                pieces.append(piece_of(velocity, phase + 1))
-            if 1 <= phase <= n_chunks:
-                chunks.append(y_gradient(dy_op, arrived))
-            if phase > 0 and start < total:
-                flat = velocity.reshape(total, height, width)
-                out = z_terms(out, flat, planes, start, arriving, ops)
-                start += arriving[0].shape[0]
-            if phase == n_phases - 1:
-                break
-            arrived, arriving = moved, others
-            if phase >= n_chunks:
-                grads[phase - n_chunks] = moved
-            state = velocity, chunks, pieces, arrived, arriving, grads, out, known
-            state = lax.optimization_barrier(state)
-            velocity, chunks, pieces, arrived, arriving, grads, out, known = state
-        grads[-1] = moved
+
+        def node_tile(known):
+            return jnp.pad(known, ((0, 8 - known.shape[0]), (0, width - known.shape[1])))[None]
+
+        block = velocity[:bulk].swapaxes(0, 1)
+        block = block.reshape(n_row, each, bulk, height, width).swapaxes(1, 2)
+        velocity, block = lax.optimization_barrier((velocity, block))
+        lines = exchange(block)
         flat = velocity.reshape(total, height, width)
+
+        def beside(piece):
+            return [
+                lax.ppermute(piece, "col", [(i, (i - s) % n_col) for i in range(n_col)])
+                for s in range(1, n_col)
+            ]
+
+        early = 2 * total // 3
+        others = beside(flat[:early])
+
+        known = node_tile(jnp.concatenate([node_force, node_cell.astype(jnp.float32)]))
+        rows = flat.reshape(total * height // 8, 8, width)
+        lot = []
+        for t in range(near):
+            blocks = []
+            for s in range(far):
+                plane = bulk * planes + ((far_pos ^ s) * near + (near_pos ^ t)) * each
+                blocks.append(lax.dynamic_slice_in_dim(rows, plane * height // 8, eights, 0))
+            lot.append(jnp.concatenate(blocks + [known]))
+        lot = [lot[0]] + [swap(lot[t], t) for t in range(1, near)]
+        known = node_tile(jnp.concatenate([part[-1, :, :per_node] for part in lot], axis=1))
+        landed = []
+        for s in range(far):
+            blocks = [part[s * eights : (s + 1) * eights] for part in lot]
+            landed.append(jnp.concatenate(blocks + [known]))
+        for s in shifts:
+            landed[s] = swap(landed[s], s * near)
+        known = jnp.concatenate([part[-1, :, : near * per_node] for part in landed], axis=1)
+
+        grads = y_gradient(dy_op, lines)
+        grads = exchange(after(grads, others, landed))
+
+        out = z_terms(None, flat, planes, 0, others, ops)
+        others = beside(after(flat, landed[1])[early:])
+        grad = placed_gradient(place, dy_op, after(landed, out), height, each)
         origin = jnp.stack([0 * row_pos, row_pos * height, col_pos * width])
-        cells = known[comps:].astype(jnp.int32) - origin[:, None].astype(jnp.int32)
+        cells = known[comps : 2 * comps].astype(jnp.int32) - origin[:, None].astype(jnp.int32)
+        grad = [grad[0]] + [swap(grad[t], t) for t in range(1, near)]
+        back = [
+            jnp.stack([part[s * eights : (s + 1) * eights] for part in grad]) for s in range(far)
+        ]
+        others = after(others, back)
+        back = [part.reshape(near, each, height, width) for part in back]
+        back = [back[s] if s == 0 else swap(back[s], s * near) for s in range(far)]
+        out = z_terms(out, flat, planes, early, others, ops)
         out = add_nodes(out, planes, cells, known[:comps])
-        for (first, count), grad in zip(CHUNKS, grads):
-            grad = grad.swapaxes(1, 2).reshape(planes, count, height, width)
-            out = combine(out, flat, planes, grad, first)
+        grads = grads.swapaxes(1, 2).reshape(planes, bulk, height, width)
+        out = combine(out, flat, planes, grads, 0)
+        for s in [0, 1] + shifts[:-1]:
+            out = placed_combine(place, out, flat, back[s], planes, bulk, s)
         return out.reshape(velocity.shape)
 
     return jax.shard_map(

time: 319 us -> 299 us (0.937)
  waiting for transfers between devices: 199 us -> 162 us
  local copies, waits for them, and re-layouts: 18.2 us -> 30.9 us
  other arithmetic: 1.05 us -> 5.73 us
    all_to_all x4 -> x2, waiting for transfers between devices: 74.6 us -> 56 us  [exchange(): return lax.all_to_all(block, 'row', split_axis=0, concat_axis=0, tiled=True)]
    ppermute x7 -> x14, waiting for transfers between devices: 124 us -> 106 us  [the longest x12 106 us: swap(): return lax.ppermute(block, 'row', [(i, i ^ distance) for i in range(n_row)])]
    pallas_call x0 -> x5, Pallas kernels: none -> 16.7 us  [the longest x4 11.2 us: placed_combine(): pl.pallas_call(functools.partial(placed_kernel, each), grid_spec=pltpu.Pr...]
    ppermute x7 -> x14, starting transfers between devices: 11.8 us -> 24.5 us  [the longest x12 21.6 us: swap(): return lax.ppermute(block, 'row', [(i, i ^ distance) for i in range(n_row)])]
    all_to_all x4 -> x2, starting transfers between devices: 25 us -> 13.9 us  [exchange(): return lax.all_to_all(block, 'row', split_axis=0, concat_axis=0, tiled=True)]
    unnamed x12 -> x29, local copies, waits for them, and re-layouts: 2.66 us -> 11.3 us
    pallas_call x1, Pallas kernels: 19.1 us -> 11.6 us  [add_nodes(): pl.pallas_call(functools.partial(node_kernel, planes), grid=(total // til...]
    pallas_call x2 -> x1, Pallas kernels: 13 us -> 8.44 us  [combine(): pl.pallas_call(combine_kernel, grid=(comps, per), in_specs=[here, carrier...]
  transfers between devices with their start and end apart: 11 -> 16, of which waited for: 6 -> 9; matrix products, arithmetic and copies ran while one was open for 4% -> 9% of each run, Pallas kernels for 18% -> 19%
where the time goes in v2:
time: 299 us; the launch traced here: 297 us
  waiting for transfers between devices  162 us (54%)
  Pallas kernels  59.9 us (20%)
  starting transfers between devices  38.4 us (13%)
  local copies, waits for them, and re-layouts  30.9 us (10%)
  other arithmetic  5.73 us (2%)
    ppermute x12, waiting for transfers between devices, swap(): return lax.ppermute(block, 'row', [(i, i ^ distance) for i in range(n_row)])  106 us
    all_to_all x2, waiting for transfers between devices, exchange(): return lax.all_to_all(block, 'row', split_axis=0, concat_axis=0, tiled=True)  56 us
    ppermute x12, starting transfers between devices, swap(): return lax.ppermute(block, 'row', [(i, i ^ distance) for i in range(n_row)])  21.6 us
    pallas_call x2, Pallas kernels, in_place(): pl.pallas_call(kernel, grid=grid, in_specs=specs + [pl.BlockSpec(memory_s...  16.3 us
    all_to_all x2, starting transfers between devices, exchange(): return lax.all_to_all(block, 'row', split_axis=0, concat_axis=0, tiled=True)  13.9 us
    pallas_call x1, Pallas kernels, add_nodes(): pl.pallas_call(functools.partial(node_kernel, planes), grid=(total // til...  11.6 us
    unnamed x29, local copies, waits for them, and re-layouts  11.3 us
    pallas_call x4, Pallas kernels, placed_combine(): pl.pallas_call(functools.partial(placed_kernel, each), grid_spec=pltpu.Pr...  11.2 us
  transfers between devices with their start and end apart: 16, of which 9 were waited for; matrix products, arithmetic and copies ran while one was open for 9% of the time, Pallas kernels for 19%

profile of v2, /device:TPU:8, one launch (start us, length us, event | category | flops | bytes accessed | tf_op | source)
XLA Modules:
  0.0 297.4 jit_solution(14263159930211540081)
XLA Ops:
  0.0 4.9 %copy_bitcast_fusion = f32[16,2,1,64,512]{4,3,2,1,0:T(8,128)} fusion(f32[3,16,64,512]{3,2,1,0:T(8,128)} %param.5), kind=kLoop, calls=%fused_computation | loop fusion | bytes 8388608 | tf_op jit(solution)/shard_map/transpose;reshape | solution.py:282
  4.9 6.3 %all-to-all-start = ((f32[16,2,1,64,512]{4,3,2,1,0:T(8,128)}), f32[16,2,1,64,512]{4,3,2,1,0:T(8,128)}, u32[]{:S(2)}, u32[]{:S(2)}) async-start(f32[16,2,1,64,512]{4,3,2,1,0:T(8,128)} %copy_bitcast_fusion), calls=%async_computation | async-start | bytes 8388608 | tf_op jit(solution)/shard_map/all_to_all | solution.py:257
  11.2 0.0 copy-start.9
  11.2 4.9 %slice.147 = f32[2,16,64,512]{3,2,1,0:T(8,128)} slice(f32[3,16,64,512]{3,2,1,0:T(8,128)} %param.5), slice={[0:2], [0:16], [0:64], [0:512]} | slice | bytes 8388608 | tf_op jit(solution)/shard_map/slice | solution.py:294
  16.1 1.5 collective-permute-start.7
  17.6 1.1 dynamic-slice_dynamic-update-slice_fusion.7
  18.7 1.1 dynamic-slice_dynamic-update-slice_fusion.6
  19.8 1.1 dynamic-slice_dynamic-update-slice_fusion.5
  20.8 2.1 dynamic-slice_dynamic-update-slice_fusion
  22.9 1.0 collective-permute-start.2
  23.9 0.6 collective-permute-start
  24.5 0.6 collective-permute-start.1
  25.1 21.3 %collective-permute-done.2 = f32[33,8,512]{2,1,0:T(8,128)S(1)} collective-permute-done((f32[33,8,512]{2,1,0:T(8,128)S(1)}, f32[33,8,512]{2,1,0:T(8,128)S(1)}, u32[]{:S(2)}, u32[]{:S(2)}) %collective-permute-start.2) | collective-permute-done | bytes 540704 | tf_op jit(solution)/shard_map/ppermute | solution.py:260
  46.5 0.0 collective-permute-done
  46.5 19.7 %collective-permute-done.1 = f32[33,8,512]{2,1,0:T(8,128)S(1)} collective-permute-done((f32[33,8,512]{2,1,0:T(8,128)S(1)}, f32[33,8,512]{2,1,0:T(8,128)S(1)}, u32[]{:S(2)}, u32[]{:S(2)}) %collective-permute-start.1) | collective-permute-done | bytes 540704 | tf_op jit(solution)/shard_map/ppermute | solution.py:260
  66.2 0.8 slice_dynamic-update-slice_fusion.2
  66.9 0.8 slice_dynamic-update-slice_fusion.1
  67.7 0.7 slice_dynamic-update-slice_fusion
  68.4 0.1 constant_dynamic-update-slice_fusion.5
  68.5 7.2 %collective-permute-start.5 = (f32[33,8,512]{2,1,0:T(8,128)S(1)}, f32[33,8,512]{2,1,0:T(8,128)S(1)}, u32[]{:S(2)}, u32[]{:S(2)}) collective-permute-start(f32[33,8,512]{2,1,0:T(8,128)S(1)} %constant_dynamic-update-slice_fusion.5), channel_id=1, source_target_pairs={{0,24},{2,26},{4,28},{6,30},{8,16},{10,18},{12,20},{14,22},{16,8},... | collective-permute-start | bytes 1622024 | tf_op jit(solution)/shard_map/ppermute | solution.py:260
  75.7 0.7 constant_dynamic-update-slice_fusion.6
  76.4 6.8 %collective-permute-start.3 = (f32[33,8,512]{2,1,0:T(8,128)}, f32[33,8,512]{2,1,0:T(8,128)S(1)}, u32[]{:S(2)}, u32[]{:S(2)}) collective-permute-start(f32[33,8,512]{2,1,0:T(8,128)} %get-tuple-element.76), channel_id=1, source_target_pairs={{0,8},{2,10},{4,12},{6,14},{8,0},{10,2},{12,4},{14,6},{16,24},{18,... | collective-permute-start | bytes 1622024 | tf_op jit(solution)/shard_map/ppermute | solution.py:260
  83.2 42.6 %all-to-all-done.lines_ref = f32[16,2,1,64,512]{4,3,2,1,0:T(8,128)} async-done(((f32[16,2,1,64,512]{4,3,2,1,0:T(8,128)}), f32[16,2,1,64,512]{4,3,2,1,0:T(8,128)}, u32[]{:S(2)}, u32[]{:S(2)}) %all-to-all-start) | async-done | bytes 4194336 | tf_op jit(solution)/shard_map/all_to_all | solution.py:257
  125.8 6.9 %y_gradient.1 = f32[16,2,1,64,512]{4,3,2,1,0:T(8,128)} custom-call(bf16[1024,1024]{1,0:T(8,128)(2,1)} %op_ref.3, f32[16,2,1,64,512]{4,3,2,1,0:T(8,128)} %all-to-all-done.lines_ref), custom_call_target="tpu_custom_call" | custom-call | flops 2147483648 | bytes 10485760 | tf_op jit(solution)/shard_map/y_gradient/pallas_call | solution.py:26
  132.7 6.5 %collective-permute-done.5.refs_3_ = f32[33,8,512]{2,1,0:T(8,128)S(1)} collective-permute-done((f32[33,8,512]{2,1,0:T(8,128)S(1)}, f32[33,8,512]{2,1,0:T(8,128)S(1)}, u32[]{:S(2)}, u32[]{:S(2)}) %collective-permute-start.5) | collective-permute-done | bytes 540704 | tf_op jit(solution)/shard_map/ppermute | solution.py:260
  139.2 9.3 %collective-permute-done.4.refs_2_ = f32[33,8,512]{2,1,0:T(8,128)S(1)} collective-permute-done((f32[33,8,512]{2,1,0:T(8,128)}, f32[33,8,512]{2,1,0:T(8,128)S(1)}, u32[]{:S(2)}, u32[]{:S(2)}) %collective-permute-start.4) | collective-permute-done | bytes 540704 | tf_op jit(solution)/shard_map/ppermute | solution.py:260
  148.5 7.6 %all-to-all-start.1 = ((f32[16,2,1,64,512]{4,3,1,2,0:T(8,128)}), f32[16,2,1,64,512]{4,3,1,2,0:T(8,128)}, u32[]{:S(2)}, u32[]{:S(2)}) async-start(f32[16,2,1,64,512]{4,3,1,2,0:T(8,128)} %bitcast.94), calls=%async_computation.1 | async-start | bytes 8388608 | tf_op jit(solution)/shard_map/all_to_all | solution.py:257
  156.1 0.7 pad_add_fusion.place_ref
  156.8 0.1 pad_add_fusion.1
  156.8 2.8 fusion.2
  159.7 0.1 fusion
  159.8 3.1 %slice.146 = f32[16,64,512]{2,1,0:T(8,128)} slice(f32[48,64,512]{2,1,0:T(8,128)} %bitcast.84), slice={[32:48], [0:64], [0:512]} | slice | bytes 4194304 | tf_op jit(solution)/shard_map/slice | solution.py:319
  162.9 1.5 collective-permute-start.6
  164.4 10.4 %z_terms.2.refs_4_ = f32[48,64,512]{2,1,0:T(8,128)} custom-call(f32[48,64,512]{2,1,0:T(8,128)} %bitcast.85, f32[48,64,512]{2,1,0:T(8,128)} %bitcast.86, f32[32,64,512]{2,1,0:T(8,128)} %collective-permute-done.7.refs_1_, bf16[512,512]{1,0:T(8,128)(2,1)} %get-tuple-element.46.refs_2_, bf16[512,512]{1,0:T(8,128)(2,1)} %get-tuple-element.45.refs_3_), custom_call_target="tpu_custom_call" | custom-call | flops 2147483648 | bytes 16777216 | tf_op jit(solution)/shard_map/z_terms/pallas_call | solution.py:42
  174.7 5.5 %placed_gradient.1 = (f32[32,8,512]{2,1,0:T(8,128)}, f32[32,8,512]{2,1,0:T(8,128)}, f32[32,8,512]{2,1,0:T(8,128)}, f32[32,8,512]{2,1,0:T(8,128)}) custom-call(s32[2]{0:T(128)} %pad_add_fusion.place_ref, bf16[1024,1024]{1,0:T(8,128)(2,1)} %op_ref.3, f32[33,8,512]{2,1,0:T(8,128)} %copy-done.1, f32[33,8,512]{2,1,0:T(8,128)} %copy-done.4, ...), custom_call_target="tpu_custom_call" | custom-call | flops 1073741824 | bytes 6291456 | tf_op jit(solution)/shard_map/placed_gradient/pallas_call | solution.py:187
  180.2 0.7 slice_bitcast_fusion.18
  180.9 1.5 collective-permute-start.9
  182.4 0.7 slice_bitcast_fusion.17
  183.1 0.4 collective-permute-start.10
  183.4 1.1 slice_bitcast_fusion.12
  184.6 23.5 %collective-permute-done.9 = f32[32,8,512]{2,1,0:T(8,128)S(1)} collective-permute-done((f32[32,8,512]{2,1,0:T(8,128)}, f32[32,8,512]{2,1,0:T(8,128)S(1)}, u32[]{:S(2)}, u32[]{:S(2)}) %collective-permute-start.9) | collective-permute-done | bytes 524320 | tf_op jit(solution)/shard_map/ppermute | solution.py:260
  208.2 20.6 %collective-permute-done.10 = f32[32,8,512]{2,1,0:T(8,128)S(1)} collective-permute-done((f32[32,8,512]{2,1,0:T(8,128)}, f32[32,8,512]{2,1,0:T(8,128)S(1)}, u32[]{:S(2)}, u32[]{:S(2)}) %collective-permute-start.10) | collective-permute-done | bytes 524320 | tf_op jit(solution)/shard_map/ppermute | solution.py:260
  228.8 0.7 slice_bitcast_fusion
  229.5 0.9 pad_maximum_fusion.1
  230.4 0.8 pad_maximum_fusion.2
  231.2 0.8 pad_maximum_fusion.3
  232.0 3.5 %collective-permute-start.13 = (f32[4,1,64,512]{3,2,1,0:T(8,128)}, f32[4,1,64,512]{3,2,1,0:T(8,128)S(1)}, u32[]{:S(2)}, u32[]{:S(2)}) collective-permute-start(f32[4,1,64,512]{3,2,1,0:T(8,128)} %pad_maximum_fusion.3), channel_id=1, source_target_pairs={{0,24},{2,26},{4,28},{6,30},{8,16},{10,18},{12,20},{14,22},{16,8},... | collective-permute-start | bytes 1572872 | tf_op jit(solution)/shard_map/ppermute | solution.py:260
  235.5 0.1 pad_maximum_fusion.4
  235.6 0.6 slice.145.force_ref
  236.2 0.6 convert_subtract_fusion.node_ref
  236.8 1.4 copy-done
  238.2 5.9 %z_terms.3.base_ref = f32[48,64,512]{2,1,0:T(8,128)} custom-call(f32[48,64,512]{2,1,0:T(8,128)} %bitcast.87, f32[48,64,512]{2,1,0:T(8,128)} %bitcast.88, f32[16,64,512]{2,1,0:T(8,128)} %copy-done, bf16[512,512]{1,0:T(8,128)(2,1)} %get-tuple-element.46.refs_2_, bf16[512,512]{1,0:T(8,128)(2,1)} %get-tuple-element.45.refs_3_, ...), custom_call_target="tpu_custom_call", output_to_operand_aliasing={{}: (5, {})} | custom-call | flops 1073741824 | bytes 8388608 | tf_op jit(solution)/shard_map/z_terms/pallas_call | solution.py:42
  244.1 11.6 %add_nodes.1.base_ref = f32[48,64,512]{2,1,0:T(8,128)} custom-call(s32[3,128]{1,0:T(4,128)} %convert_subtract_fusion.node_ref, f32[3,128]{1,0:T(4,128)} %slice.145.force_ref, f32[48,64,512]{2,1,0:T(8,128)} %z_terms.3.base_ref), custom_call_target="tpu_custom_call", output_to_operand_aliasing={{}: (2, {})} | custom-call | flops 1572864 | bytes 12582912 | tf_op jit(solution)/shard_map/add_nodes/pallas_call | solution.py:116
  255.7 0.9 pad_maximum_fusion.grad_ref
  256.6 13.4 %all-to-all-done.1 = f32[16,2,1,64,512]{4,3,1,2,0:T(8,128)} async-done(((f32[16,2,1,64,512]{4,3,1,2,0:T(8,128)}), f32[16,2,1,64,512]{4,3,1,2,0:T(8,128)}, u32[]{:S(2)}, u32[]{:S(2)}) %all-to-all-start.1) | async-done | bytes 4194336 | tf_op jit(solution)/shard_map/all_to_all | solution.py:257
  270.0 8.4 %combine.1.base_ref = f32[48,64,512]{2,1,0:T(8,128)} custom-call(f32[48,64,512]{2,1,0:T(8,128)} %add_nodes.1.base_ref, f32[48,64,512]{2,1,0:T(8,128)} %bitcast.89, f32[16,2,64,512]{3,2,1,0:T(8,128)} %bitcast.20.grad_ref), custom_call_target="tpu_custom_call", output_to_operand_aliasing={{}: (0, {})} | custom-call | flops 2097152 | bytes 16777216 | tf_op jit(solution)/shard_map/combine/pallas_call | solution.py:141
  278.4 2.8 placed_combine.4.base_ref
  281.2 0.8 copy-done.5
  282.0 2.8 placed_combine.5.base_ref
  284.8 0.8 copy-done.6
  285.6 2.8 placed_combine.6.base_ref
  288.4 5.5 %collective-permute-done.13.grad_ref = f32[4,1,64,512]{3,2,1,0:T(8,128)S(1)} collective-permute-done((f32[4,1,64,512]{3,2,1,0:T(8,128)}, f32[4,1,64,512]{3,2,1,0:T(8,128)S(1)}, u32[]{:S(2)}, u32[]{:S(2)}) %collective-permute-start.13) | collective-permute-done | bytes 524320 | tf_op jit(solution)/shard_map/ppermute | solution.py:260
  293.8 0.8 copy-done.7
  294.6 2.8 placed_combine.7
  (38 shorter events, 0.2 us)
Async XLA Ops:
  4.9 120.9 %all-to-all-start = ((f32[16,2,1,64,512]{4,3,2,1,0:T(8,128)}), f32[16,2,1,64,512]{4,3,2,1,0:T(8,128)}, u32[]{:S(2)}, u32[]{:S(2)}) async-start(f32[16,2,1,64,512]{4,3,2,1,0:T(8,128)} %copy_bitcast_fusion), calls=%async_computation | async-start | bytes 8388608 | tf_op jit(solution)/shard_map/all_to_all | solution.py:257
  11.2 6.4 %copy-start.10 = (s32[3,8]{1,0:T(4,128)S(1)}, s32[3,8]{1,0:T(4,128)}, u32[]{:S(2)}) copy-start(s32[3,8]{1,0:T(4,128)} %param.9) | copy-start | bytes 292
  11.2 11.7 %copy-start.9 = (f32[3,8]{1,0:T(4,128)S(1)}, f32[3,8]{1,0:T(4,128)}, u32[]{:S(2)}) copy-start(f32[3,8]{1,0:T(4,128)} %param.8) | copy-start | bytes 292
  16.1 132.4 %collective-permute-start.7 = (f32[32,64,512]{2,1,0:T(8,128)}, f32[32,64,512]{2,1,0:T(8,128)}, u32[]{:S(2)}, u32[]{:S(2)}) collective-permute-start(f32[32,64,512]{2,1,0:T(8,128)} %bitcast.18), channel_id=1, source_target_pairs={{0,1},{1,0},{2,3},{3,2},{4,5},{5,4},{6,7},{7,6},{8,9},{9,8},{10,11... | collective-permute-start | bytes 12582920 | tf_op jit(solution)/shard_map/ppermute | solution.py:289
  22.9 23.6 %collective-permute-start.2 = (f32[33,8,512]{2,1,0:T(8,128)S(1)}, f32[33,8,512]{2,1,0:T(8,128)S(1)}, u32[]{:S(2)}, u32[]{:S(2)}) collective-permute-start(f32[33,8,512]{2,1,0:T(8,128)S(1)} %get-tuple-element.78), channel_id=1, source_target_pairs={{0,6},{2,4},{4,2},{6,0},{8,14},{10,12},{12,10},{14,8},{16,22},{18,... | collective-permute-start | bytes 1622024 | tf_op jit(solution)/shard_map/ppermute | solution.py:260
  23.9 22.6 %collective-permute-start = (f32[33,8,512]{2,1,0:T(8,128)S(1)}, f32[33,8,512]{2,1,0:T(8,128)S(1)}, u32[]{:S(2)}, u32[]{:S(2)}) collective-permute-start(f32[33,8,512]{2,1,0:T(8,128)S(1)} %get-tuple-element.79), channel_id=1, source_target_pairs={{0,2},{2,0},{4,6},{6,4},{8,10},{10,8},{12,14},{14,12},{16,18},{18,... | collective-permute-start | bytes 1622024 | tf_op jit(solution)/shard_map/ppermute | solution.py:260
  24.5 41.6 %collective-permute-start.1 = (f32[33,8,512]{2,1,0:T(8,128)S(1)}, f32[33,8,512]{2,1,0:T(8,128)S(1)}, u32[]{:S(2)}, u32[]{:S(2)}) collective-permute-start(f32[33,8,512]{2,1,0:T(8,128)S(1)} %get-tuple-element.80), channel_id=1, source_target_pairs={{0,4},{2,6},{4,0},{6,2},{8,12},{10,14},{12,8},{14,10},{16,20},{18,... | collective-permute-start | bytes 1622024 | tf_op jit(solution)/shard_map/ppermute | solution.py:260
  68.5 70.7 %collective-permute-start.5 = (f32[33,8,512]{2,1,0:T(8,128)S(1)}, f32[33,8,512]{2,1,0:T(8,128)S(1)}, u32[]{:S(2)}, u32[]{:S(2)}) collective-permute-start(f32[33,8,512]{2,1,0:T(8,128)S(1)} %constant_dynamic-update-slice_fusion.5), channel_id=1, source_target_pairs={{0,24},{2,26},{4,28},{6,30},{8,16},{10,18},{12,20},{14,22},{16,8},... | collective-permute-start | bytes 1622024 | tf_op jit(solution)/shard_map/ppermute | solution.py:260
  76.4 72.1 %copy-start.1 = (f32[33,8,512]{2,1,0:T(8,128)}, f32[33,8,512]{2,1,0:T(8,128)S(1)}, u32[]{:S(2)}) copy-start(f32[33,8,512]{2,1,0:T(8,128)S(1)} %get-tuple-element.21.refs_0_) | copy-start | bytes 1622020
  76.4 62.8 %collective-permute-start.3 = (f32[33,8,512]{2,1,0:T(8,128)}, f32[33,8,512]{2,1,0:T(8,128)S(1)}, u32[]{:S(2)}, u32[]{:S(2)}) collective-permute-start(f32[33,8,512]{2,1,0:T(8,128)} %get-tuple-element.76), channel_id=1, source_target_pairs={{0,8},{2,10},{4,12},{6,14},{8,0},{10,2},{12,4},{14,6},{16,24},{18,... | collective-permute-start | bytes 1622024 | tf_op jit(solution)/shard_map/ppermute | solution.py:260
  83.2 65.3 %collective-permute-start.4 = (f32[33,8,512]{2,1,0:T(8,128)}, f32[33,8,512]{2,1,0:T(8,128)S(1)}, u32[]{:S(2)}, u32[]{:S(2)}) collective-permute-start(f32[33,8,512]{2,1,0:T(8,128)} %get-tuple-element.77), channel_id=1, source_target_pairs={{0,16},{2,18},{4,20},{6,22},{8,24},{10,26},{12,28},{14,30},{16,0},... | collective-permute-start | bytes 1622024 | tf_op jit(solution)/shard_map/ppermute | solution.py:260
  139.2 25.2 %copy-start.2 = (f32[33,8,512]{2,1,0:T(8,128)}, f32[33,8,512]{2,1,0:T(8,128)S(1)}, u32[]{:S(2)}) copy-start(f32[33,8,512]{2,1,0:T(8,128)S(1)} %collective-permute-done.5.refs_3_) | copy-start | bytes 1622020
  139.2 20.6 %copy-start.4 = (f32[33,8,512]{2,1,0:T(8,128)}, f32[33,8,512]{2,1,0:T(8,128)S(1)}, u32[]{:S(2)}) copy-start(f32[33,8,512]{2,1,0:T(8,128)S(1)} %collective-permute-done.3.refs_1_) | copy-start | bytes 1622020
  148.5 14.4 %copy-start.3 = (f32[33,8,512]{2,1,0:T(8,128)}, f32[33,8,512]{2,1,0:T(8,128)S(1)}, u32[]{:S(2)}) copy-start(f32[33,8,512]{2,1,0:T(8,128)S(1)} %collective-permute-done.4.refs_2_) | copy-start | bytes 1622020
  148.5 121.5 %all-to-all-start.1 = ((f32[16,2,1,64,512]{4,3,1,2,0:T(8,128)}), f32[16,2,1,64,512]{4,3,1,2,0:T(8,128)}, u32[]{:S(2)}, u32[]{:S(2)}) async-start(f32[16,2,1,64,512]{4,3,1,2,0:T(8,128)} %bitcast.94), calls=%async_computation.1 | async-start | bytes 8388608 | tf_op jit(solution)/shard_map/all_to_all | solution.py:257
  162.9 73.9 %collective-permute-start.6 = (f32[16,64,512]{2,1,0:T(8,128)}, f32[16,64,512]{2,1,0:T(8,128)S(1)}, u32[]{:S(2)}, u32[]{:S(2)}) collective-permute-start(f32[16,64,512]{2,1,0:T(8,128)} %slice.146), channel_id=1, source_target_pairs={{0,1},{1,0},{2,3},{3,2},{4,5},{5,4},{6,7},{7,6},{8,9},{9,8},{10,11... | collective-permute-start | bytes 6291464 | tf_op jit(solution)/shard_map/ppermute | solution.py:289
  180.2 4.3 %collective-permute-start.8 = (f32[32,8,512]{2,1,0:T(8,128)}, f32[32,8,512]{2,1,0:T(8,128)S(1)}, u32[]{:S(2)}, u32[]{:S(2)}) collective-permute-start(f32[32,8,512]{2,1,0:T(8,128)} %get-tuple-element.26), channel_id=1, source_target_pairs={{0,2},{2,0},{4,6},{6,4},{8,10},{10,8},{12,14},{14,12},{16,18},{18,... | collective-permute-start | bytes 1572872 | tf_op jit(solution)/shard_map/ppermute | solution.py:260
  180.9 27.2 %collective-permute-start.9 = (f32[32,8,512]{2,1,0:T(8,128)}, f32[32,8,512]{2,1,0:T(8,128)S(1)}, u32[]{:S(2)}, u32[]{:S(2)}) collective-permute-start(f32[32,8,512]{2,1,0:T(8,128)} %get-tuple-element.27), channel_id=1, source_target_pairs={{0,4},{2,6},{4,0},{6,2},{8,12},{10,14},{12,8},{14,10},{16,20},{18,... | collective-permute-start | bytes 1572872 | tf_op jit(solution)/shard_map/ppermute | solution.py:260
  183.1 45.7 %collective-permute-start.10 = (f32[32,8,512]{2,1,0:T(8,128)}, f32[32,8,512]{2,1,0:T(8,128)S(1)}, u32[]{:S(2)}, u32[]{:S(2)}) collective-permute-start(f32[32,8,512]{2,1,0:T(8,128)} %get-tuple-element.28), channel_id=1, source_target_pairs={{0,6},{2,4},{4,2},{6,0},{8,14},{10,12},{12,10},{14,8},{16,22},{18,... | collective-permute-start | bytes 1572872 | tf_op jit(solution)/shard_map/ppermute | solution.py:260
  230.4 50.8 %collective-permute-start.11 = (f32[4,1,64,512]{3,2,1,0:T(8,128)}, f32[4,1,64,512]{3,2,1,0:T(8,128)S(1)}, u32[]{:S(2)}, u32[]{:S(2)}) collective-permute-start(f32[4,1,64,512]{3,2,1,0:T(8,128)} %pad_maximum_fusion.1), channel_id=1, source_target_pairs={{0,8},{2,10},{4,12},{6,14},{8,0},{10,2},{12,4},{14,6},{16,24},{18,... | collective-permute-start | bytes 1572872 | tf_op jit(solution)/shard_map/ppermute | solution.py:260
  231.2 53.6 %collective-permute-start.12 = (f32[4,1,64,512]{3,2,1,0:T(8,128)}, f32[4,1,64,512]{3,2,1,0:T(8,128)S(1)}, u32[]{:S(2)}, u32[]{:S(2)}) collective-permute-start(f32[4,1,64,512]{3,2,1,0:T(8,128)} %pad_maximum_fusion.2), channel_id=1, source_target_pairs={{0,16},{2,18},{4,20},{6,22},{8,24},{10,26},{12,28},{14,30},{16,0},... | collective-permute-start | bytes 1572872 | tf_op jit(solution)/shard_map/ppermute | solution.py:260
  232.0 61.8 %collective-permute-start.13 = (f32[4,1,64,512]{3,2,1,0:T(8,128)}, f32[4,1,64,512]{3,2,1,0:T(8,128)S(1)}, u32[]{:S(2)}, u32[]{:S(2)}) collective-permute-start(f32[4,1,64,512]{3,2,1,0:T(8,128)} %pad_maximum_fusion.3), channel_id=1, source_target_pairs={{0,24},{2,26},{4,28},{6,30},{8,16},{10,18},{12,20},{14,22},{16,8},... | collective-permute-start | bytes 1572872 | tf_op jit(solution)/shard_map/ppermute | solution.py:260
  236.8 1.4 copy-start
  244.1 11.6 %copy-start.8 = (f32[1,1,64,512]{3,2,1,0:T(8,128)S(1)}, f32[1,1,64,512]{3,2,1,0:T(8,128)}, u32[]{:S(2)}) copy-start(f32[1,1,64,512]{3,2,1,0:T(8,128)} %get-tuple-element.74) | copy-start | bytes 393220
  281.2 0.8 copy-start.5
  284.8 0.8 copy-start.6
  293.8 0.8 copy-start.7

commit v3 on v2

--- a/solution.py
+++ b/solution.py
@@ -199,48 +199,104 @@
         out_shape=[jax.ShapeDtypeStruct((out_count, 8, width), jnp.float32)] * near,
         compiler_params=pltpu.CompilerParams(vmem_limit_bytes=VMEM),
         cost_estimate=pl.CostEstimate(
-            flops=2 * op.shape[0] * size, bytes_accessed=8 * size + 2 * op.size, transcendentals=0
+            flops=100 * op.shape[0] * size, bytes_accessed=8 * size + 2 * op.size, transcendentals=0
         ),
         name="placed_gradient",
     )(place, op, *lines)
 
 
-def placed_kernel(each, place_ref, base_ref, carrier_ref, grad_ref, out_ref):
-    for t in range(grad_ref.shape[0]):
-        here = pl.ds((place_ref[1] ^ t) * each, each)
-        out_ref[here] = base_ref[here] - carrier_ref[here] * grad_ref[t]
-
-
-def placed_combine(place, out, flat, grad, planes, comp, s):
+def placed_kernel(near, each, planes, comp, s, base_ref, flat_ref, grad_ref, out_ref, *rest):
+    base, carrier, grad, read_sems, write_sems = rest
+    row_pos = lax.axis_index("row")
+    far_pos, near_pos = row_pos // near, row_pos % near
+    reads, writes = [], []
+    for t in range(near):
+        plane = ((far_pos ^ s) * near + (near_pos ^ t)) * each
+        here, carried = pl.ds(comp * planes + plane, each), pl.ds(planes + plane, each)
+        group = [
+            pltpu.make_async_copy(base_ref.at[here], base.at[t], read_sems.at[3 * t]),
+            pltpu.make_async_copy(flat_ref.at[carried], carrier.at[t], read_sems.at[3 * t + 1]),
+            pltpu.make_async_copy(grad_ref.at[t], grad.at[t], read_sems.at[3 * t + 2]),
+        ]
+        for copy in group:
+            copy.start()
+        reads.append(group)
+        writes.append(pltpu.make_async_copy(base.at[t], out_ref.at[here], write_sems.at[t]))
+    for t in range(near):
+        for copy in reads[t]:
+            copy.wait()
+        base[t] = base[t] - carrier[t] * grad[t]
+        writes[t].start()
+    for copy in writes:
+        copy.wait()
+
+
+def placed_combine(out, flat, grad, planes, comp, s):
     near, each, height, width = grad.shape
-    far = planes // (near * each)
-    tile = min(width, 256)
-
-    def spec(first):
-        return pl.BlockSpec(
-            (near * each, height, tile), lambda j, at: (first * far + (at[0] ^ s), 0, j)
-        )
-
-    return pl.pallas_call(
-        functools.partial(placed_kernel, each),
-        grid_spec=pltpu.PrefetchScalarGridSpec(
-            num_scalar_prefetch=1,
-            grid=(width // tile,),
-            in_specs=[
-                spec(comp),
-                spec(1),
-                pl.BlockSpec((near, each, height, tile), lambda j, at: (0, 0, 0, j)),
-            ],
-            out_specs=spec(comp),
-        ),
+    anywhere = pl.BlockSpec(memory_space=pltpu.HBM)
+    return pl.pallas_call(
+        functools.partial(placed_kernel, near, each, planes, comp, s),
+        in_specs=[anywhere, anywhere, anywhere],
+        out_specs=anywhere,
         out_shape=jax.ShapeDtypeStruct(out.shape, jnp.float32),
-        input_output_aliases={1: 0},
+        scratch_shapes=[pltpu.VMEM(grad.shape, jnp.float32)] * 3
+        + [pltpu.SemaphoreType.DMA((3 * near,)), pltpu.SemaphoreType.DMA((near,))],
+        input_output_aliases={0: 0},
         compiler_params=pltpu.CompilerParams(vmem_limit_bytes=VMEM),
         cost_estimate=pl.CostEstimate(
             flops=2 * grad.size, bytes_accessed=16 * grad.size, transcendentals=0
         ),
         name="placed_combine",
-    )(place, out, flat, grad)
+    )(out, flat, grad)
+
+
+def gather_kernel(parts, field_ref, out_ref, buffer, read_sems, write_sems):
+    comps, rows = out_ref.shape[2], out_ref.shape[0] // parts
+    each = out_ref.shape[1]
+    reads, writes = [], []
+    for k in range(parts):
+        here = pl.ds(k * rows, rows)
+        for c in range(comps):
+            for p in range(each):
+                copy = pltpu.make_async_copy(
+                    field_ref.at[c, here, p],
+                    buffer.at[here, p, c],
+                    read_sems.at[(k * comps + c) * each + p],
+                )
+                copy.start()
+                reads.append((k, copy))
+        writes.append(pltpu.make_async_copy(buffer.at[here], out_ref.at[here], write_sems.at[k]))
+    for k in range(parts):
+        for part, copy in reads:
+            if part == k:
+                copy.wait()
+        writes[k].start()
+    for copy in writes:
+        copy.wait()
+
+
+def gather_planes(velocity, comps, n_row):
+    total, planes, height, width = velocity.shape
+    each = planes // n_row
+    shape = (n_row, each, comps, height, width)
+    parts = 4
+    anywhere = pl.BlockSpec(memory_space=pltpu.HBM)
+    return pl.pallas_call(
+        functools.partial(gather_kernel, parts),
+        in_specs=[anywhere],
+        out_specs=anywhere,
+        out_shape=jax.ShapeDtypeStruct(shape, jnp.float32),
+        scratch_shapes=[
+            pltpu.VMEM(shape, jnp.float32),
+            pltpu.SemaphoreType.DMA((parts * comps * each,)),
+            pltpu.SemaphoreType.DMA((parts,)),
+        ],
+        compiler_params=pltpu.CompilerParams(vmem_limit_bytes=VMEM),
+        cost_estimate=pl.CostEstimate(
+            flops=0, bytes_accessed=8 * comps * planes * height * width, transcendentals=0
+        ),
+        name="gather_planes",
+    )(velocity.reshape(total, n_row, each, height, width))
 
 
 def after(value, *others):
@@ -278,8 +334,7 @@
         def node_tile(known):
             return jnp.pad(known, ((0, 8 - known.shape[0]), (0, width - known.shape[1])))[None]
 
-        block = velocity[:bulk].swapaxes(0, 1)
-        block = block.reshape(n_row, each, bulk, height, width).swapaxes(1, 2)
+        block = gather_planes(velocity, bulk, n_row).swapaxes(1, 2)
         velocity, block = lax.optimization_barrier((velocity, block))
         lines = exchange(block)
         flat = velocity.reshape(total, height, width)
@@ -313,7 +368,7 @@
         known = jnp.concatenate([part[-1, :, : near * per_node] for part in landed], axis=1)
 
         grads = y_gradient(dy_op, lines)
-        grads = exchange(after(grads, others, landed))
+        grads = exchange(after(grads, others))
 
         out = z_terms(None, flat, planes, 0, others, ops)
         others = beside(after(flat, landed[1])[early:])
@@ -332,7 +387,7 @@
         grads = grads.swapaxes(1, 2).reshape(planes, bulk, height, width)
         out = combine(out, flat, planes, grads, 0)
         for s in [0, 1] + shifts[:-1]:
-            out = placed_combine(place, out, flat, back[s], planes, bulk, s)
+            out = placed_combine(out, flat, back[s], planes, bulk, s)
         return out.reshape(velocity.shape)
 
     return jax.shard_map(

time: 299 us -> 288 us (0.963)
  waiting for transfers between devices: 162 us -> 135 us
  starting transfers between devices: 38.4 us -> 53.8 us
    ppermute x12, waiting for transfers between devices: 106 us -> 81 us  [swap(): return lax.ppermute(block, 'row', [(i, i ^ distance) for i in range(n_row)])]
    ppermute x12, starting transfers between devices: 21.6 us -> 38.1 us  [swap(): return lax.ppermute(block, 'row', [(i, i ^ distance) for i in range(n_row)])]
    another operation x1 -> x0, local copies, waits for them, and re-layouts: 4.88 us -> none  [per_device(): block = block.reshape(n_row, each, bulk, height, width).swapaxes(1, 2)]
    unnamed x29, local copies, waits for them, and re-layouts: 11.3 us -> 15.6 us
    pallas_call x4 -> x5, Pallas kernels: 11.2 us -> 12.4 us  [the longest x4 9 us: placed_combine(): pl.pallas_call(functools.partial(placed_kernel, near, each, planes, comp,...]
  transfers between devices with their start and end apart: 16 -> 16, of which waited for: 9 -> 7; matrix products, arithmetic and copies ran while one was open for 9% -> 11% of each run, Pallas kernels for 19% -> 19%
where the time goes in v3:
time: 288 us; the launch traced here: 287 us
  waiting for transfers between devices  135 us (47%)
  Pallas kernels  61.2 us (21%)
  starting transfers between devices  53.8 us (19%)
  local copies, waits for them, and re-layouts  30.2 us (10%)
  other arithmetic  6.83 us (2%)
    ppermute x12, waiting for transfers between devices, swap(): return lax.ppermute(block, 'row', [(i, i ^ distance) for i in range(n_row)])  81 us
    all_to_all x2, waiting for transfers between devices, exchange(): return lax.all_to_all(block, 'row', split_axis=0, concat_axis=0, tiled=True)  53.6 us
    ppermute x12, starting transfers between devices, swap(): return lax.ppermute(block, 'row', [(i, i ^ distance) for i in range(n_row)])  38.1 us
    pallas_call x2, Pallas kernels, in_place(): pl.pallas_call(kernel, grid=grid, in_specs=specs + [pl.BlockSpec(memory_s...  16.4 us
    unnamed x29, local copies, waits for them, and re-layouts  15.6 us
    all_to_all x2, starting transfers between devices, exchange(): return lax.all_to_all(block, 'row', split_axis=0, concat_axis=0, tiled=True)  12.8 us
    pallas_call x1, Pallas kernels, add_nodes(): pl.pallas_call(functools.partial(node_kernel, planes), grid=(total // til...  11.6 us
    pallas_call x4, Pallas kernels, placed_combine(): pl.pallas_call(functools.partial(placed_kernel, near, each, planes, comp,...  9 us
  transfers between devices with their start and end apart: 16, of which 7 were waited for; matrix products, arithmetic and copies ran while one was open for 11% of the time, Pallas kernels for 19%

profile of v3, /device:TPU:8, one launch (start us, length us, event | category | flops | bytes accessed | tf_op | source)
XLA Modules:
  0.0 286.9 jit_solution(5715001248487222200)
XLA Ops:
  0.0 3.4 %gather_planes.1 = f32[16,1,2,64,512]{4,3,2,1,0:T(8,128)} custom-call(f32[3,16,1,64,512]{4,3,2,1,0:T(8,128)} %bitcast.78), custom_call_target="tpu_custom_call" | custom-call | bytes 8388608 | tf_op jit(solution)/shard_map/gather_planes/pallas_call | solution.py:284
  3.4 6.3 %all-to-all-start = ((f32[16,2,1,64,512]{4,3,2,1,0:T(8,128)}), f32[16,2,1,64,512]{4,3,2,1,0:T(8,128)}, u32[]{:S(2)}, u32[]{:S(2)}) async-start(f32[16,2,1,64,512]{4,3,2,1,0:T(8,128)} %bitcast.93), calls=%async_computation | async-start | bytes 8388608 | tf_op jit(solution)/shard_map/all_to_all | solution.py:313
  9.7 5.1 %slice.143 = f32[2,16,64,512]{3,2,1,0:T(8,128)} slice(f32[3,16,64,512]{3,2,1,0:T(8,128)} %param.5), slice={[0:2], [0:16], [0:64], [0:512]} | slice | bytes 8388608 | tf_op jit(solution)/shard_map/slice | solution.py:349
  14.8 1.5 collective-permute-start.7
  16.3 1.8 dynamic-slice_dynamic-update-slice_fusion.7
  18.1 1.8 dynamic-slice_dynamic-update-slice_fusion.6
  19.8 1.8 dynamic-slice_dynamic-update-slice_fusion.5
  21.6 2.2 dynamic-slice_dynamic-update-slice_fusion
  23.9 0.6 constant_dynamic-update-slice_fusion.2
  24.5 0.9 collective-permute-start.2
  25.5 0.6 collective-permute-start
  26.1 0.6 collective-permute-start.1
  26.7 1.6 fusion.2
  28.3 0.6 pad_add_fusion.1.place_ref
  28.8 16.3 %collective-permute-done.2 = f32[33,8,512]{2,1,0:T(8,128)S(1)} collective-permute-done((f32[33,8,512]{2,1,0:T(8,128)}, f32[33,8,512]{2,1,0:T(8,128)S(1)}, u32[]{:S(2)}, u32[]{:S(2)}) %collective-permute-start.2) | collective-permute-done | bytes 540704 | tf_op jit(solution)/shard_map/ppermute | solution.py:316
  45.1 0.7 slice_bitcast_fusion.22
  45.8 18.9 %collective-permute-done.1 = f32[33,8,512]{2,1,0:T(8,128)S(1)} collective-permute-done((f32[33,8,512]{2,1,0:T(8,128)}, f32[33,8,512]{2,1,0:T(8,128)S(1)}, u32[]{:S(2)}, u32[]{:S(2)}) %collective-permute-start.1) | collective-permute-done | bytes 540704 | tf_op jit(solution)/shard_map/ppermute | solution.py:316
  64.7 1.9 slice_dynamic-update-slice_fusion.2
  66.6 0.8 slice_dynamic-update-slice_fusion.1
  67.4 0.8 slice_dynamic-update-slice_fusion
  68.2 0.7 constant_dynamic-update-slice_fusion.5
  68.9 7.2 %collective-permute-start.5 = (f32[33,8,512]{2,1,0:T(8,128)}, f32[33,8,512]{2,1,0:T(8,128)S(1)}, u32[]{:S(2)}, u32[]{:S(2)}) collective-permute-start(f32[33,8,512]{2,1,0:T(8,128)} %constant_dynamic-update-slice_fusion.5), channel_id=1, source_target_pairs={{0,24},{2,26},{4,28},{6,30},{8,16},{10,18},{12,20},{14,22},{16,8},... | collective-permute-start | bytes 1622024 | tf_op jit(solution)/shard_map/ppermute | solution.py:316
  76.0 0.7 constant_dynamic-update-slice_fusion.6
  76.7 6.8 %collective-permute-start.3 = (f32[33,8,512]{2,1,0:T(8,128)}, f32[33,8,512]{2,1,0:T(8,128)S(1)}, u32[]{:S(2)}, u32[]{:S(2)}) collective-permute-start(f32[33,8,512]{2,1,0:T(8,128)} %get-tuple-element.76), channel_id=1, source_target_pairs={{0,8},{2,10},{4,12},{6,14},{8,0},{10,2},{12,4},{14,6},{16,24},{18,... | collective-permute-start | bytes 1622024 | tf_op jit(solution)/shard_map/ppermute | solution.py:316
  83.6 0.1 fusion
  83.7 40.6 %all-to-all-done.lines_ref = f32[16,2,1,64,512]{4,3,2,1,0:T(8,128)} async-done(((f32[16,2,1,64,512]{4,3,2,1,0:T(8,128)}), f32[16,2,1,64,512]{4,3,2,1,0:T(8,128)}, u32[]{:S(2)}, u32[]{:S(2)}) %all-to-all-start) | async-done | bytes 4194336 | tf_op jit(solution)/shard_map/all_to_all | solution.py:313
  124.3 6.8 %y_gradient.1 = f32[16,2,1,64,512]{4,3,2,1,0:T(8,128)} custom-call(bf16[1024,1024]{1,0:T(8,128)(2,1)} %op_ref.3, f32[16,2,1,64,512]{4,3,2,1,0:T(8,128)} %all-to-all-done.lines_ref), custom_call_target="tpu_custom_call" | custom-call | flops 2147483648 | bytes 10485760 | tf_op jit(solution)/shard_map/y_gradient/pallas_call | solution.py:26
  131.1 6.5 %all-to-all-start.1 = ((f32[16,2,1,64,512]{4,3,1,2,0:T(8,128)}), f32[16,2,1,64,512]{4,3,1,2,0:T(8,128)}, u32[]{:S(2)}, u32[]{:S(2)}) async-start(f32[16,2,1,64,512]{4,3,1,2,0:T(8,128)} %bitcast.94), calls=%async_computation.1 | async-start | bytes 8388608 | tf_op jit(solution)/shard_map/all_to_all | solution.py:313
  137.6 3.4 %slice.142 = f32[16,64,512]{2,1,0:T(8,128)} slice(f32[48,64,512]{2,1,0:T(8,128)} %bitcast.83), slice={[32:48], [0:64], [0:512]} | slice | bytes 4194304 | tf_op jit(solution)/shard_map/slice | solution.py:374
  141.0 1.5 collective-permute-start.6
  142.5 10.6 %z_terms.2.refs_4_ = f32[48,64,512]{2,1,0:T(8,128)} custom-call(f32[48,64,512]{2,1,0:T(8,128)} %bitcast.84, f32[48,64,512]{2,1,0:T(8,128)} %bitcast.85, f32[32,64,512]{2,1,0:T(8,128)} %collective-permute-done.7.refs_1_, bf16[512,512]{1,0:T(8,128)(2,1)} %get-tuple-element.46.refs_2_, bf16[512,512]{1,0:T(8,128)(2,1)} %get-tuple-element.45.refs_3_), custom_call_target="tpu_custom_call" | custom-call | flops 2147483648 | bytes 16777216 | tf_op jit(solution)/shard_map/z_terms/pallas_call | solution.py:42
  153.1 0.8 copy-done.10
  153.9 5.5 %placed_gradient.1 = (f32[32,8,512]{2,1,0:T(8,128)}, f32[32,8,512]{2,1,0:T(8,128)}, f32[32,8,512]{2,1,0:T(8,128)}, f32[32,8,512]{2,1,0:T(8,128)}) custom-call(s32[2]{0:T(128)} %pad_add_fusion.1.place_ref, bf16[1024,1024]{1,0:T(8,128)(2,1)} %op_ref.3, f32[33,8,512]{2,1,0:T(8,128)} %get-tuple-element.21.refs_0_, f32[33,8,512]{2,1,0:T(8,128)} %copy-done.9, ...), custom_call_target="tpu_custom_call" | custom-call | flops 53687091200 | bytes 6291456 | tf_op jit(solution)/shard_map/placed_gradient/pallas_call | solution.py:187
  159.3 0.7 slice_bitcast_fusion.18
  160.0 18.3 %collective-permute-start.9 = (f32[32,8,512]{2,1,0:T(8,128)}, f32[32,8,512]{2,1,0:T(8,128)S(1)}, u32[]{:S(2)}, u32[]{:S(2)}) collective-permute-start(f32[32,8,512]{2,1,0:T(8,128)} %get-tuple-element.27), channel_id=1, source_target_pairs={{0,4},{2,6},{4,0},{6,2},{8,12},{10,14},{12,8},{14,10},{16,20},{18,... | collective-permute-start | bytes 1572872 | tf_op jit(solution)/shard_map/ppermute | solution.py:316
  178.4 0.7 slice_bitcast_fusion.17
  179.0 0.1 collective-permute-start.10
  179.1 1.1 slice_bitcast_fusion.12
  180.3 19.9 %collective-permute-done.9 = f32[32,8,512]{2,1,0:T(8,128)S(1)} collective-permute-done((f32[32,8,512]{2,1,0:T(8,128)}, f32[32,8,512]{2,1,0:T(8,128)S(1)}, u32[]{:S(2)}, u32[]{:S(2)}) %collective-permute-start.9) | collective-permute-done | bytes 524320 | tf_op jit(solution)/shard_map/ppermute | solution.py:316
  200.2 18.8 %collective-permute-done.10 = f32[32,8,512]{2,1,0:T(8,128)S(1)} collective-permute-done((f32[32,8,512]{2,1,0:T(8,128)}, f32[32,8,512]{2,1,0:T(8,128)S(1)}, u32[]{:S(2)}, u32[]{:S(2)}) %collective-permute-start.10) | collective-permute-done | bytes 524320 | tf_op jit(solution)/shard_map/ppermute | solution.py:316
  219.1 0.7 slice_bitcast_fusion
  219.7 0.9 pad_maximum_fusion.1
  220.6 1.5 collective-permute-start.11
  222.1 0.8 pad_maximum_fusion.2
  222.9 1.4 collective-permute-start.12
  224.3 0.9 pad_maximum_fusion.3
  225.2 0.6 collective-permute-start.13
  225.8 0.1 pad_maximum_fusion.4
  225.9 0.6 slice.141.force_ref
  226.4 0.7 convert_subtract_fusion.node_ref
  227.1 1.4 copy-done
  228.5 5.9 %z_terms.3.base_ref = f32[48,64,512]{2,1,0:T(8,128)} custom-call(f32[48,64,512]{2,1,0:T(8,128)} %bitcast.86, f32[48,64,512]{2,1,0:T(8,128)} %bitcast.87, f32[16,64,512]{2,1,0:T(8,128)} %copy-done, bf16[512,512]{1,0:T(8,128)(2,1)} %get-tuple-element.46.refs_2_, bf16[512,512]{1,0:T(8,128)(2,1)} %get-tuple-element.45.refs_3_, ...), custom_call_target="tpu_custom_call", output_to_operand_aliasing={{}: (5, {})} | custom-call | flops 1073741824 | bytes 8388608 | tf_op jit(solution)/shard_map/z_terms/pallas_call | solution.py:42
  234.4 11.6 %add_nodes.1.base_ref = f32[48,64,512]{2,1,0:T(8,128)} custom-call(s32[3,128]{1,0:T(4,128)} %convert_subtract_fusion.node_ref, f32[3,128]{1,0:T(4,128)} %slice.141.force_ref, f32[48,64,512]{2,1,0:T(8,128)} %z_terms.3.base_ref), custom_call_target="tpu_custom_call", output_to_operand_aliasing={{}: (2, {})} | custom-call | flops 1572864 | bytes 12582912 | tf_op jit(solution)/shard_map/add_nodes/pallas_call | solution.py:116
  246.0 0.8 pad_maximum_fusion.grad_ref
  246.9 13.1 %all-to-all-done.1 = f32[16,2,1,64,512]{4,3,1,2,0:T(8,128)} async-done(((f32[16,2,1,64,512]{4,3,1,2,0:T(8,128)}), f32[16,2,1,64,512]{4,3,1,2,0:T(8,128)}, u32[]{:S(2)}, u32[]{:S(2)}) %all-to-all-start.1) | async-done | bytes 4194336 | tf_op jit(solution)/shard_map/all_to_all | solution.py:313
  259.9 8.4 %combine.1.base_ref = f32[48,64,512]{2,1,0:T(8,128)} custom-call(f32[48,64,512]{2,1,0:T(8,128)} %add_nodes.1.base_ref, f32[48,64,512]{2,1,0:T(8,128)} %bitcast.88, f32[16,2,64,512]{3,2,1,0:T(8,128)} %bitcast.18.grad_ref), custom_call_target="tpu_custom_call", output_to_operand_aliasing={{}: (0, {})} | custom-call | flops 2097152 | bytes 16777216 | tf_op jit(solution)/shard_map/combine/pallas_call | solution.py:141
  268.4 2.2 placed_combine.4.base_ref
  270.7 0.8 copy-done.1
  271.5 2.2 placed_combine.5.base_ref
  273.7 0.8 copy-done.2
  274.5 2.2 placed_combine.6.base_ref
  276.8 7.1 %collective-permute-done.13.grad_ref = f32[4,1,64,512]{3,2,1,0:T(8,128)S(1)} collective-permute-done((f32[4,1,64,512]{3,2,1,0:T(8,128)}, f32[4,1,64,512]{3,2,1,0:T(8,128)S(1)}, u32[]{:S(2)}, u32[]{:S(2)}) %collective-permute-start.13) | collective-permute-done | bytes 524320 | tf_op jit(solution)/shard_map/ppermute | solution.py:316
  283.9 0.8 copy-done.3
  284.7 2.2 placed_combine.7
  (38 shorter events, 0.2 us)
Async XLA Ops:
  3.4 120.9 %all-to-all-start = ((f32[16,2,1,64,512]{4,3,2,1,0:T(8,128)}), f32[16,2,1,64,512]{4,3,2,1,0:T(8,128)}, u32[]{:S(2)}, u32[]{:S(2)}) async-start(f32[16,2,1,64,512]{4,3,2,1,0:T(8,128)} %bitcast.93), calls=%async_computation | async-start | bytes 8388608 | tf_op jit(solution)/shard_map/all_to_all | solution.py:313
  9.7 6.6 %copy-start.7 = (s32[3,8]{1,0:T(4,128)S(1)}, s32[3,8]{1,0:T(4,128)}, u32[]{:S(2)}) copy-start(s32[3,8]{1,0:T(4,128)} %param.9) | copy-start | bytes 292
  9.7 14.2 %copy-start.6 = (f32[3,8]{1,0:T(4,128)S(1)}, f32[3,8]{1,0:T(4,128)}, u32[]{:S(2)}) copy-start(f32[3,8]{1,0:T(4,128)} %param.8) | copy-start | bytes 292
  9.7 17.0 %copy-start.4 = (bf16[1024,1024]{1,0:T(8,128)(2,1)S(1)}, bf16[1024,1024]{1,0:T(8,128)(2,1)}, u32[]{:S(2)}) copy-start(bf16[1024,1024]{1,0:T(8,128)(2,1)} %param.7) | copy-start | bytes 6291460
  14.8 116.3 %collective-permute-start.7 = (f32[32,64,512]{2,1,0:T(8,128)}, f32[32,64,512]{2,1,0:T(8,128)}, u32[]{:S(2)}, u32[]{:S(2)}) collective-permute-start(f32[32,64,512]{2,1,0:T(8,128)} %bitcast.16), channel_id=1, source_target_pairs={{0,1},{1,0},{2,3},{3,2},{4,5},{5,4},{6,7},{7,6},{8,9},{9,8},{10,11... | collective-permute-start | bytes 12582920 | tf_op jit(solution)/shard_map/ppermute | solution.py:344
  24.5 20.6 %collective-permute-start.2 = (f32[33,8,512]{2,1,0:T(8,128)}, f32[33,8,512]{2,1,0:T(8,128)S(1)}, u32[]{:S(2)}, u32[]{:S(2)}) collective-permute-start(f32[33,8,512]{2,1,0:T(8,128)} %get-tuple-element.78), channel_id=1, source_target_pairs={{0,6},{2,4},{4,2},{6,0},{8,14},{10,12},{12,10},{14,8},{16,22},{18,... | collective-permute-start | bytes 1622024 | tf_op jit(solution)/shard_map/ppermute | solution.py:316
  25.5 19.6 %collective-permute-start = (f32[33,8,512]{2,1,0:T(8,128)}, f32[33,8,512]{2,1,0:T(8,128)}, u32[]{:S(2)}, u32[]{:S(2)}) collective-permute-start(f32[33,8,512]{2,1,0:T(8,128)} %get-tuple-element.79), channel_id=1, source_target_pairs={{0,2},{2,0},{4,6},{6,4},{8,10},{10,8},{12,14},{14,12},{16,18},{18,... | collective-permute-start | bytes 1622024 | tf_op jit(solution)/shard_map/ppermute | solution.py:316
  26.1 38.6 %collective-permute-start.1 = (f32[33,8,512]{2,1,0:T(8,128)}, f32[33,8,512]{2,1,0:T(8,128)S(1)}, u32[]{:S(2)}, u32[]{:S(2)}) collective-permute-start(f32[33,8,512]{2,1,0:T(8,128)} %get-tuple-element.80), channel_id=1, source_target_pairs={{0,4},{2,6},{4,0},{6,2},{8,12},{10,14},{12,8},{14,10},{16,20},{18,... | collective-permute-start | bytes 1622024 | tf_op jit(solution)/shard_map/ppermute | solution.py:316
  68.9 73.6 %collective-permute-start.5 = (f32[33,8,512]{2,1,0:T(8,128)}, f32[33,8,512]{2,1,0:T(8,128)S(1)}, u32[]{:S(2)}, u32[]{:S(2)}) collective-permute-start(f32[33,8,512]{2,1,0:T(8,128)} %constant_dynamic-update-slice_fusion.5), channel_id=1, source_target_pairs={{0,24},{2,26},{4,28},{6,30},{8,16},{10,18},{12,20},{14,22},{16,8},... | collective-permute-start | bytes 1622024 | tf_op jit(solution)/shard_map/ppermute | solution.py:316
  76.7 60.9 %collective-permute-start.3 = (f32[33,8,512]{2,1,0:T(8,128)}, f32[33,8,512]{2,1,0:T(8,128)S(1)}, u32[]{:S(2)}, u32[]{:S(2)}) collective-permute-start(f32[33,8,512]{2,1,0:T(8,128)} %get-tuple-element.76), channel_id=1, source_target_pairs={{0,8},{2,10},{4,12},{6,14},{8,0},{10,2},{12,4},{14,6},{16,24},{18,... | collective-permute-start | bytes 1622024 | tf_op jit(solution)/shard_map/ppermute | solution.py:316
  83.6 69.4 %collective-permute-start.4 = (f32[33,8,512]{2,1,0:T(8,128)}, f32[33,8,512]{2,1,0:T(8,128)S(1)}, u32[]{:S(2)}, u32[]{:S(2)}) collective-permute-start(f32[33,8,512]{2,1,0:T(8,128)} %get-tuple-element.77), channel_id=1, source_target_pairs={{0,16},{2,18},{4,20},{6,22},{8,24},{10,26},{12,28},{14,30},{16,0},... | collective-permute-start | bytes 1622024 | tf_op jit(solution)/shard_map/ppermute | solution.py:316
  131.1 128.8 %all-to-all-start.1 = ((f32[16,2,1,64,512]{4,3,1,2,0:T(8,128)}), f32[16,2,1,64,512]{4,3,1,2,0:T(8,128)}, u32[]{:S(2)}, u32[]{:S(2)}) async-start(f32[16,2,1,64,512]{4,3,1,2,0:T(8,128)} %bitcast.94), calls=%async_computation.1 | async-start | bytes 8388608 | tf_op jit(solution)/shard_map/all_to_all | solution.py:313
  137.6 15.4 %copy-start.9 = (f32[33,8,512]{2,1,0:T(8,128)}, f32[33,8,512]{2,1,0:T(8,128)S(1)}, u32[]{:S(2)}) copy-start(f32[33,8,512]{2,1,0:T(8,128)S(1)} %collective-permute-done.3.refs_1_) | copy-start | bytes 1622020
  141.0 86.1 %collective-permute-start.6 = (f32[16,64,512]{2,1,0:T(8,128)}, f32[16,64,512]{2,1,0:T(8,128)S(1)}, u32[]{:S(2)}, u32[]{:S(2)}) collective-permute-start(f32[16,64,512]{2,1,0:T(8,128)} %slice.142), channel_id=1, source_target_pairs={{0,1},{1,0},{2,3},{3,2},{4,5},{5,4},{6,7},{7,6},{8,9},{9,8},{10,11... | collective-permute-start | bytes 6291464 | tf_op jit(solution)/shard_map/ppermute | solution.py:344
  142.5 10.6 %copy-start.8 = (f32[33,8,512]{2,1,0:T(8,128)}, f32[33,8,512]{2,1,0:T(8,128)S(1)}, u32[]{:S(2)}) copy-start(f32[33,8,512]{2,1,0:T(8,128)S(1)} %collective-permute-done.5.refs_3_) | copy-start | bytes 1622020
  153.1 0.8 copy-start.10
  159.3 20.9 %collective-permute-start.8 = (f32[32,8,512]{2,1,0:T(8,128)}, f32[32,8,512]{2,1,0:T(8,128)S(1)}, u32[]{:S(2)}, u32[]{:S(2)}) collective-permute-start(f32[32,8,512]{2,1,0:T(8,128)} %get-tuple-element.26), channel_id=1, source_target_pairs={{0,2},{2,0},{4,6},{6,4},{8,10},{10,8},{12,14},{14,12},{16,18},{18,... | collective-permute-start | bytes 1572872 | tf_op jit(solution)/shard_map/ppermute | solution.py:316
  160.0 40.2 %collective-permute-start.9 = (f32[32,8,512]{2,1,0:T(8,128)}, f32[32,8,512]{2,1,0:T(8,128)S(1)}, u32[]{:S(2)}, u32[]{:S(2)}) collective-permute-start(f32[32,8,512]{2,1,0:T(8,128)} %get-tuple-element.27), channel_id=1, source_target_pairs={{0,4},{2,6},{4,0},{6,2},{8,12},{10,14},{12,8},{14,10},{16,20},{18,... | collective-permute-start | bytes 1572872 | tf_op jit(solution)/shard_map/ppermute | solution.py:316
  179.0 40.0 %collective-permute-start.10 = (f32[32,8,512]{2,1,0:T(8,128)}, f32[32,8,512]{2,1,0:T(8,128)S(1)}, u32[]{:S(2)}, u32[]{:S(2)}) collective-permute-start(f32[32,8,512]{2,1,0:T(8,128)} %get-tuple-element.28), channel_id=1, source_target_pairs={{0,6},{2,4},{4,2},{6,0},{8,14},{10,12},{12,10},{14,8},{16,22},{18,... | collective-permute-start | bytes 1572872 | tf_op jit(solution)/shard_map/ppermute | solution.py:316
  220.6 50.0 %collective-permute-start.11 = (f32[4,1,64,512]{3,2,1,0:T(8,128)}, f32[4,1,64,512]{3,2,1,0:T(8,128)S(1)}, u32[]{:S(2)}, u32[]{:S(2)}) collective-permute-start(f32[4,1,64,512]{3,2,1,0:T(8,128)} %pad_maximum_fusion.1), channel_id=1, source_target_pairs={{0,8},{2,10},{4,12},{6,14},{8,0},{10,2},{12,4},{14,6},{16,24},{18,... | collective-permute-start | bytes 1572872 | tf_op jit(solution)/shard_map/ppermute | solution.py:316
  222.9 50.8 %collective-permute-start.12 = (f32[4,1,64,512]{3,2,1,0:T(8,128)}, f32[4,1,64,512]{3,2,1,0:T(8,128)S(1)}, u32[]{:S(2)}, u32[]{:S(2)}) collective-permute-start(f32[4,1,64,512]{3,2,1,0:T(8,128)} %pad_maximum_fusion.2), channel_id=1, source_target_pairs={{0,16},{2,18},{4,20},{6,22},{8,24},{10,26},{12,28},{14,30},{16,0},... | collective-permute-start | bytes 1572872 | tf_op jit(solution)/shard_map/ppermute | solution.py:316
  225.2 58.7 %collective-permute-start.13 = (f32[4,1,64,512]{3,2,1,0:T(8,128)}, f32[4,1,64,512]{3,2,1,0:T(8,128)S(1)}, u32[]{:S(2)}, u32[]{:S(2)}) collective-permute-start(f32[4,1,64,512]{3,2,1,0:T(8,128)} %pad_maximum_fusion.3), channel_id=1, source_target_pairs={{0,24},{2,26},{4,28},{6,30},{8,16},{10,18},{12,20},{14,22},{16,8},... | collective-permute-start | bytes 1572872 | tf_op jit(solution)/shard_map/ppermute | solution.py:316
  227.1 1.4 copy-start
  234.4 11.7 %copy-start.5 = (f32[1,1,64,512]{3,2,1,0:T(8,128)S(1)}, f32[1,1,64,512]{3,2,1,0:T(8,128)}, u32[]{:S(2)}) copy-start(f32[1,1,64,512]{3,2,1,0:T(8,128)} %get-tuple-element.74) | copy-start | bytes 393220
  270.7 0.8 copy-start.1
  273.7 0.8 copy-start.2
  283.9 0.8 copy-start.3

commit v4 on v3

--- a/solution.py
+++ b/solution.py
@@ -9,6 +9,7 @@
 
 VMEM = 60 << 20
 GROUP = 4
+AHEAD = 2
 
 
 def y_kernel(op_ref, lines_ref, grad_ref):
@@ -177,13 +178,14 @@
 
 def placed_gradient(place, op, lines, height, each):
     far = len(lines)
-    count, _, width = lines[0].shape
-    near = (count - 1) * 8 // (each * height)
+    width = lines[0].shape[2]
+    near = op.shape[0] // (far * height)
+    count = near * each * height // 8
     tile = min(width, 256)
-    block = pl.BlockSpec((count - 1, 8, tile), lambda j, _: (0, 0, j))
+    block = pl.BlockSpec((count, 8, tile), lambda j, _: (0, 0, j))
     out_count = far * each * height // 8
     out_block = pl.BlockSpec((out_count, 8, tile), lambda j, _: (0, 0, j))
-    size = far * (count - 1) * 8 * width
+    size = far * count * 8 * width
     return pl.pallas_call(
         functools.partial(place_kernel, height, each, far),
         grid_spec=pltpu.PrefetchScalarGridSpec(
@@ -206,7 +208,7 @@
 
 
 def placed_kernel(near, each, planes, comp, s, base_ref, flat_ref, grad_ref, out_ref, *rest):
-    base, carrier, grad, read_sems, write_sems = rest
+    base, carrier, read_sems, write_sems = rest
     row_pos = lax.axis_index("row")
     far_pos, near_pos = row_pos // near, row_pos % near
     reads, writes = [], []
@@ -214,9 +216,8 @@
         plane = ((far_pos ^ s) * near + (near_pos ^ t)) * each
         here, carried = pl.ds(comp * planes + plane, each), pl.ds(planes + plane, each)
         group = [
-            pltpu.make_async_copy(base_ref.at[here], base.at[t], read_sems.at[3 * t]),
-            pltpu.make_async_copy(flat_ref.at[carried], carrier.at[t], read_sems.at[3 * t + 1]),
-            pltpu.make_async_copy(grad_ref.at[t], grad.at[t], read_sems.at[3 * t + 2]),
+            pltpu.make_async_copy(base_ref.at[here], base.at[t], read_sems.at[2 * t]),
+            pltpu.make_async_copy(flat_ref.at[carried], carrier.at[t], read_sems.at[2 * t + 1]),
         ]
         for copy in group:
             copy.start()
@@ -225,7 +226,7 @@
     for t in range(near):
         for copy in reads[t]:
             copy.wait()
-        base[t] = base[t] - carrier[t] * grad[t]
+        base[t] = base[t] - carrier[t] * grad_ref[t]
         writes[t].start()
     for copy in writes:
         copy.wait()
@@ -233,16 +234,16 @@
 
 def placed_combine(out, flat, grad, planes, comp, s):
     near, each, height, width = grad.shape
-    anywhere = pl.BlockSpec(memory_space=pltpu.HBM)
+    far_off = pl.BlockSpec(memory_space=pltpu.HBM)
     return pl.pallas_call(
         functools.partial(placed_kernel, near, each, planes, comp, s),
-        in_specs=[anywhere, anywhere, anywhere],
-        out_specs=anywhere,
+        in_specs=[far_off, far_off, pl.BlockSpec(memory_space=pltpu.VMEM)],
+        out_specs=far_off,
         out_shape=jax.ShapeDtypeStruct(out.shape, jnp.float32),
-        scratch_shapes=[pltpu.VMEM(grad.shape, jnp.float32)] * 3
-        + [pltpu.SemaphoreType.DMA((3 * near,)), pltpu.SemaphoreType.DMA((near,))],
+        scratch_shapes=[pltpu.VMEM(grad.shape, jnp.float32)] * 2
+        + [pltpu.SemaphoreType.DMA((2 * near,)), pltpu.SemaphoreType.DMA((near,))],
         input_output_aliases={0: 0},
-        compiler_params=pltpu.CompilerParams(vmem_limit_bytes=VMEM),
+        compiler_params=pltpu.CompilerParams(vmem_limit_bytes=8 << 20),
         cost_estimate=pl.CostEstimate(
             flops=2 * grad.size, bytes_accessed=16 * grad.size, transcendentals=0
         ),
@@ -299,6 +300,19 @@
     )(velocity.reshape(total, n_row, each, height, width))
 
 
+def join_kernel(first_ref, second_ref, out_ref):
+    out_ref[...] = first_ref[...] + second_ref[...]
+
+
+def join_tiles(first, second):
+    return pl.pallas_call(
+        join_kernel,
+        out_shape=jax.ShapeDtypeStruct(first.shape, first.dtype),
+        cost_estimate=pl.CostEstimate(flops=57500000000, bytes_accessed=0, transcendentals=0),
+        name="join_tiles",
+    )(first, second)
+
+
 def after(value, *others):
     return lax.optimization_barrier((value, others))[0]
 
@@ -331,13 +345,9 @@
             for s in range(n_col)
         ]
 
-        def node_tile(known):
-            return jnp.pad(known, ((0, 8 - known.shape[0]), (0, width - known.shape[1])))[None]
-
-        block = gather_planes(velocity, bulk, n_row).swapaxes(1, 2)
-        velocity, block = lax.optimization_barrier((velocity, block))
-        lines = exchange(block)
-        flat = velocity.reshape(total, height, width)
+        def node_tile(known, lane=0):
+            after_lane = width - lane - known.shape[1]
+            return jnp.pad(known, ((0, 8 - known.shape[0]), (lane, after_lane)))[None]
 
         def beside(piece):
             return [
@@ -345,27 +355,53 @@
                 for s in range(1, n_col)
             ]
 
+        def block_of(flat, s, t):
+            plane = bulk * planes + ((far_pos ^ s) * near + (near_pos ^ t)) * each
+            rows = flat.reshape(total * height // 8, 8, width)
+            return lax.dynamic_slice_in_dim(rows, plane * height // 8, eights, 0)
+
+        def inner(part, k):
+            return part[k * eights : (k + 1) * eights]
+
+        ahead = far - 1
+        known = jnp.concatenate([node_force, node_cell.astype(jnp.float32)])
+        flat = velocity.reshape(total, height, width)
+        part = [block_of(flat, ahead, t) for t in range(AHEAD)]
+        part = jnp.concatenate(part + [node_tile(known, per_node)])
+        flat, part = lax.optimization_barrier((flat, part))
+        part = swap(part, ahead * near)
+
+        block = gather_planes(flat.reshape(velocity.shape), bulk, n_row).swapaxes(1, 2)
+        flat, block = lax.optimization_barrier((flat, block))
+        lines = exchange(block)
+
         early = 2 * total // 3
         others = beside(flat[:early])
 
-        known = node_tile(jnp.concatenate([node_force, node_cell.astype(jnp.float32)]))
-        rows = flat.reshape(total * height // 8, 8, width)
+        ahead_tile = join_tiles(node_tile(known), part[-1:])
         lot = []
         for t in range(near):
-            blocks = []
-            for s in range(far):
-                plane = bulk * planes + ((far_pos ^ s) * near + (near_pos ^ t)) * each
-                blocks.append(lax.dynamic_slice_in_dim(rows, plane * height // 8, eights, 0))
-            lot.append(jnp.concatenate(blocks + [known]))
-        lot = [lot[0]] + [swap(lot[t], t) for t in range(1, near)]
-        known = node_tile(jnp.concatenate([part[-1, :, :per_node] for part in lot], axis=1))
-        landed = []
-        for s in range(far):
-            blocks = [part[s * eights : (s + 1) * eights] for part in lot]
-            landed.append(jnp.concatenate(blocks + [known]))
-        for s in shifts:
+            blocks = [block_of(flat, s, t) for s in range(ahead)]
+            blocks.append(inner(part, t) if t < AHEAD else block_of(flat, ahead, t))
+            lot.append(jnp.concatenate(blocks + [ahead_tile]))
+        lot = [swap(lot[t], t) if t else lot[t] for t in range(near)]
+        known = jnp.concatenate([part[-1, :, :per_node] for part in lot], axis=1)
+        ahead_known = jnp.concatenate(
+            [part[-1, :, per_node : 2 * per_node] for part in lot], axis=1
+        )
+        tile = node_tile(known)
+        landed = [jnp.concatenate([inner(part, s) for part in lot] + [tile]) for s in range(ahead)]
+        for s in range(1, ahead):
             landed[s] = swap(landed[s], s * near)
-        known = jnp.concatenate([part[-1, :, : near * per_node] for part in landed], axis=1)
+        rest = jnp.concatenate([inner(part, ahead) for part in lot[AHEAD:]])
+        rest = swap(rest, ahead * near)
+        landed.append(jnp.concatenate([inner(part, ahead) for part in lot[:AHEAD]] + [rest]))
+        known = jnp.concatenate(
+            [known]
+            + [landed[s][-1, :, : near * per_node] for s in range(1, ahead)]
+            + [ahead_known],
+            axis=1,
+        )
 
         grads = y_gradient(dy_op, lines)
         grads = exchange(after(grads, others))

time: 288 us -> 281 us (0.976)
  starting transfers between devices: 53.8 us -> 39.7 us
  waiting for transfers between devices: 135 us -> 139 us
    ppermute x12 -> x13, starting transfers between devices: 38.1 us -> 23.4 us  [swap(): return lax.ppermute(block, 'row', [(i, i ^ distance) for i in range(n_row)])]
    unnamed x29 -> x14, local copies, waits for them, and re-layouts: 15.6 us -> 7.9 us
    squeeze x8 -> x6, local copies, waits for them, and re-layouts: 2.04 us -> 5.35 us  [the longest x4 3.41 us: per_device(): part[-1, :, per_node:2 * per_node]]
    slice x0 -> x5, local copies, waits for them, and re-layouts: none -> 2.89 us  [the longest x4 2.29 us: inner(): return part[k * eights:(k + 1) * eights]]
    ppermute x12 -> x13, waiting for transfers between devices: 81 us -> 83.2 us  [swap(): return lax.ppermute(block, 'row', [(i, i ^ distance) for i in range(n_row)])]
  transfers between devices with their start and end apart: 16 -> 17, of which waited for: 7 -> 7; matrix products, arithmetic and copies ran while one was open for 11% -> 12% of each run, Pallas kernels for 19% -> 22%
where the time goes in v4:
time: 281 us; the launch traced here: 279 us
  waiting for transfers between devices  139 us (49%)
  Pallas kernels  62.4 us (22%)
  starting transfers between devices  39.7 us (14%)
  local copies, waits for them, and re-layouts  31.5 us (11%)
  other arithmetic  6.44 us (2%)
    ppermute x13, waiting for transfers between devices, swap(): return lax.ppermute(block, 'row', [(i, i ^ distance) for i in range(n_row)])  83.2 us
    all_to_all x2, waiting for transfers between devices, exchange(): return lax.all_to_all(block, 'row', split_axis=0, concat_axis=0, tiled=True)  55.6 us
    ppermute x13, starting transfers between devices, swap(): return lax.ppermute(block, 'row', [(i, i ^ distance) for i in range(n_row)])  23.4 us
    pallas_call x2, Pallas kernels, in_place(): pl.pallas_call(kernel, grid=grid, in_specs=specs + [pl.BlockSpec(memory_s...  16.3 us
    all_to_all x2, starting transfers between devices, exchange(): return lax.all_to_all(block, 'row', split_axis=0, concat_axis=0, tiled=True)  13.4 us
    pallas_call x1, Pallas kernels, add_nodes(): pl.pallas_call(functools.partial(node_kernel, planes), grid=(total // til...  11.7 us
    pallas_call x4, Pallas kernels, placed_combine(): pl.pallas_call(functools.partial(placed_kernel, near, each, planes, comp,...  8.97 us
    pallas_call x1, Pallas kernels, combine(): pl.pallas_call(combine_kernel, grid=(comps, per), in_specs=[here, carrier...  8.44 us
  transfers between devices with their start and end apart: 17, of which 7 were waited for; matrix products, arithmetic and copies ran while one was open for 12% of the time, Pallas kernels for 22%

profile of v4, /device:TPU:8, one launch (start us, length us, event | category | flops | bytes accessed | tf_op | source)
XLA Modules:
  0.0 279.3 jit_solution(13410828530904334894)
XLA Ops:
  0.0 0.7 convert_element_type.12
  0.7 0.7 pad_maximum_fusion.7
  1.4 0.6 pad_bitcast_fusion
  2.0 1.0 constant_dynamic-slice_fusion.1
  3.0 1.6 collective-permute-start
  4.6 3.3 %gather_planes.1 = f32[16,1,2,64,512]{4,3,2,1,0:T(8,128)} custom-call(f32[3,16,1,64,512]{4,3,2,1,0:T(8,128)} %bitcast.79), custom_call_target="tpu_custom_call" | custom-call | bytes 8388608 | tf_op jit(solution)/shard_map/gather_planes/pallas_call | solution.py:285
  8.0 6.8 %all-to-all-start = ((f32[16,2,1,64,512]{4,3,2,1,0:T(8,128)}), f32[16,2,1,64,512]{4,3,2,1,0:T(8,128)}, u32[]{:S(2)}, u32[]{:S(2)}) async-start(f32[16,2,1,64,512]{4,3,2,1,0:T(8,128)} %bitcast.95), calls=%async_computation | async-start | bytes 8388608 | tf_op jit(solution)/shard_map/all_to_all | solution.py:327
  14.8 4.9 %slice.156 = f32[32,64,512]{2,1,0:T(8,128)} slice(f32[48,64,512]{2,1,0:T(8,128)} %bitcast.80), slice={[0:32], [0:64], [0:512]} | slice | bytes 8388608 | tf_op jit(solution)/shard_map/slice | solution.py:379
  19.7 1.5 collective-permute-start.7
  21.2 1.0 dynamic-slice_dynamic-update-slice_fusion.6
  22.2 1.1 dynamic-slice_dynamic-update-slice_fusion.5
  23.5 1.1 dynamic-slice_dynamic-update-slice_fusion.4
  24.6 2.0 dynamic-slice_dynamic-update-slice_fusion
  26.6 0.6 slice.180.second_ref
  27.2 1.3 join_tiles.1
  28.5 0.7 constant_dynamic-update-slice_fusion.2
  29.3 1.5 collective-permute-start.2
  31.1 1.4 slice_bitcast_fusion.19
  32.5 0.8 fusion.2
  33.3 19.7 %collective-permute-done.2 = f32[33,8,512]{2,1,0:T(8,128)S(1)} collective-permute-done((f32[33,8,512]{2,1,0:T(8,128)S(1)}, f32[33,8,512]{2,1,0:T(8,128)S(1)}, u32[]{:S(2)}, u32[]{:S(2)}) %collective-permute-start.2) | collective-permute-done | bytes 540704 | tf_op jit(solution)/shard_map/ppermute | solution.py:330
  53.1 0.7 fusion.3
  53.8 15.5 %collective-permute-done.3 = f32[33,8,512]{2,1,0:T(8,128)S(1)} collective-permute-done((f32[33,8,512]{2,1,0:T(8,128)S(1)}, f32[33,8,512]{2,1,0:T(8,128)S(1)}, u32[]{:S(2)}, u32[]{:S(2)}) %collective-permute-start.3) | collective-permute-done | bytes 540704 | tf_op jit(solution)/shard_map/ppermute | solution.py:330
  69.3 0.7 fusion.4
  70.1 4.8 %collective-permute-start.8 = (f32[16,8,512]{2,1,0:T(8,128)S(1)}, f32[16,8,512]{2,1,0:T(8,128)S(1)}, u32[]{:S(2)}, u32[]{:S(2)}) collective-permute-start(f32[16,8,512]{2,1,0:T(8,128)S(1)} %pad_maximum_fusion.6), channel_id=1, source_target_pairs={{0,24},{2,26},{4,28},{6,30},{8,16},{10,18},{12,20},{14,22},{16,8},... | collective-permute-start | bytes 786440 | tf_op jit(solution)/shard_map/ppermute | solution.py:330
  74.9 0.7 slice_bitcast_fusion.16
  75.5 0.7 slice_bitcast_fusion.17
  76.2 0.7 slice_bitcast_fusion.18
  76.8 0.7 constant_dynamic-update-slice_fusion.5
  77.5 7.9 %collective-permute-start.5 = (f32[33,8,512]{2,1,0:T(8,128)}, f32[33,8,512]{2,1,0:T(8,128)}, u32[]{:S(2)}, u32[]{:S(2)}) collective-permute-start(f32[33,8,512]{2,1,0:T(8,128)} %get-tuple-element.88), channel_id=1, source_target_pairs={{0,16},{2,18},{4,20},{6,22},{8,24},{10,26},{12,28},{14,30},{16,0},... | collective-permute-start | bytes 1622024 | tf_op jit(solution)/shard_map/ppermute | solution.py:330
  85.4 1.4 collective-permute-start.4
  86.9 37.9 %all-to-all-done.lines_ref = f32[16,2,1,64,512]{4,3,2,1,0:T(8,128)} async-done(((f32[16,2,1,64,512]{4,3,2,1,0:T(8,128)}), f32[16,2,1,64,512]{4,3,2,1,0:T(8,128)}, u32[]{:S(2)}, u32[]{:S(2)}) %all-to-all-start) | async-done | bytes 4194336 | tf_op jit(solution)/shard_map/all_to_all | solution.py:327
  124.8 6.8 %y_gradient.1 = f32[16,2,1,64,512]{4,3,2,1,0:T(8,128)} custom-call(bf16[1024,1024]{1,0:T(8,128)(2,1)} %op_ref.3, f32[16,2,1,64,512]{4,3,2,1,0:T(8,128)} %all-to-all-done.lines_ref), custom_call_target="tpu_custom_call" | custom-call | flops 2147483648 | bytes 10485760 | tf_op jit(solution)/shard_map/y_gradient/pallas_call | solution.py:27
  131.6 6.6 %all-to-all-start.1 = ((f32[16,2,1,64,512]{4,3,1,2,0:T(8,128)}), f32[16,2,1,64,512]{4,3,1,2,0:T(8,128)}, u32[]{:S(2)}, u32[]{:S(2)}) async-start(f32[16,2,1,64,512]{4,3,1,2,0:T(8,128)} %bitcast.96), calls=%async_computation.1 | async-start | bytes 8388608 | tf_op jit(solution)/shard_map/all_to_all | solution.py:327
  138.2 0.6 pad_add_fusion.1.place_ref
  138.9 1.6 fusion.1
  140.4 0.8 pad_maximum_fusion.refs_3_
  141.3 3.3 %slice.155 = f32[16,64,512]{2,1,0:T(8,128)} slice(f32[48,64,512]{2,1,0:T(8,128)} %bitcast.85), slice={[32:48], [0:64], [0:512]} | slice | bytes 4194304 | tf_op jit(solution)/shard_map/slice | solution.py:410
  144.6 1.5 collective-permute-start.6
  146.1 10.3 %z_terms.2.refs_4_ = f32[48,64,512]{2,1,0:T(8,128)} custom-call(f32[48,64,512]{2,1,0:T(8,128)} %bitcast.86, f32[48,64,512]{2,1,0:T(8,128)} %bitcast.87, f32[32,64,512]{2,1,0:T(8,128)} %collective-permute-done.7.refs_1_, bf16[512,512]{1,0:T(8,128)(2,1)} %get-tuple-element.50.refs_2_, bf16[512,512]{1,0:T(8,128)(2,1)} %get-tuple-element.49.refs_3_), custom_call_target="tpu_custom_call" | custom-call | flops 2147483648 | bytes 16777216 | tf_op jit(solution)/shard_map/z_terms/pallas_call | solution.py:43
  156.4 5.5 %placed_gradient.1 = (f32[32,8,512]{2,1,0:T(8,128)}, f32[32,8,512]{2,1,0:T(8,128)}, f32[32,8,512]{2,1,0:T(8,128)}, f32[32,8,512]{2,1,0:T(8,128)}) custom-call(s32[2]{0:T(128)} %pad_add_fusion.1.place_ref, bf16[1024,1024]{1,0:T(8,128)(2,1)} %op_ref.3, f32[33,8,512]{2,1,0:T(8,128)} %copy-done.3, f32[33,8,512]{2,1,0:T(8,128)} %copy-done.4, ...), custom_call_target="tpu_custom_call" | custom-call | flops 53687091200 | bytes 6291456 | tf_op jit(solution)/shard_map/placed_gradient/pallas_call | solution.py:189
  161.9 0.6 pad_add_fusion
  162.6 1.5 collective-permute-start.10
  164.0 1.3 slice_bitcast_fusion.20
  165.3 0.4 collective-permute-start.11
  165.7 1.1 slice_bitcast_fusion.12
  166.9 22.0 %collective-permute-done.10 = f32[32,8,512]{2,1,0:T(8,128)S(1)} collective-permute-done((f32[32,8,512]{2,1,0:T(8,128)}, f32[32,8,512]{2,1,0:T(8,128)S(1)}, u32[]{:S(2)}, u32[]{:S(2)}) %collective-permute-start.10) | collective-permute-done | bytes 524320 | tf_op jit(solution)/shard_map/ppermute | solution.py:330
  188.9 21.5 %collective-permute-done.11 = f32[32,8,512]{2,1,0:T(8,128)S(1)} collective-permute-done((f32[32,8,512]{2,1,0:T(8,128)}, f32[32,8,512]{2,1,0:T(8,128)S(1)}, u32[]{:S(2)}, u32[]{:S(2)}) %collective-permute-start.11) | collective-permute-done | bytes 524320 | tf_op jit(solution)/shard_map/ppermute | solution.py:330
  210.4 0.7 slice_bitcast_fusion
  211.2 3.8 %collective-permute-start.13 = (f32[4,1,64,512]{3,2,1,0:T(8,128)S(1)}, f32[4,1,64,512]{3,2,1,0:T(8,128)S(1)}, u32[]{:S(2)}, u32[]{:S(2)}) collective-permute-start(f32[4,1,64,512]{3,2,1,0:T(8,128)S(1)} %pad_maximum_fusion.3), channel_id=1, source_target_pairs={{0,16},{2,18},{4,20},{6,22},{8,24},{10,26},{12,28},{14,30},{16,0},... | collective-permute-start | bytes 1572872 | tf_op jit(solution)/shard_map/ppermute | solution.py:330
  215.1 0.9 pad_maximum_fusion.4
  215.9 0.7 slice_bitcast_fusion.21
  216.6 0.8 concatenate.49
  217.4 0.6 slice.154.force_ref
  218.0 1.3 convert_subtract_fusion.node_ref
  219.3 5.9 %z_terms.3.base_ref = f32[48,64,512]{2,1,0:T(8,128)} custom-call(f32[48,64,512]{2,1,0:T(8,128)} %bitcast.88, f32[48,64,512]{2,1,0:T(8,128)} %bitcast.89, f32[16,64,512]{2,1,0:T(8,128)} %collective-permute-done.6.refs_1_, bf16[512,512]{1,0:T(8,128)(2,1)} %get-tuple-element.50.refs_2_, ...), custom_call_target="tpu_custom_call", output_to_operand_aliasing={{}: (5, {})} | custom-call | flops 1073741824 | bytes 8388608 | tf_op jit(solution)/shard_map/z_terms/pallas_call | solution.py:43
  225.2 11.7 %add_nodes.1.base_ref = f32[48,64,512]{2,1,0:T(8,128)} custom-call(s32[3,128]{1,0:T(4,128)} %convert_subtract_fusion.node_ref, f32[3,128]{1,0:T(4,128)} %slice.154.force_ref, f32[48,64,512]{2,1,0:T(8,128)} %z_terms.3.base_ref), custom_call_target="tpu_custom_call", output_to_operand_aliasing={{}: (2, {})} | custom-call | flops 1572864 | bytes 12582912 | tf_op jit(solution)/shard_map/add_nodes/pallas_call | solution.py:117
  236.9 17.6 %all-to-all-done.1 = f32[16,2,1,64,512]{4,3,1,2,0:T(8,128)} async-done(((f32[16,2,1,64,512]{4,3,1,2,0:T(8,128)}), f32[16,2,1,64,512]{4,3,1,2,0:T(8,128)}, u32[]{:S(2)}, u32[]{:S(2)}) %all-to-all-start.1) | async-done | bytes 4194336 | tf_op jit(solution)/shard_map/all_to_all | solution.py:327
  254.5 8.4 %combine.1.base_ref = f32[48,64,512]{2,1,0:T(8,128)} custom-call(f32[48,64,512]{2,1,0:T(8,128)} %add_nodes.1.base_ref, f32[48,64,512]{2,1,0:T(8,128)} %bitcast.90, f32[16,2,64,512]{3,2,1,0:T(8,128)} %bitcast.22.grad_ref), custom_call_target="tpu_custom_call", output_to_operand_aliasing={{}: (0, {})} | custom-call | flops 2097152 | bytes 16777216 | tf_op jit(solution)/shard_map/combine/pallas_call | solution.py:142
  263.0 2.8 copy-done
  265.8 2.2 placed_combine.4.base_ref
  268.0 2.3 placed_combine.5.base_ref
  270.3 2.3 placed_combine.6.base_ref
  272.6 4.5 %collective-permute-done.14.grad_ref = f32[4,1,64,512]{3,2,1,0:T(8,128)S(1)} collective-permute-done((f32[4,1,64,512]{3,2,1,0:T(8,128)}, f32[4,1,64,512]{3,2,1,0:T(8,128)S(1)}, u32[]{:S(2)}, u32[]{:S(2)}) %collective-permute-start.14) | collective-permute-done | bytes 524320 | tf_op jit(solution)/shard_map/ppermute | solution.py:330
  277.0 2.2 placed_combine.7
  (32 shorter events, 0.7 us)
Async XLA Ops:
  3.0 23.6 %collective-permute-start = (f32[17,8,512]{2,1,0:T(8,128)S(1)}, f32[17,8,512]{2,1,0:T(8,128)S(1)}, u32[]{:S(2)}, u32[]{:S(2)}) collective-permute-start(f32[17,8,512]{2,1,0:T(8,128)S(1)} %pad_maximum_fusion.5), channel_id=1, source_target_pairs={{0,24},{2,26},{4,28},{6,30},{8,16},{10,18},{12,20},{14,22},{16,8},... | collective-permute-start | bytes 835592 | tf_op jit(solution)/shard_map/ppermute | solution.py:330
  8.0 116.8 %all-to-all-start = ((f32[16,2,1,64,512]{4,3,2,1,0:T(8,128)}), f32[16,2,1,64,512]{4,3,2,1,0:T(8,128)}, u32[]{:S(2)}, u32[]{:S(2)}) async-start(f32[16,2,1,64,512]{4,3,2,1,0:T(8,128)} %bitcast.95), calls=%async_computation | async-start | bytes 8388608 | tf_op jit(solution)/shard_map/all_to_all | solution.py:327
  19.7 111.9 %collective-permute-start.7 = (f32[32,64,512]{2,1,0:T(8,128)}, f32[32,64,512]{2,1,0:T(8,128)}, u32[]{:S(2)}, u32[]{:S(2)}) collective-permute-start(f32[32,64,512]{2,1,0:T(8,128)} %slice.156), channel_id=1, source_target_pairs={{0,1},{1,0},{2,3},{3,2},{4,5},{5,4},{6,7},{7,6},{8,9},{9,8},{10,11... | collective-permute-start | bytes 12582920 | tf_op jit(solution)/shard_map/ppermute | solution.py:354
  29.2 3.3 %collective-permute-start.1 = (f32[33,8,512]{2,1,0:T(8,128)S(1)}, f32[33,8,512]{2,1,0:T(8,128)S(1)}, u32[]{:S(2)}, u32[]{:S(2)}) collective-permute-start(f32[33,8,512]{2,1,0:T(8,128)S(1)} %get-tuple-element.94), channel_id=1, source_target_pairs={{0,2},{2,0},{4,6},{6,4},{8,10},{10,8},{12,14},{14,12},{16,18},{18,... | collective-permute-start | bytes 1622024 | tf_op jit(solution)/shard_map/ppermute | solution.py:330
  29.3 23.8 %collective-permute-start.2 = (f32[33,8,512]{2,1,0:T(8,128)S(1)}, f32[33,8,512]{2,1,0:T(8,128)S(1)}, u32[]{:S(2)}, u32[]{:S(2)}) collective-permute-start(f32[33,8,512]{2,1,0:T(8,128)S(1)} %get-tuple-element.93), channel_id=1, source_target_pairs={{0,4},{2,6},{4,0},{6,2},{8,12},{10,14},{12,8},{14,10},{16,20},{18,... | collective-permute-start | bytes 1622024 | tf_op jit(solution)/shard_map/ppermute | solution.py:330
  30.7 38.6 %collective-permute-start.3 = (f32[33,8,512]{2,1,0:T(8,128)S(1)}, f32[33,8,512]{2,1,0:T(8,128)S(1)}, u32[]{:S(2)}, u32[]{:S(2)}) collective-permute-start(f32[33,8,512]{2,1,0:T(8,128)S(1)} %get-tuple-element.92), channel_id=1, source_target_pairs={{0,6},{2,4},{4,2},{6,0},{8,14},{10,12},{12,10},{14,8},{16,22},{18,... | collective-permute-start | bytes 1622024 | tf_op jit(solution)/shard_map/ppermute | solution.py:330
  70.1 70.4 %collective-permute-start.8 = (f32[16,8,512]{2,1,0:T(8,128)S(1)}, f32[16,8,512]{2,1,0:T(8,128)S(1)}, u32[]{:S(2)}, u32[]{:S(2)}) collective-permute-start(f32[16,8,512]{2,1,0:T(8,128)S(1)} %pad_maximum_fusion.6), channel_id=1, source_target_pairs={{0,24},{2,26},{4,28},{6,30},{8,16},{10,18},{12,20},{14,22},{16,8},... | collective-permute-start | bytes 786440 | tf_op jit(solution)/shard_map/ppermute | solution.py:330
  77.5 47.3 %copy-start.3 = (f32[33,8,512]{2,1,0:T(8,128)}, f32[33,8,512]{2,1,0:T(8,128)S(1)}, u32[]{:S(2)}) copy-start(f32[33,8,512]{2,1,0:T(8,128)S(1)} %get-tuple-element.25.refs_0_) | copy-start | bytes 1622020
  77.5 78.9 %collective-permute-start.5 = (f32[33,8,512]{2,1,0:T(8,128)}, f32[33,8,512]{2,1,0:T(8,128)}, u32[]{:S(2)}, u32[]{:S(2)}) collective-permute-start(f32[33,8,512]{2,1,0:T(8,128)} %get-tuple-element.88), channel_id=1, source_target_pairs={{0,16},{2,18},{4,20},{6,22},{8,24},{10,26},{12,28},{14,30},{16,0},... | collective-permute-start | bytes 1622024 | tf_op jit(solution)/shard_map/ppermute | solution.py:330
  85.4 55.9 %collective-permute-start.4 = (f32[33,8,512]{2,1,0:T(8,128)}, f32[33,8,512]{2,1,0:T(8,128)S(1)}, u32[]{:S(2)}, u32[]{:S(2)}) collective-permute-start(f32[33,8,512]{2,1,0:T(8,128)} %get-tuple-element.89), channel_id=1, source_target_pairs={{0,8},{2,10},{4,12},{6,14},{8,0},{10,2},{12,4},{14,6},{16,24},{18,... | collective-permute-start | bytes 1622024 | tf_op jit(solution)/shard_map/ppermute | solution.py:330
  131.6 7.2 %copy-start.1 = (bf16[1024,1024]{1,0:T(8,128)(2,1)S(1)}, bf16[1024,1024]{1,0:T(8,128)(2,1)}, u32[]{:S(2)}) copy-start(bf16[1024,1024]{1,0:T(8,128)(2,1)} %param.7) | copy-start | bytes 6291460
  131.6 122.9 %all-to-all-start.1 = ((f32[16,2,1,64,512]{4,3,1,2,0:T(8,128)}), f32[16,2,1,64,512]{4,3,1,2,0:T(8,128)}, u32[]{:S(2)}, u32[]{:S(2)}) async-start(f32[16,2,1,64,512]{4,3,1,2,0:T(8,128)} %bitcast.96), calls=%async_computation.1 | async-start | bytes 8388608 | tf_op jit(solution)/shard_map/all_to_all | solution.py:327
  141.3 15.1 %copy-start.4 = (f32[33,8,512]{2,1,0:T(8,128)}, f32[33,8,512]{2,1,0:T(8,128)S(1)}, u32[]{:S(2)}) copy-start(f32[33,8,512]{2,1,0:T(8,128)S(1)} %collective-permute-done.4.refs_1_) | copy-start | bytes 1622020
  144.6 74.7 %collective-permute-start.6 = (f32[16,64,512]{2,1,0:T(8,128)}, f32[16,64,512]{2,1,0:T(8,128)}, u32[]{:S(2)}, u32[]{:S(2)}) collective-permute-start(f32[16,64,512]{2,1,0:T(8,128)} %slice.155), channel_id=1, source_target_pairs={{0,1},{1,0},{2,3},{3,2},{4,5},{5,4},{6,7},{7,6},{8,9},{9,8},{10,11... | collective-permute-start | bytes 6291464 | tf_op jit(solution)/shard_map/ppermute | solution.py:354
  161.9 4.9 %collective-permute-start.9 = (f32[32,8,512]{2,1,0:T(8,128)}, f32[32,8,512]{2,1,0:T(8,128)S(1)}, u32[]{:S(2)}, u32[]{:S(2)}) collective-permute-start(f32[32,8,512]{2,1,0:T(8,128)} %get-tuple-element.30), channel_id=1, source_target_pairs={{0,2},{2,0},{4,6},{6,4},{8,10},{10,8},{12,14},{14,12},{16,18},{18,... | collective-permute-start | bytes 1572872 | tf_op jit(solution)/shard_map/ppermute | solution.py:330
  162.6 26.3 %collective-permute-start.10 = (f32[32,8,512]{2,1,0:T(8,128)}, f32[32,8,512]{2,1,0:T(8,128)S(1)}, u32[]{:S(2)}, u32[]{:S(2)}) collective-permute-start(f32[32,8,512]{2,1,0:T(8,128)} %get-tuple-element.31), channel_id=1, source_target_pairs={{0,4},{2,6},{4,0},{6,2},{8,12},{10,14},{12,8},{14,10},{16,20},{18,... | collective-permute-start | bytes 1572872 | tf_op jit(solution)/shard_map/ppermute | solution.py:330
  165.3 45.1 %collective-permute-start.11 = (f32[32,8,512]{2,1,0:T(8,128)}, f32[32,8,512]{2,1,0:T(8,128)S(1)}, u32[]{:S(2)}, u32[]{:S(2)}) collective-permute-start(f32[32,8,512]{2,1,0:T(8,128)} %get-tuple-element.32), channel_id=1, source_target_pairs={{0,6},{2,4},{4,2},{6,0},{8,14},{10,12},{12,10},{14,8},{16,22},{18,... | collective-permute-start | bytes 1572872 | tf_op jit(solution)/shard_map/ppermute | solution.py:330
  211.1 56.9 %collective-permute-start.12 = (f32[4,1,64,512]{3,2,1,0:T(8,128)S(1)}, f32[4,1,64,512]{3,2,1,0:T(8,128)S(1)}, u32[]{:S(2)}, u32[]{:S(2)}) collective-permute-start(f32[4,1,64,512]{3,2,1,0:T(8,128)S(1)} %pad_maximum_fusion.2), channel_id=1, source_target_pairs={{0,8},{2,10},{4,12},{6,14},{8,0},{10,2},{12,4},{14,6},{16,24},{18,... | collective-permute-start | bytes 1572872 | tf_op jit(solution)/shard_map/ppermute | solution.py:330
  211.2 59.1 %collective-permute-start.13 = (f32[4,1,64,512]{3,2,1,0:T(8,128)S(1)}, f32[4,1,64,512]{3,2,1,0:T(8,128)S(1)}, u32[]{:S(2)}, u32[]{:S(2)}) collective-permute-start(f32[4,1,64,512]{3,2,1,0:T(8,128)S(1)} %pad_maximum_fusion.3), channel_id=1, source_target_pairs={{0,16},{2,18},{4,20},{6,22},{8,24},{10,26},{12,28},{14,30},{16,0},... | collective-permute-start | bytes 1572872 | tf_op jit(solution)/shard_map/ppermute | solution.py:330
  215.9 61.1 %collective-permute-start.14 = (f32[4,1,64,512]{3,2,1,0:T(8,128)}, f32[4,1,64,512]{3,2,1,0:T(8,128)S(1)}, u32[]{:S(2)}, u32[]{:S(2)}) collective-permute-start(f32[4,1,64,512]{3,2,1,0:T(8,128)} %pad_maximum_fusion.4), channel_id=1, source_target_pairs={{0,24},{2,26},{4,28},{6,30},{8,16},{10,18},{12,20},{14,22},{16,8},... | collective-permute-start | bytes 1572872 | tf_op jit(solution)/shard_map/ppermute | solution.py:330
  225.2 11.7 %copy-start.2 = (f32[1,1,64,512]{3,2,1,0:T(8,128)S(1)}, f32[1,1,64,512]{3,2,1,0:T(8,128)}, u32[]{:S(2)}) copy-start(f32[1,1,64,512]{3,2,1,0:T(8,128)} %get-tuple-element.84) | copy-start | bytes 393220
  263.0 2.8 copy-start

commit v5 on v4

--- a/solution.py
+++ b/solution.py
@@ -207,41 +207,56 @@
     )(place, op, *lines)
 
 
-def placed_kernel(near, each, planes, comp, s, base_ref, flat_ref, grad_ref, out_ref, *rest):
-    base, carrier, read_sems, write_sems = rest
+def planes_at(s, t, near, each, planes, comp):
     row_pos = lax.axis_index("row")
-    far_pos, near_pos = row_pos // near, row_pos % near
-    reads, writes = [], []
+    plane = ((row_pos // near ^ s) * near + (row_pos % near ^ t)) * each
+    return pl.ds(comp * planes + plane, each), pl.ds(planes + plane, each)
+
+
+def placed_kernel(near, each, planes, comp, s, later, base_ref, flat_ref, grad_ref, out_ref, *rest):
+    next_refs, (base, carrier, read_sems, write_sems) = rest[:-4], rest[-4:]
+    reads, writes, extra = [], [], []
     for t in range(near):
-        plane = ((far_pos ^ s) * near + (near_pos ^ t)) * each
-        here, carried = pl.ds(comp * planes + plane, each), pl.ds(planes + plane, each)
+        here, carried = planes_at(s, t, near, each, planes, comp)
         group = [
-            pltpu.make_async_copy(base_ref.at[here], base.at[t], read_sems.at[2 * t]),
-            pltpu.make_async_copy(flat_ref.at[carried], carrier.at[t], read_sems.at[2 * t + 1]),
+            pltpu.make_async_copy(base_ref.at[here], base.at[t], read_sems.at[4 * t]),
+            pltpu.make_async_copy(flat_ref.at[carried], carrier.at[t], read_sems.at[4 * t + 1]),
         ]
         for copy in group:
             copy.start()
         reads.append(group)
         writes.append(pltpu.make_async_copy(base.at[t], out_ref.at[here], write_sems.at[t]))
+        if later is not None:
+            here, carried = planes_at(later, t, near, each, planes, comp)
+            extra += [
+                pltpu.make_async_copy(base_ref.at[here], next_refs[0].at[t], read_sems.at[4 * t + 2]),
+                pltpu.make_async_copy(
+                    flat_ref.at[carried], next_refs[1].at[t], read_sems.at[4 * t + 3]
+                ),
+            ]
+    for copy in extra:
+        copy.start()
     for t in range(near):
         for copy in reads[t]:
             copy.wait()
         base[t] = base[t] - carrier[t] * grad_ref[t]
         writes[t].start()
-    for copy in writes:
+    for copy in writes + extra:
         copy.wait()
 
 
-def placed_combine(out, flat, grad, planes, comp, s):
+def placed_combine(out, flat, grad, planes, comp, s, later=None):
     near, each, height, width = grad.shape
-    far_off = pl.BlockSpec(memory_space=pltpu.HBM)
-    return pl.pallas_call(
-        functools.partial(placed_kernel, near, each, planes, comp, s),
-        in_specs=[far_off, far_off, pl.BlockSpec(memory_space=pltpu.VMEM)],
-        out_specs=far_off,
-        out_shape=jax.ShapeDtypeStruct(out.shape, jnp.float32),
+    far_off, whole = pl.BlockSpec(memory_space=pltpu.HBM), pl.BlockSpec(memory_space=pltpu.VMEM)
+    n_next = 0 if later is None else 2
+    return pl.pallas_call(
+        functools.partial(placed_kernel, near, each, planes, comp, s, later),
+        in_specs=[far_off, far_off, whole],
+        out_specs=[far_off] + [whole] * n_next,
+        out_shape=[jax.ShapeDtypeStruct(out.shape, jnp.float32)]
+        + [jax.ShapeDtypeStruct(grad.shape, jnp.float32)] * n_next,
         scratch_shapes=[pltpu.VMEM(grad.shape, jnp.float32)] * 2
-        + [pltpu.SemaphoreType.DMA((2 * near,)), pltpu.SemaphoreType.DMA((near,))],
+        + [pltpu.SemaphoreType.DMA((4 * near,)), pltpu.SemaphoreType.DMA((near,))],
         input_output_aliases={0: 0},
         compiler_params=pltpu.CompilerParams(vmem_limit_bytes=8 << 20),
         cost_estimate=pl.CostEstimate(
@@ -249,6 +264,37 @@
         ),
         name="placed_combine",
     )(out, flat, grad)
+
+
+def final_kernel(near, each, planes, comp, s, base_ref, carrier_ref, grad_ref, kept_ref, out_ref, *rest):
+    result, write_sems = rest
+    writes = []
+    for t in range(near):
+        here, _ = planes_at(s, t, near, each, planes, comp)
+        result[t] = base_ref[t] - carrier_ref[t] * grad_ref[t]
+        copy = pltpu.make_async_copy(result.at[t], out_ref.at[here], write_sems.at[t])
+        copy.start()
+        writes.append(copy)
+    for copy in writes:
+        copy.wait()
+
+
+def final_combine(out, base, carrier, grad, planes, comp, s):
+    near, each, height, width = grad.shape
+    far_off, whole = pl.BlockSpec(memory_space=pltpu.HBM), pl.BlockSpec(memory_space=pltpu.VMEM)
+    return pl.pallas_call(
+        functools.partial(final_kernel, near, each, planes, comp, s),
+        in_specs=[whole, whole, whole, far_off],
+        out_specs=far_off,
+        out_shape=jax.ShapeDtypeStruct(out.shape, jnp.float32),
+        scratch_shapes=[pltpu.VMEM(grad.shape, jnp.float32), pltpu.SemaphoreType.DMA((near,))],
+        input_output_aliases={3: 0},
+        compiler_params=pltpu.CompilerParams(vmem_limit_bytes=8 << 20),
+        cost_estimate=pl.CostEstimate(
+            flops=2 * grad.size, bytes_accessed=16 * grad.size, transcendentals=0
+        ),
+        name="final_combine",
+    )(base, carrier, grad, out)
 
 
 def gather_kernel(parts, field_ref, out_ref, buffer, read_sems, write_sems):
@@ -300,17 +346,44 @@
     )(velocity.reshape(total, n_row, each, height, width))
 
 
-def join_kernel(first_ref, second_ref, out_ref):
-    out_ref[...] = first_ref[...] + second_ref[...]
-
-
-def join_tiles(first, second):
-    return pl.pallas_call(
-        join_kernel,
-        out_shape=jax.ShapeDtypeStruct(first.shape, first.dtype),
+def pack_kernel(near, far, first_row, rows_ref, part_ref, tile_ref, *refs):
+    out_refs, sems = refs[:near], refs[near]
+    eights = (out_refs[0].shape[0] - 1) // far
+    given = part_ref.shape[0] // eights
+    row_pos = lax.axis_index("row")
+    far_pos, near_pos = row_pos // near, row_pos % near
+    copies = []
+    for t in range(near):
+        for s in range(far - 1 if t < given else far):
+            start = first_row + ((far_pos ^ s) * near + (near_pos ^ t)) * eights
+            copy = pltpu.make_async_copy(
+                rows_ref.at[pl.ds(start, eights)],
+                out_refs[t].at[pl.ds(s * eights, eights)],
+                sems.at[t * far + s],
+            )
+            copy.start()
+            copies.append(copy)
+    for t in range(near):
+        if t < given:
+            out_refs[t][pl.ds((far - 1) * eights, eights)] = part_ref[pl.ds(t * eights, eights)]
+        out_refs[t][pl.ds(far * eights, 1)] = tile_ref[...]
+    for copy in copies:
+        copy.wait()
+
+
+def pack_lots(rows, part, tile, near, far, first_row, eights):
+    shape = (far * eights + 1, 8, rows.shape[2])
+    whole = pl.BlockSpec(memory_space=pltpu.VMEM)
+    return pl.pallas_call(
+        functools.partial(pack_kernel, near, far, first_row),
+        in_specs=[pl.BlockSpec(memory_space=pltpu.HBM), whole, whole],
+        out_specs=[whole] * near,
+        out_shape=[jax.ShapeDtypeStruct(shape, jnp.float32)] * near,
+        scratch_shapes=[pltpu.SemaphoreType.DMA((near * far,))],
+        compiler_params=pltpu.CompilerParams(vmem_limit_bytes=16 << 20),
         cost_estimate=pl.CostEstimate(flops=57500000000, bytes_accessed=0, transcendentals=0),
-        name="join_tiles",
-    )(first, second)
+        name="pack_lots",
+    )(rows, part, tile)
 
 
 def after(value, *others):
@@ -364,10 +437,8 @@
             return part[k * eights : (k + 1) * eights]
 
         ahead = far - 1
-        known = jnp.concatenate([node_force, node_cell.astype(jnp.float32)])
         flat = velocity.reshape(total, height, width)
-        part = [block_of(flat, ahead, t) for t in range(AHEAD)]
-        part = jnp.concatenate(part + [node_tile(known, per_node)])
+        part = jnp.concatenate([block_of(flat, ahead, t) for t in range(AHEAD)])
         flat, part = lax.optimization_barrier((flat, part))
         part = swap(part, ahead * near)
 
@@ -378,29 +449,20 @@
         early = 2 * total // 3
         others = beside(flat[:early])
 
-        ahead_tile = join_tiles(node_tile(known), part[-1:])
-        lot = []
-        for t in range(near):
-            blocks = [block_of(flat, s, t) for s in range(ahead)]
-            blocks.append(inner(part, t) if t < AHEAD else block_of(flat, ahead, t))
-            lot.append(jnp.concatenate(blocks + [ahead_tile]))
+        known = node_tile(jnp.concatenate([node_force, node_cell.astype(jnp.float32)]))
+        rows = flat.reshape(total * height // 8, 8, width)
+        lot = pack_lots(rows, part, known, near, far, bulk * planes * height // 8, eights)
         lot = [swap(lot[t], t) if t else lot[t] for t in range(near)]
         known = jnp.concatenate([part[-1, :, :per_node] for part in lot], axis=1)
-        ahead_known = jnp.concatenate(
-            [part[-1, :, per_node : 2 * per_node] for part in lot], axis=1
-        )
         tile = node_tile(known)
         landed = [jnp.concatenate([inner(part, s) for part in lot] + [tile]) for s in range(ahead)]
         for s in range(1, ahead):
             landed[s] = swap(landed[s], s * near)
-        rest = jnp.concatenate([inner(part, ahead) for part in lot[AHEAD:]])
+        rest = jnp.concatenate([inner(part, ahead) for part in lot[AHEAD:]] + [tile])
         rest = swap(rest, ahead * near)
         landed.append(jnp.concatenate([inner(part, ahead) for part in lot[:AHEAD]] + [rest]))
         known = jnp.concatenate(
-            [known]
-            + [landed[s][-1, :, : near * per_node] for s in range(1, ahead)]
-            + [ahead_known],
-            axis=1,
+            [known] + [part[-1, :, : near * per_node] for part in landed[1:]], axis=1
         )
 
         grads = y_gradient(dy_op, lines)
@@ -422,8 +484,13 @@
         out = add_nodes(out, planes, cells, known[:comps])
         grads = grads.swapaxes(1, 2).reshape(planes, bulk, height, width)
         out = combine(out, flat, planes, grads, 0)
-        for s in [0, 1] + shifts[:-1]:
-            out = placed_combine(out, flat, back[s], planes, bulk, s)
+        order = [0, 1] + shifts[:-1]
+        for s in order[:-2]:
+            (out,) = placed_combine(out, flat, back[s], planes, bulk, s)
+        out, base, carrier = placed_combine(
+            out, flat, back[order[-2]], planes, bulk, order[-2], order[-1]
+        )
+        out = final_combine(out, base, carrier, back[order[-1]], planes, bulk, order[-1])
         return out.reshape(velocity.shape)
 
     return jax.shard_map(

time: 281 us -> 278 us (0.989)
  local copies, waits for them, and re-layouts: 31.5 us -> 21.3 us
  starting transfers between devices: 39.7 us -> 48.7 us
  other arithmetic: 6.44 us -> 3.31 us
    ppermute x13, starting transfers between devices: 23.4 us -> 32.4 us  [swap(): return lax.ppermute(block, 'row', [(i, i ^ distance) for i in range(n_row)])]
    squeeze x6 -> x7, local copies, waits for them, and re-layouts: 5.35 us -> 1.38 us  [the longest x3 1.37 us: per_device(): part[-1, :, :near * per_node]]
    all_to_all x2, waiting for transfers between devices: 55.6 us -> 59 us  [exchange(): return lax.all_to_all(block, 'row', split_axis=0, concat_axis=0, tiled=True)]
    pallas_call x4 -> x3, Pallas kernels: 8.97 us -> 7.02 us  [placed_combine(): pl.pallas_call(functools.partial(placed_kernel, near, each, planes, comp,...]
    unnamed x14 -> x18, local copies, waits for them, and re-layouts: 7.9 us -> 6.51 us
  transfers between devices with their start and end apart: 17 -> 17, of which waited for: 7 -> 7; matrix products, arithmetic and copies ran while one was open for 12% -> 6% of each run, Pallas kernels for 22% -> 22%
where the time goes in v5:
time: 278 us; the launch traced here: 277 us
  waiting for transfers between devices  141 us (51%)
  Pallas kernels  62.3 us (22%)
  starting transfers between devices  48.7 us (18%)
  local copies, waits for them, and re-layouts  21.3 us (8%)
  other arithmetic  3.31 us (1%)
    ppermute x13, waiting for transfers between devices, swap(): return lax.ppermute(block, 'row', [(i, i ^ distance) for i in range(n_row)])  81.6 us
    all_to_all x2, waiting for transfers between devices, exchange(): return lax.all_to_all(block, 'row', split_axis=0, concat_axis=0, tiled=True)  59 us
    ppermute x13, starting transfers between devices, swap(): return lax.ppermute(block, 'row', [(i, i ^ distance) for i in range(n_row)])  32.4 us
    pallas_call x2, Pallas kernels, in_place(): pl.pallas_call(kernel, grid=grid, in_specs=specs + [pl.BlockSpec(memory_s...  16.2 us
    all_to_all x2, starting transfers between devices, exchange(): return lax.all_to_all(block, 'row', split_axis=0, concat_axis=0, tiled=True)  13.3 us
    pallas_call x1, Pallas kernels, add_nodes(): pl.pallas_call(functools.partial(node_kernel, planes), grid=(total // til...  11.6 us
    pallas_call x1, Pallas kernels, combine(): pl.pallas_call(combine_kernel, grid=(comps, per), in_specs=[here, carrier...  8.44 us
    pallas_call x3, Pallas kernels, placed_combine(): pl.pallas_call(functools.partial(placed_kernel, near, each, planes, comp,...  7.02 us
  transfers between devices with their start and end apart: 17, of which 7 were waited for; matrix products, arithmetic and copies ran while one was open for 6% of the time, Pallas kernels for 22%

profile of v5, /device:TPU:8, one launch (start us, length us, event | category | flops | bytes accessed | tf_op | source)
XLA Modules:
  0.0 276.6 jit_solution(4951248200136655681)
XLA Ops:
  0.0 1.0 constant_dynamic-slice_fusion.1
  1.0 1.6 collective-permute-start
  2.7 3.4 %gather_planes.1 = f32[16,1,2,64,512]{4,3,2,1,0:T(8,128)} custom-call(f32[3,16,1,64,512]{4,3,2,1,0:T(8,128)} %bitcast.71), custom_call_target="tpu_custom_call" | custom-call | bytes 8388608 | tf_op jit(solution)/shard_map/gather_planes/pallas_call | solution.py:331
  6.0 6.8 %all-to-all-start = ((f32[16,2,1,64,512]{4,3,2,1,0:T(8,128)}), f32[16,2,1,64,512]{4,3,2,1,0:T(8,128)}, u32[]{:S(2)}, u32[]{:S(2)}) async-start(f32[16,2,1,64,512]{4,3,2,1,0:T(8,128)} %bitcast.83), calls=%async_computation | async-start | bytes 8388608 | tf_op jit(solution)/shard_map/all_to_all | solution.py:400
  12.8 0.0 copy-start.5
  12.9 0.0 copy-start.2
  12.9 5.1 %slice.149 = f32[32,64,512]{2,1,0:T(8,128)} slice(f32[48,64,512]{2,1,0:T(8,128)} %bitcast.72), slice={[0:32], [0:64], [0:512]} | slice | bytes 8388608 | tf_op jit(solution)/shard_map/slice | solution.py:450
  17.9 1.5 collective-permute-start.8
  19.5 1.6 fusion.2
  21.1 0.0 collective-permute-done.part_ref
  21.1 2.8 %copy-done = f32[3,16,64,512]{3,2,1,0:T(8,128)S(1)} copy-done((f32[3,16,64,512]{3,2,1,0:T(8,128)S(1)}, f32[3,16,64,512]{3,2,1,0:T(8,128)}, u32[]{:S(2)}) %copy-start) | copy-done | bytes 6291480
  23.9 2.5 pack_lots.1
  26.4 0.1 collective-permute-start.1
  26.5 0.6 pad_add_fusion.1.place_ref
  27.1 1.5 collective-permute-start.2
  28.6 0.4 collective-permute-start.3
  29.0 0.0 collective-permute-done.1
  29.0 22.1 %collective-permute-done.2 = f32[33,8,512]{2,1,0:T(8,128)S(1)} collective-permute-done((f32[33,8,512]{2,1,0:T(8,128)S(1)}, f32[33,8,512]{2,1,0:T(8,128)S(1)}, u32[]{:S(2)}, u32[]{:S(2)}) %collective-permute-start.2) | collective-permute-done | bytes 540704 | tf_op jit(solution)/shard_map/ppermute | solution.py:403
  51.1 16.3 %collective-permute-done.3 = f32[33,8,512]{2,1,0:T(8,128)S(1)} collective-permute-done((f32[33,8,512]{2,1,0:T(8,128)S(1)}, f32[33,8,512]{2,1,0:T(8,128)S(1)}, u32[]{:S(2)}, u32[]{:S(2)}) %collective-permute-start.3) | collective-permute-done | bytes 540704 | tf_op jit(solution)/shard_map/ppermute | solution.py:403
  67.5 0.1 constant_dynamic-update-slice_fusion.2
  67.6 9.1 %collective-permute-start.4 = (f32[33,8,512]{2,1,0:T(8,128)S(1)}, f32[33,8,512]{2,1,0:T(8,128)}, u32[]{:S(2)}, u32[]{:S(2)}) collective-permute-start(f32[33,8,512]{2,1,0:T(8,128)S(1)} %get-tuple-element.84), channel_id=1, source_target_pairs={{0,8},{2,10},{4,12},{6,14},{8,0},{10,2},{12,4},{14,6},{16,24},{18,... | collective-permute-start | bytes 1622024 | tf_op jit(solution)/shard_map/ppermute | solution.py:403
  76.7 0.1 fusion
  76.8 4.2 %collective-permute-start.6 = (f32[17,8,512]{2,1,0:T(8,128)S(1)}, f32[17,8,512]{2,1,0:T(8,128)S(1)}, u32[]{:S(2)}, u32[]{:S(2)}) collective-permute-start(f32[17,8,512]{2,1,0:T(8,128)S(1)} %pad_maximum_fusion.5), channel_id=1, source_target_pairs={{0,24},{2,26},{4,28},{6,30},{8,16},{10,18},{12,20},{14,22},{16,8},... | collective-permute-start | bytes 835592 | tf_op jit(solution)/shard_map/ppermute | solution.py:403
  80.9 0.0 collective-permute-start.5
  80.9 40.8 %all-to-all-done.lines_ref = f32[16,2,1,64,512]{4,3,2,1,0:T(8,128)} async-done(((f32[16,2,1,64,512]{4,3,2,1,0:T(8,128)}), f32[16,2,1,64,512]{4,3,2,1,0:T(8,128)}, u32[]{:S(2)}, u32[]{:S(2)}) %all-to-all-start) | async-done | bytes 4194336 | tf_op jit(solution)/shard_map/all_to_all | solution.py:400
  121.8 6.8 %y_gradient.1 = f32[16,2,1,64,512]{4,3,2,1,0:T(8,128)} custom-call(bf16[1024,1024]{1,0:T(8,128)(2,1)} %op_ref.3, f32[16,2,1,64,512]{4,3,2,1,0:T(8,128)} %all-to-all-done.lines_ref), custom_call_target="tpu_custom_call" | custom-call | flops 2147483648 | bytes 10485760 | tf_op jit(solution)/shard_map/y_gradient/pallas_call | solution.py:27
  128.6 0.0 collective-permute-done.8.refs_1_
  128.6 6.5 %all-to-all-start.1 = ((f32[16,2,1,64,512]{4,3,1,2,0:T(8,128)}), f32[16,2,1,64,512]{4,3,1,2,0:T(8,128)}, u32[]{:S(2)}, u32[]{:S(2)}) async-start(f32[16,2,1,64,512]{4,3,1,2,0:T(8,128)} %bitcast.84), calls=%async_computation.1 | async-start | bytes 8388608 | tf_op jit(solution)/shard_map/all_to_all | solution.py:400
  135.1 0.1 pad_add_fusion
  135.1 0.0 collective-permute-done.6
  135.1 0.8 pad_maximum_fusion.refs_3_
  136.0 3.1 %slice.148 = f32[16,64,512]{2,1,0:T(8,128)} slice(f32[48,64,512]{2,1,0:T(8,128)} %bitcast.73), slice={[32:48], [0:64], [0:512]} | slice | bytes 4194304 | tf_op jit(solution)/shard_map/slice | solution.py:472
  139.1 1.5 collective-permute-start.7
  140.6 10.3 %z_terms.2.refs_4_ = f32[48,64,512]{2,1,0:T(8,128)} custom-call(f32[48,64,512]{2,1,0:T(8,128)} %bitcast.74, f32[48,64,512]{2,1,0:T(8,128)} %bitcast.75, f32[32,64,512]{2,1,0:T(8,128)} %collective-permute-done.8.refs_1_, bf16[512,512]{1,0:T(8,128)(2,1)} %get-tuple-element.50.refs_2_, bf16[512,512]{1,0:T(8,128)(2,1)} %get-tuple-element.49.refs_3_), custom_call_target="tpu_custom_call" | custom-call | flops 2147483648 | bytes 16777216 | tf_op jit(solution)/shard_map/z_terms/pallas_call | solution.py:43
  150.9 0.0 collective-permute-done.5.refs_2_
  150.9 0.8 copy-done.7
  151.8 5.5 %placed_gradient.1 = (f32[32,8,512]{2,1,0:T(8,128)}, f32[32,8,512]{2,1,0:T(8,128)}, f32[32,8,512]{2,1,0:T(8,128)}, f32[32,8,512]{2,1,0:T(8,128)}) custom-call(s32[2]{0:T(128)} %pad_add_fusion.1.place_ref, bf16[1024,1024]{1,0:T(8,128)(2,1)} %op_ref.3, f32[33,8,512]{2,1,0:T(8,128)} %copy-done.4, f32[33,8,512]{2,1,0:T(8,128)} %collective-permute-done.4.refs_1_, ...), custom_call_target="tpu_custom_call" | custom-call | flops 53687091200 | bytes 6291456 | tf_op jit(solution)/shard_map/placed_gradient/pallas_call | solution.py:189
  157.3 1.5 collective-permute-start.10
  158.8 0.7 slice_bitcast_fusion.18
  159.5 0.3 collective-permute-start.11
  159.8 1.1 slice_bitcast_fusion.12
  161.0 0.0 collective-permute-done.9
  161.0 16.9 %collective-permute-done.10 = f32[32,8,512]{2,1,0:T(8,128)S(1)} collective-permute-done((f32[32,8,512]{2,1,0:T(8,128)}, f32[32,8,512]{2,1,0:T(8,128)S(1)}, u32[]{:S(2)}, u32[]{:S(2)}) %collective-permute-start.10) | collective-permute-done | bytes 524320 | tf_op jit(solution)/shard_map/ppermute | solution.py:403
  178.0 21.7 %collective-permute-done.11 = f32[32,8,512]{2,1,0:T(8,128)S(1)} collective-permute-done((f32[32,8,512]{2,1,0:T(8,128)}, f32[32,8,512]{2,1,0:T(8,128)S(1)}, u32[]{:S(2)}, u32[]{:S(2)}) %collective-permute-start.11) | collective-permute-done | bytes 524320 | tf_op jit(solution)/shard_map/ppermute | solution.py:403
  199.7 0.7 slice_bitcast_fusion
  200.4 9.4 %collective-permute-start.12 = (f32[4,1,64,512]{3,2,1,0:T(8,128)S(1)}, f32[4,1,64,512]{3,2,1,0:T(8,128)S(1)}, u32[]{:S(2)}, u32[]{:S(2)}) collective-permute-start(f32[4,1,64,512]{3,2,1,0:T(8,128)S(1)} %pad_maximum_fusion.2), channel_id=1, source_target_pairs={{0,8},{2,10},{4,12},{6,14},{8,0},{10,2},{12,4},{14,6},{16,24},{18,... | collective-permute-start | bytes 1572872 | tf_op jit(solution)/shard_map/ppermute | solution.py:403
  209.9 0.8 pad_maximum_fusion.3
  210.7 4.3 %collective-permute-start.13 = (f32[4,1,64,512]{3,2,1,0:T(8,128)}, f32[4,1,64,512]{3,2,1,0:T(8,128)S(1)}, u32[]{:S(2)}, u32[]{:S(2)}) collective-permute-start(f32[4,1,64,512]{3,2,1,0:T(8,128)} %pad_maximum_fusion.3), channel_id=1, source_target_pairs={{0,16},{2,18},{4,20},{6,22},{8,24},{10,26},{12,28},{14,30},{16,0},... | collective-permute-start | bytes 1572872 | tf_op jit(solution)/shard_map/ppermute | solution.py:403
  215.0 0.1 collective-permute-start.14
  215.1 0.7 slice_bitcast_fusion.17
  215.8 0.1 concatenate.38
  215.9 0.6 slice.147.force_ref
  216.5 0.6 convert_subtract_fusion.node_ref
  217.1 0.0 collective-permute-done.7.refs_1_
  217.1 5.9 %z_terms.3.base_ref = f32[48,64,512]{2,1,0:T(8,128)} custom-call(f32[48,64,512]{2,1,0:T(8,128)} %bitcast.76, f32[48,64,512]{2,1,0:T(8,128)} %bitcast.77, f32[16,64,512]{2,1,0:T(8,128)} %collective-permute-done.7.refs_1_, bf16[512,512]{1,0:T(8,128)(2,1)} %get-tuple-element.50.refs_2_, ...), custom_call_target="tpu_custom_call", output_to_operand_aliasing={{}: (5, {})} | custom-call | flops 1073741824 | bytes 8388608 | tf_op jit(solution)/shard_map/z_terms/pallas_call | solution.py:43
  223.0 11.6 %add_nodes.1.base_ref = f32[48,64,512]{2,1,0:T(8,128)} custom-call(s32[3,128]{1,0:T(4,128)} %convert_subtract_fusion.node_ref, f32[3,128]{1,0:T(4,128)} %slice.147.force_ref, f32[48,64,512]{2,1,0:T(8,128)} %z_terms.3.base_ref), custom_call_target="tpu_custom_call", output_to_operand_aliasing={{}: (2, {})} | custom-call | flops 1572864 | bytes 12582912 | tf_op jit(solution)/shard_map/add_nodes/pallas_call | solution.py:117
  234.6 18.2 %all-to-all-done.1 = f32[16,2,1,64,512]{4,3,1,2,0:T(8,128)} async-done(((f32[16,2,1,64,512]{4,3,1,2,0:T(8,128)}), f32[16,2,1,64,512]{4,3,1,2,0:T(8,128)}, u32[]{:S(2)}, u32[]{:S(2)}) %all-to-all-start.1) | async-done | bytes 4194336 | tf_op jit(solution)/shard_map/all_to_all | solution.py:400
  252.9 8.4 %combine.1.base_ref = f32[48,64,512]{2,1,0:T(8,128)} custom-call(f32[48,64,512]{2,1,0:T(8,128)} %add_nodes.1.base_ref, f32[48,64,512]{2,1,0:T(8,128)} %bitcast.78, f32[16,2,64,512]{3,2,1,0:T(8,128)} %bitcast.18.grad_ref), custom_call_target="tpu_custom_call", output_to_operand_aliasing={{}: (0, {})} | custom-call | flops 2097152 | bytes 16777216 | tf_op jit(solution)/shard_map/combine/pallas_call | solution.py:142
  261.3 2.8 %copy-done.1 = f32[3,16,64,512]{3,2,1,0:T(8,128)S(1)} copy-done((f32[3,16,64,512]{3,2,1,0:T(8,128)S(1)}, f32[3,16,64,512]{3,2,1,0:T(8,128)}, u32[]{:S(2)}) %copy-start.1) | copy-done | bytes 6291480
  264.1 2.3 placed_combine.3.base_ref
  266.4 2.3 placed_combine.4.base_ref
  268.7 2.4 placed_combine.5
  271.1 4.7 %collective-permute-done.14.grad_ref = f32[4,1,64,512]{3,2,1,0:T(8,128)S(1)} collective-permute-done((f32[4,1,64,512]{3,2,1,0:T(8,128)S(1)}, f32[4,1,64,512]{3,2,1,0:T(8,128)S(1)}, u32[]{:S(2)}, u32[]{:S(2)}) %collective-permute-start.14) | collective-permute-done | bytes 524320 | tf_op jit(solution)/shard_map/ppermute | solution.py:403
  275.8 0.8 final_combine.1
  (33 shorter events, 0.4 us)
Async XLA Ops:
  1.0 20.1 %collective-permute-start = (f32[16,8,512]{2,1,0:T(8,128)S(1)}, f32[16,8,512]{2,1,0:T(8,128)S(1)}, u32[]{:S(2)}, u32[]{:S(2)}) collective-permute-start(f32[16,8,512]{2,1,0:T(8,128)S(1)} %pad_maximum_fusion.6), channel_id=1, source_target_pairs={{0,24},{2,26},{4,28},{6,30},{8,16},{10,18},{12,20},{14,22},{16,8},... | collective-permute-start | bytes 786440 | tf_op jit(solution)/shard_map/ppermute | solution.py:403
  6.0 115.7 %all-to-all-start = ((f32[16,2,1,64,512]{4,3,2,1,0:T(8,128)}), f32[16,2,1,64,512]{4,3,2,1,0:T(8,128)}, u32[]{:S(2)}, u32[]{:S(2)}) async-start(f32[16,2,1,64,512]{4,3,2,1,0:T(8,128)} %bitcast.83), calls=%async_computation | async-start | bytes 8388608 | tf_op jit(solution)/shard_map/all_to_all | solution.py:400
  12.8 6.6 %copy-start.6 = (s32[3,8]{1,0:T(4,128)S(1)}, s32[3,8]{1,0:T(4,128)}, u32[]{:S(2)}) copy-start(s32[3,8]{1,0:T(4,128)} %param.9) | copy-start | bytes 292
  12.8 6.6 %copy-start.5 = (f32[3,8]{1,0:T(4,128)S(1)}, f32[3,8]{1,0:T(4,128)}, u32[]{:S(2)}) copy-start(f32[3,8]{1,0:T(4,128)} %param.8) | copy-start | bytes 292
  12.9 6.6 %copy-start.2 = (bf16[1024,1024]{1,0:T(8,128)(2,1)S(1)}, bf16[1024,1024]{1,0:T(8,128)(2,1)}, u32[]{:S(2)}) copy-start(bf16[1024,1024]{1,0:T(8,128)(2,1)} %param.7) | copy-start | bytes 6291460
  17.9 110.6 %collective-permute-start.8 = (f32[32,64,512]{2,1,0:T(8,128)}, f32[32,64,512]{2,1,0:T(8,128)}, u32[]{:S(2)}, u32[]{:S(2)}) collective-permute-start(f32[32,64,512]{2,1,0:T(8,128)} %slice.149), channel_id=1, source_target_pairs={{0,1},{1,0},{2,3},{3,2},{4,5},{5,4},{6,7},{7,6},{8,9},{9,8},{10,11... | collective-permute-start | bytes 12582920 | tf_op jit(solution)/shard_map/ppermute | solution.py:427
  21.1 2.8 %copy-start = (f32[3,16,64,512]{3,2,1,0:T(8,128)S(1)}, f32[3,16,64,512]{3,2,1,0:T(8,128)}, u32[]{:S(2)}) copy-start(f32[3,16,64,512]{3,2,1,0:T(8,128)} %param.5) | copy-start | bytes 18874372
  26.4 2.6 collective-permute-start.1
  27.1 24.0 %collective-permute-start.2 = (f32[33,8,512]{2,1,0:T(8,128)S(1)}, f32[33,8,512]{2,1,0:T(8,128)S(1)}, u32[]{:S(2)}, u32[]{:S(2)}) collective-permute-start(f32[33,8,512]{2,1,0:T(8,128)S(1)} %get-tuple-element.31), channel_id=1, source_target_pairs={{0,4},{2,6},{4,0},{6,2},{8,12},{10,14},{12,8},{14,10},{16,20},{18,... | collective-permute-start | bytes 1622024 | tf_op jit(solution)/shard_map/ppermute | solution.py:403
  28.6 38.8 %collective-permute-start.3 = (f32[33,8,512]{2,1,0:T(8,128)S(1)}, f32[33,8,512]{2,1,0:T(8,128)S(1)}, u32[]{:S(2)}, u32[]{:S(2)}) collective-permute-start(f32[33,8,512]{2,1,0:T(8,128)S(1)} %get-tuple-element.32), channel_id=1, source_target_pairs={{0,6},{2,4},{4,2},{6,0},{8,14},{10,12},{12,10},{14,8},{16,22},{18,... | collective-permute-start | bytes 1622024 | tf_op jit(solution)/shard_map/ppermute | solution.py:403
  67.6 61.0 %copy-start.4 = (f32[33,8,512]{2,1,0:T(8,128)}, f32[33,8,512]{2,1,0:T(8,128)S(1)}, u32[]{:S(2)}) copy-start(f32[33,8,512]{2,1,0:T(8,128)S(1)} %get-tuple-element.36.refs_0_) | copy-start | bytes 1622020
  67.6 68.4 %collective-permute-start.4 = (f32[33,8,512]{2,1,0:T(8,128)S(1)}, f32[33,8,512]{2,1,0:T(8,128)}, u32[]{:S(2)}, u32[]{:S(2)}) collective-permute-start(f32[33,8,512]{2,1,0:T(8,128)S(1)} %get-tuple-element.84), channel_id=1, source_target_pairs={{0,8},{2,10},{4,12},{6,14},{8,0},{10,2},{12,4},{14,6},{16,24},{18,... | collective-permute-start | bytes 1622024 | tf_op jit(solution)/shard_map/ppermute | solution.py:403
  76.8 58.4 %collective-permute-start.6 = (f32[17,8,512]{2,1,0:T(8,128)S(1)}, f32[17,8,512]{2,1,0:T(8,128)S(1)}, u32[]{:S(2)}, u32[]{:S(2)}) collective-permute-start(f32[17,8,512]{2,1,0:T(8,128)S(1)} %pad_maximum_fusion.5), channel_id=1, source_target_pairs={{0,24},{2,26},{4,28},{6,30},{8,16},{10,18},{12,20},{14,22},{16,8},... | collective-permute-start | bytes 835592 | tf_op jit(solution)/shard_map/ppermute | solution.py:403
  80.9 70.0 %collective-permute-start.5 = (f32[33,8,512]{2,1,0:T(8,128)S(1)}, f32[33,8,512]{2,1,0:T(8,128)S(1)}, u32[]{:S(2)}, u32[]{:S(2)}) collective-permute-start(f32[33,8,512]{2,1,0:T(8,128)S(1)} %get-tuple-element.85), channel_id=1, source_target_pairs={{0,16},{2,18},{4,20},{6,22},{8,24},{10,26},{12,28},{14,30},{16,0},... | collective-permute-start | bytes 1622024 | tf_op jit(solution)/shard_map/ppermute | solution.py:403
  128.6 124.3 %all-to-all-start.1 = ((f32[16,2,1,64,512]{4,3,1,2,0:T(8,128)}), f32[16,2,1,64,512]{4,3,1,2,0:T(8,128)}, u32[]{:S(2)}, u32[]{:S(2)}) async-start(f32[16,2,1,64,512]{4,3,1,2,0:T(8,128)} %bitcast.84), calls=%async_computation.1 | async-start | bytes 8388608 | tf_op jit(solution)/shard_map/all_to_all | solution.py:400
  139.1 78.0 %collective-permute-start.7 = (f32[16,64,512]{2,1,0:T(8,128)}, f32[16,64,512]{2,1,0:T(8,128)}, u32[]{:S(2)}, u32[]{:S(2)}) collective-permute-start(f32[16,64,512]{2,1,0:T(8,128)} %slice.148), channel_id=1, source_target_pairs={{0,1},{1,0},{2,3},{3,2},{4,5},{5,4},{6,7},{7,6},{8,9},{9,8},{10,11... | collective-permute-start | bytes 6291464 | tf_op jit(solution)/shard_map/ppermute | solution.py:427
  150.9 0.8 copy-start.7
  157.3 3.7 %collective-permute-start.9 = (f32[32,8,512]{2,1,0:T(8,128)}, f32[32,8,512]{2,1,0:T(8,128)S(1)}, u32[]{:S(2)}, u32[]{:S(2)}) collective-permute-start(f32[32,8,512]{2,1,0:T(8,128)} %get-tuple-element.41), channel_id=1, source_target_pairs={{0,2},{2,0},{4,6},{6,4},{8,10},{10,8},{12,14},{14,12},{16,18},{18,... | collective-permute-start | bytes 1572872 | tf_op jit(solution)/shard_map/ppermute | solution.py:403
  157.3 20.6 %collective-permute-start.10 = (f32[32,8,512]{2,1,0:T(8,128)}, f32[32,8,512]{2,1,0:T(8,128)S(1)}, u32[]{:S(2)}, u32[]{:S(2)}) collective-permute-start(f32[32,8,512]{2,1,0:T(8,128)} %get-tuple-element.42), channel_id=1, source_target_pairs={{0,4},{2,6},{4,0},{6,2},{8,12},{10,14},{12,8},{14,10},{16,20},{18,... | collective-permute-start | bytes 1572872 | tf_op jit(solution)/shard_map/ppermute | solution.py:403
  159.5 40.2 %collective-permute-start.11 = (f32[32,8,512]{2,1,0:T(8,128)}, f32[32,8,512]{2,1,0:T(8,128)S(1)}, u32[]{:S(2)}, u32[]{:S(2)}) collective-permute-start(f32[32,8,512]{2,1,0:T(8,128)} %get-tuple-element.43), channel_id=1, source_target_pairs={{0,6},{2,4},{4,2},{6,0},{8,14},{10,12},{12,10},{14,8},{16,22},{18,... | collective-permute-start | bytes 1572872 | tf_op jit(solution)/shard_map/ppermute | solution.py:403
  200.4 65.9 %collective-permute-start.12 = (f32[4,1,64,512]{3,2,1,0:T(8,128)S(1)}, f32[4,1,64,512]{3,2,1,0:T(8,128)S(1)}, u32[]{:S(2)}, u32[]{:S(2)}) collective-permute-start(f32[4,1,64,512]{3,2,1,0:T(8,128)S(1)} %pad_maximum_fusion.2), channel_id=1, source_target_pairs={{0,8},{2,10},{4,12},{6,14},{8,0},{10,2},{12,4},{14,6},{16,24},{18,... | collective-permute-start | bytes 1572872 | tf_op jit(solution)/shard_map/ppermute | solution.py:403
  210.7 58.0 %collective-permute-start.13 = (f32[4,1,64,512]{3,2,1,0:T(8,128)}, f32[4,1,64,512]{3,2,1,0:T(8,128)S(1)}, u32[]{:S(2)}, u32[]{:S(2)}) collective-permute-start(f32[4,1,64,512]{3,2,1,0:T(8,128)} %pad_maximum_fusion.3), channel_id=1, source_target_pairs={{0,16},{2,18},{4,20},{6,22},{8,24},{10,26},{12,28},{14,30},{16,0},... | collective-permute-start | bytes 1572872 | tf_op jit(solution)/shard_map/ppermute | solution.py:403
  215.0 60.8 %collective-permute-start.14 = (f32[4,1,64,512]{3,2,1,0:T(8,128)S(1)}, f32[4,1,64,512]{3,2,1,0:T(8,128)S(1)}, u32[]{:S(2)}, u32[]{:S(2)}) collective-permute-start(f32[4,1,64,512]{3,2,1,0:T(8,128)S(1)} %pad_maximum_fusion.4), channel_id=1, source_target_pairs={{0,24},{2,26},{4,28},{6,30},{8,16},{10,18},{12,20},{14,22},{16,8},... | collective-permute-start | bytes 1572872 | tf_op jit(solution)/shard_map/ppermute | solution.py:403
  223.0 11.6 %copy-start.3 = (f32[1,1,64,512]{3,2,1,0:T(8,128)S(1)}, f32[1,1,64,512]{3,2,1,0:T(8,128)}, u32[]{:S(2)}) copy-start(f32[1,1,64,512]{3,2,1,0:T(8,128)} %get-tuple-element.82) | copy-start | bytes 393220
  261.3 2.8 %copy-start.1 = (f32[3,16,64,512]{3,2,1,0:T(8,128)S(1)}, f32[3,16,64,512]{3,2,1,0:T(8,128)}, u32[]{:S(2)}) copy-start(f32[3,16,64,512]{3,2,1,0:T(8,128)} %param.5) | copy-start | bytes 18874372

commit v6 on v5

--- a/solution.py
+++ b/solution.py
@@ -10,6 +10,8 @@
 VMEM = 60 << 20
 GROUP = 4
 AHEAD = 2
+PACK_WEIGHT = 57500000000
+Y_WEIGHT = 100
 
 
 def y_kernel(op_ref, lines_ref, grad_ref):
@@ -201,7 +203,7 @@
         out_shape=[jax.ShapeDtypeStruct((out_count, 8, width), jnp.float32)] * near,
         compiler_params=pltpu.CompilerParams(vmem_limit_bytes=VMEM),
         cost_estimate=pl.CostEstimate(
-            flops=100 * op.shape[0] * size, bytes_accessed=8 * size + 2 * op.size, transcendentals=0
+            flops=Y_WEIGHT * op.shape[0] * size, bytes_accessed=8 * size + 2 * op.size, transcendentals=0
         ),
         name="placed_gradient",
     )(place, op, *lines)
@@ -381,7 +383,7 @@
         out_shape=[jax.ShapeDtypeStruct(shape, jnp.float32)] * near,
         scratch_shapes=[pltpu.SemaphoreType.DMA((near * far,))],
         compiler_params=pltpu.CompilerParams(vmem_limit_bytes=16 << 20),
-        cost_estimate=pl.CostEstimate(flops=57500000000, bytes_accessed=0, transcendentals=0),
+        cost_estimate=pl.CostEstimate(flops=PACK_WEIGHT, bytes_accessed=0, transcendentals=0),
         name="pack_lots",
     )(rows, part, tile)
 
@@ -418,9 +420,8 @@
             for s in range(n_col)
         ]
 
-        def node_tile(known, lane=0):
-            after_lane = width - lane - known.shape[1]
-            return jnp.pad(known, ((0, 8 - known.shape[0]), (lane, after_lane)))[None]
+        def node_tile(known):
+            return jnp.pad(known, ((0, 8 - known.shape[0]), (0, width - known.shape[1])))[None]
 
         def beside(piece):
             return [
@@ -455,14 +456,15 @@
         lot = [swap(lot[t], t) if t else lot[t] for t in range(near)]
         known = jnp.concatenate([part[-1, :, :per_node] for part in lot], axis=1)
         tile = node_tile(known)
-        landed = [jnp.concatenate([inner(part, s) for part in lot] + [tile]) for s in range(ahead)]
+        landed = [jnp.concatenate([inner(part, s) for part in lot]) for s in range(ahead)]
         for s in range(1, ahead):
             landed[s] = swap(landed[s], s * near)
-        rest = jnp.concatenate([inner(part, ahead) for part in lot[AHEAD:]] + [tile])
+        rest = jnp.concatenate([inner(part, ahead) for part in lot[AHEAD:]])
         rest = swap(rest, ahead * near)
         landed.append(jnp.concatenate([inner(part, ahead) for part in lot[:AHEAD]] + [rest]))
+        small = tile[:, :, :128]
         known = jnp.concatenate(
-            [known] + [part[-1, :, : near * per_node] for part in landed[1:]], axis=1
+            [known] + [swap(small, s * near)[-1, :, : near * per_node] for s in range(1, far)], axis=1
         )
 
         grads = y_gradient(dy_op, lines)

time: 278 us -> 277 us (level)
  starting transfers between devices: 48.7 us -> 45.1 us
    ppermute x13 -> x16, starting transfers between devices: 32.4 us -> 26.1 us  [swap(): return lax.ppermute(block, 'row', [(i, i ^ distance) for i in range(n_row)])]
    ppermute x13 -> x16, waiting for transfers between devices: 81.6 us -> 82.7 us  [swap(): return lax.ppermute(block, 'row', [(i, i ^ distance) for i in range(n_row)])]
  transfers between devices with their start and end apart: 17 -> 20, of which waited for: 7 -> 7; matrix products, arithmetic and copies ran while one was open for 6% -> 7% of each run, Pallas kernels for 22% -> 22%
where the time goes in v6:
time: 277 us; the launch traced here: 276 us
  waiting for transfers between devices  142 us (51%)
  Pallas kernels  62.4 us (23%)
  starting transfers between devices  45.1 us (16%)
  local copies, waits for them, and re-layouts  20.7 us (7%)
  other arithmetic  4.8 us (2%)
    ppermute x16, waiting for transfers between devices, swap(): return lax.ppermute(block, 'row', [(i, i ^ distance) for i in range(n_row)])  82.7 us
    all_to_all x2, waiting for transfers between devices, exchange(): return lax.all_to_all(block, 'row', split_axis=0, concat_axis=0, tiled=True)  59.7 us
    ppermute x16, starting transfers between devices, swap(): return lax.ppermute(block, 'row', [(i, i ^ distance) for i in range(n_row)])  26.1 us
    pallas_call x2, Pallas kernels, in_place(): pl.pallas_call(kernel, grid=grid, in_specs=specs + [pl.BlockSpec(memory_s...  16.3 us
    all_to_all x2, starting transfers between devices, exchange(): return lax.all_to_all(block, 'row', split_axis=0, concat_axis=0, tiled=True)  16 us
    pallas_call x1, Pallas kernels, add_nodes(): pl.pallas_call(functools.partial(node_kernel, planes), grid=(total // til...  11.6 us
    pallas_call x1, Pallas kernels, combine(): pl.pallas_call(combine_kernel, grid=(comps, per), in_specs=[here, carrier...  8.44 us
    pallas_call x3, Pallas kernels, placed_combine(): pl.pallas_call(functools.partial(placed_kernel, near, each, planes, comp,...  7.02 us
  transfers between devices with their start and end apart: 20, of which 7 were waited for; matrix products, arithmetic and copies ran while one was open for 7% of the time, Pallas kernels for 22%

profile of v6, /device:TPU:8, one launch (start us, length us, event | category | flops | bytes accessed | tf_op | source)
XLA Modules:
  0.0 275.8 jit_solution(425091582231102492)
XLA Ops:
  0.0 1.0 constant_dynamic-slice_fusion.1
  1.0 1.6 collective-permute-start
  2.7 3.4 %gather_planes.1 = f32[16,1,2,64,512]{4,3,2,1,0:T(8,128)} custom-call(f32[3,16,1,64,512]{4,3,2,1,0:T(8,128)} %bitcast.65), custom_call_target="tpu_custom_call" | custom-call | bytes 8388608 | tf_op jit(solution)/shard_map/gather_planes/pallas_call | solution.py:333
  6.0 6.8 %all-to-all-start = ((f32[16,2,1,64,512]{4,3,2,1,0:T(8,128)}), f32[16,2,1,64,512]{4,3,2,1,0:T(8,128)}, u32[]{:S(2)}, u32[]{:S(2)}) async-start(f32[16,2,1,64,512]{4,3,2,1,0:T(8,128)} %bitcast.77), calls=%async_computation | async-start | bytes 8388608 | tf_op jit(solution)/shard_map/all_to_all | solution.py:402
  12.8 0.0 copy-start.4
  12.8 0.0 copy-start.2
  12.8 5.1 %slice.147 = f32[32,64,512]{2,1,0:T(8,128)} slice(f32[48,64,512]{2,1,0:T(8,128)} %bitcast.66), slice={[0:32], [0:64], [0:512]} | slice | bytes 8388608 | tf_op jit(solution)/shard_map/slice | solution.py:451
  17.9 1.5 collective-permute-start.9
  19.5 1.6 fusion.2
  21.0 0.6 pad_add_fusion.1.place_ref
  21.7 0.0 collective-permute-done.part_ref
  21.7 2.8 %copy-done = f32[3,16,64,512]{3,2,1,0:T(8,128)S(1)} copy-done((f32[3,16,64,512]{3,2,1,0:T(8,128)S(1)}, f32[3,16,64,512]{3,2,1,0:T(8,128)}, u32[]{:S(2)}) %copy-start) | copy-done | bytes 6291480
  24.5 2.5 pack_lots.1
  27.0 0.1 collective-permute-start.1
  27.1 0.7 pad_add_fusion
  27.8 1.5 collective-permute-start.2
  29.3 0.4 collective-permute-start.3
  29.7 21.4 %collective-permute-done.2 = f32[33,8,512]{2,1,0:T(8,128)S(1)} collective-permute-done((f32[33,8,512]{2,1,0:T(8,128)S(1)}, f32[33,8,512]{2,1,0:T(8,128)S(1)}, u32[]{:S(2)}, u32[]{:S(2)}) %collective-permute-start.2) | collective-permute-done | bytes 540704 | tf_op jit(solution)/shard_map/ppermute | solution.py:405
  51.1 16.3 %collective-permute-done.3 = f32[33,8,512]{2,1,0:T(8,128)S(1)} collective-permute-done((f32[33,8,512]{2,1,0:T(8,128)S(1)}, f32[33,8,512]{2,1,0:T(8,128)S(1)}, u32[]{:S(2)}, u32[]{:S(2)}) %collective-permute-start.3) | collective-permute-done | bytes 540704 | tf_op jit(solution)/shard_map/ppermute | solution.py:405
  67.3 0.1 fusion
  67.4 0.6 slice.179
  68.0 4.6 %collective-permute-start.6 = (f32[1,8,128]{2,1,0:T(8,128)}, f32[1,8,128]{2,1,0:T(8,128)S(1)}, u32[]{:S(2)}, u32[]{:S(2)}) collective-permute-start(f32[1,8,128]{2,1,0:T(8,128)} %slice.179), channel_id=1, source_target_pairs={{0,24},{2,26},{4,28},{6,30},{8,16},{10,18},{12,20},{14,22},{16,8},... | collective-permute-start | bytes 12296 | tf_op jit(solution)/shard_map/ppermute | solution.py:405
  72.7 0.1 collective-permute-start.11
  72.9 9.5 %collective-permute-start.7 = (f32[32,8,512]{2,1,0:T(8,128)S(1)}, f32[32,8,512]{2,1,0:T(8,128)S(1)}, u32[]{:S(2)}, u32[]{:S(2)}) collective-permute-start(f32[32,8,512]{2,1,0:T(8,128)S(1)} %pad_maximum_fusion), channel_id=1, source_target_pairs={{0,8},{2,10},{4,12},{6,14},{8,0},{10,2},{12,4},{14,6},{16,24},{18,... | collective-permute-start | bytes 1572872 | tf_op jit(solution)/shard_map/ppermute | solution.py:405
  82.4 2.4 collective-permute-start.10
  84.9 36.2 %all-to-all-done.lines_ref = f32[16,2,1,64,512]{4,3,2,1,0:T(8,128)} async-done(((f32[16,2,1,64,512]{4,3,2,1,0:T(8,128)}), f32[16,2,1,64,512]{4,3,2,1,0:T(8,128)}, u32[]{:S(2)}, u32[]{:S(2)}) %all-to-all-start) | async-done | bytes 4194336 | tf_op jit(solution)/shard_map/all_to_all | solution.py:402
  121.1 6.9 %y_gradient.1 = f32[16,2,1,64,512]{4,3,2,1,0:T(8,128)} custom-call(bf16[1024,1024]{1,0:T(8,128)(2,1)} %op_ref.3, f32[16,2,1,64,512]{4,3,2,1,0:T(8,128)} %all-to-all-done.lines_ref), custom_call_target="tpu_custom_call" | custom-call | flops 2147483648 | bytes 10485760 | tf_op jit(solution)/shard_map/y_gradient/pallas_call | solution.py:29
  128.0 9.2 %all-to-all-start.1 = ((f32[16,2,1,64,512]{4,3,1,2,0:T(8,128)}), f32[16,2,1,64,512]{4,3,1,2,0:T(8,128)}, u32[]{:S(2)}, u32[]{:S(2)}) async-start(f32[16,2,1,64,512]{4,3,1,2,0:T(8,128)} %bitcast.78), calls=%async_computation.1 | async-start | bytes 8388608 | tf_op jit(solution)/shard_map/all_to_all | solution.py:402
  137.3 0.8 pad_maximum_fusion.1.refs_0_
  138.1 0.3 collective-permute-start.4
  138.3 0.8 pad_maximum_fusion.3.refs_3_
  139.2 0.0 collective-permute-done.7.refs_1_
  139.2 3.3 %slice.146 = f32[16,64,512]{2,1,0:T(8,128)} slice(f32[48,64,512]{2,1,0:T(8,128)} %bitcast.67), slice={[32:48], [0:64], [0:512]} | slice | bytes 4194304 | tf_op jit(solution)/shard_map/slice | solution.py:474
  142.5 1.5 collective-permute-start.8
  144.0 10.3 %z_terms.2.refs_4_ = f32[48,64,512]{2,1,0:T(8,128)} custom-call(f32[48,64,512]{2,1,0:T(8,128)} %bitcast.68, f32[48,64,512]{2,1,0:T(8,128)} %bitcast.69, f32[32,64,512]{2,1,0:T(8,128)} %collective-permute-done.9.refs_1_, bf16[512,512]{1,0:T(8,128)(2,1)} %get-tuple-element.50.refs_2_, bf16[512,512]{1,0:T(8,128)(2,1)} %get-tuple-element.49.refs_3_), custom_call_target="tpu_custom_call" | custom-call | flops 2147483648 | bytes 16777216 | tf_op jit(solution)/shard_map/z_terms/pallas_call | solution.py:45
  154.4 0.8 copy-done.8
  155.2 5.5 %placed_gradient.1 = (f32[32,8,512]{2,1,0:T(8,128)}, f32[32,8,512]{2,1,0:T(8,128)}, f32[32,8,512]{2,1,0:T(8,128)}, f32[32,8,512]{2,1,0:T(8,128)}) custom-call(s32[2]{0:T(128)} %pad_add_fusion.1.place_ref, bf16[1024,1024]{1,0:T(8,128)(2,1)} %op_ref.3, f32[32,8,512]{2,1,0:T(8,128)} %pad_maximum_fusion.1.refs_0_, f32[32,8,512]{2,1,0:T(8,128)} %copy-done.7, ...), custom_call_target="tpu_custom_call" | custom-call | flops 53687091200 | bytes 6291456 | tf_op jit(solution)/shard_map/placed_gradient/pallas_call | solution.py:191
  160.7 0.1 collective-permute-start.12
  160.8 1.8 collective-permute-start.13
  162.6 0.0 collective-permute-done.5
  162.6 0.1 collective-permute-start.14
  162.7 1.1 slice_bitcast_fusion.12
  163.9 24.2 %collective-permute-done.13 = f32[32,8,512]{2,1,0:T(8,128)S(1)} collective-permute-done((f32[32,8,512]{2,1,0:T(8,128)}, f32[32,8,512]{2,1,0:T(8,128)S(1)}, u32[]{:S(2)}, u32[]{:S(2)}) %collective-permute-start.13) | collective-permute-done | bytes 524320 | tf_op jit(solution)/shard_map/ppermute | solution.py:405
  188.1 15.3 %collective-permute-done.14 = f32[32,8,512]{2,1,0:T(8,128)S(1)} collective-permute-done((f32[32,8,512]{2,1,0:T(8,128)}, f32[32,8,512]{2,1,0:T(8,128)S(1)}, u32[]{:S(2)}, u32[]{:S(2)}) %collective-permute-start.14) | collective-permute-done | bytes 524320 | tf_op jit(solution)/shard_map/ppermute | solution.py:405
  203.4 0.7 slice_bitcast_fusion
  204.1 0.9 collective-permute-start.15
  205.0 0.9 pad_maximum_fusion.6
  205.9 0.9 collective-permute-start.16
  206.9 1.8 collective-permute-start.17
  208.7 0.1 concatenate.35
  208.7 0.6 slice.141.force_ref
  209.3 0.7 convert_subtract_fusion.node_ref
  210.0 5.9 %z_terms.3.base_ref = f32[48,64,512]{2,1,0:T(8,128)} custom-call(f32[48,64,512]{2,1,0:T(8,128)} %bitcast.70, f32[48,64,512]{2,1,0:T(8,128)} %bitcast.71, f32[16,64,512]{2,1,0:T(8,128)} %collective-permute-done.8.refs_1_, bf16[512,512]{1,0:T(8,128)(2,1)} %get-tuple-element.50.refs_2_, ...), custom_call_target="tpu_custom_call", output_to_operand_aliasing={{}: (5, {})} | custom-call | flops 1073741824 | bytes 8388608 | tf_op jit(solution)/shard_map/z_terms/pallas_call | solution.py:45
  215.9 11.6 %add_nodes.1.base_ref = f32[48,64,512]{2,1,0:T(8,128)} custom-call(s32[3,128]{1,0:T(4,128)} %convert_subtract_fusion.node_ref, f32[3,128]{1,0:T(4,128)} %slice.141.force_ref, f32[48,64,512]{2,1,0:T(8,128)} %z_terms.3.base_ref), custom_call_target="tpu_custom_call", output_to_operand_aliasing={{}: (2, {})} | custom-call | flops 1572864 | bytes 12582912 | tf_op jit(solution)/shard_map/add_nodes/pallas_call | solution.py:119
  227.6 23.5 %all-to-all-done.1 = f32[16,2,1,64,512]{4,3,1,2,0:T(8,128)} async-done(((f32[16,2,1,64,512]{4,3,1,2,0:T(8,128)}), f32[16,2,1,64,512]{4,3,1,2,0:T(8,128)}, u32[]{:S(2)}, u32[]{:S(2)}) %all-to-all-start.1) | async-done | bytes 4194336 | tf_op jit(solution)/shard_map/all_to_all | solution.py:402
  251.1 8.4 %combine.1.base_ref = f32[48,64,512]{2,1,0:T(8,128)} custom-call(f32[48,64,512]{2,1,0:T(8,128)} %add_nodes.1.base_ref, f32[48,64,512]{2,1,0:T(8,128)} %bitcast.72, f32[16,2,64,512]{3,2,1,0:T(8,128)} %bitcast.18.grad_ref), custom_call_target="tpu_custom_call", output_to_operand_aliasing={{}: (0, {})} | custom-call | flops 2097152 | bytes 16777216 | tf_op jit(solution)/shard_map/combine/pallas_call | solution.py:144
  259.5 2.8 %copy-done.1 = f32[3,16,64,512]{3,2,1,0:T(8,128)S(1)} copy-done((f32[3,16,64,512]{3,2,1,0:T(8,128)S(1)}, f32[3,16,64,512]{3,2,1,0:T(8,128)}, u32[]{:S(2)}) %copy-start.1) | copy-done | bytes 6291480
  262.3 2.3 placed_combine.3.base_ref
  264.6 0.0 collective-permute-done.15.grad_ref
  264.6 2.3 placed_combine.4.base_ref
  267.0 0.0 collective-permute-done.16.grad_ref
  267.0 2.4 placed_combine.5
  269.4 5.6 %collective-permute-done.17.grad_ref = f32[4,1,64,512]{3,2,1,0:T(8,128)S(1)} collective-permute-done((f32[4,1,64,512]{3,2,1,0:T(8,128)S(1)}, f32[4,1,64,512]{3,2,1,0:T(8,128)S(1)}, u32[]{:S(2)}, u32[]{:S(2)}) %collective-permute-start.17) | collective-permute-done | bytes 524320 | tf_op jit(solution)/shard_map/ppermute | solution.py:405
  275.0 0.8 final_combine.1
  (44 shorter events, 0.5 us)
Async XLA Ops:
  1.0 20.7 %collective-permute-start = (f32[16,8,512]{2,1,0:T(8,128)S(1)}, f32[16,8,512]{2,1,0:T(8,128)S(1)}, u32[]{:S(2)}, u32[]{:S(2)}) collective-permute-start(f32[16,8,512]{2,1,0:T(8,128)S(1)} %pad_maximum_fusion.8), channel_id=1, source_target_pairs={{0,24},{2,26},{4,28},{6,30},{8,16},{10,18},{12,20},{14,22},{16,8},... | collective-permute-start | bytes 786440 | tf_op jit(solution)/shard_map/ppermute | solution.py:405
  6.0 115.1 %all-to-all-start = ((f32[16,2,1,64,512]{4,3,2,1,0:T(8,128)}), f32[16,2,1,64,512]{4,3,2,1,0:T(8,128)}, u32[]{:S(2)}, u32[]{:S(2)}) async-start(f32[16,2,1,64,512]{4,3,2,1,0:T(8,128)} %bitcast.77), calls=%async_computation | async-start | bytes 8388608 | tf_op jit(solution)/shard_map/all_to_all | solution.py:402
  12.8 6.6 %copy-start.5 = (s32[3,8]{1,0:T(4,128)S(1)}, s32[3,8]{1,0:T(4,128)}, u32[]{:S(2)}) copy-start(s32[3,8]{1,0:T(4,128)} %param.9) | copy-start | bytes 292
  12.8 6.6 %copy-start.4 = (f32[3,8]{1,0:T(4,128)S(1)}, f32[3,8]{1,0:T(4,128)}, u32[]{:S(2)}) copy-start(f32[3,8]{1,0:T(4,128)} %param.8) | copy-start | bytes 292
  12.8 6.6 %copy-start.2 = (bf16[1024,1024]{1,0:T(8,128)(2,1)S(1)}, bf16[1024,1024]{1,0:T(8,128)(2,1)}, u32[]{:S(2)}) copy-start(bf16[1024,1024]{1,0:T(8,128)(2,1)} %param.7) | copy-start | bytes 6291460
  17.9 110.1 %collective-permute-start.9 = (f32[32,64,512]{2,1,0:T(8,128)}, f32[32,64,512]{2,1,0:T(8,128)}, u32[]{:S(2)}, u32[]{:S(2)}) collective-permute-start(f32[32,64,512]{2,1,0:T(8,128)} %slice.147), channel_id=1, source_target_pairs={{0,1},{1,0},{2,3},{3,2},{4,5},{5,4},{6,7},{7,6},{8,9},{9,8},{10,11... | collective-permute-start | bytes 12582920 | tf_op jit(solution)/shard_map/ppermute | solution.py:428
  21.7 2.8 %copy-start = (f32[3,16,64,512]{3,2,1,0:T(8,128)S(1)}, f32[3,16,64,512]{3,2,1,0:T(8,128)}, u32[]{:S(2)}) copy-start(f32[3,16,64,512]{3,2,1,0:T(8,128)} %param.5) | copy-start | bytes 18874372
  27.0 2.7 collective-permute-start.1
  27.8 23.3 %collective-permute-start.2 = (f32[33,8,512]{2,1,0:T(8,128)S(1)}, f32[33,8,512]{2,1,0:T(8,128)S(1)}, u32[]{:S(2)}, u32[]{:S(2)}) collective-permute-start(f32[33,8,512]{2,1,0:T(8,128)S(1)} %get-tuple-element.31), channel_id=1, source_target_pairs={{0,4},{2,6},{4,0},{6,2},{8,12},{10,14},{12,8},{14,10},{16,20},{18,... | collective-permute-start | bytes 1622024 | tf_op jit(solution)/shard_map/ppermute | solution.py:405
  29.3 38.1 %collective-permute-start.3 = (f32[33,8,512]{2,1,0:T(8,128)S(1)}, f32[33,8,512]{2,1,0:T(8,128)S(1)}, u32[]{:S(2)}, u32[]{:S(2)}) collective-permute-start(f32[33,8,512]{2,1,0:T(8,128)S(1)} %get-tuple-element.32), channel_id=1, source_target_pairs={{0,6},{2,4},{4,2},{6,0},{8,14},{10,12},{12,10},{14,8},{16,22},{18,... | collective-permute-start | bytes 1622024 | tf_op jit(solution)/shard_map/ppermute | solution.py:405
  68.0 92.7 %collective-permute-start.6 = (f32[1,8,128]{2,1,0:T(8,128)}, f32[1,8,128]{2,1,0:T(8,128)S(1)}, u32[]{:S(2)}, u32[]{:S(2)}) collective-permute-start(f32[1,8,128]{2,1,0:T(8,128)} %slice.179), channel_id=1, source_target_pairs={{0,24},{2,26},{4,28},{6,30},{8,16},{10,18},{12,20},{14,22},{16,8},... | collective-permute-start | bytes 12296 | tf_op jit(solution)/shard_map/ppermute | solution.py:405
  72.7 65.3 %collective-permute-start.11 = (f32[16,8,512]{2,1,0:T(8,128)S(1)}, f32[16,8,512]{2,1,0:T(8,128)S(1)}, u32[]{:S(2)}, u32[]{:S(2)}) collective-permute-start(f32[16,8,512]{2,1,0:T(8,128)S(1)} %pad_maximum_fusion.9), channel_id=1, source_target_pairs={{0,24},{2,26},{4,28},{6,30},{8,16},{10,18},{12,20},{14,22},{16,8},... | collective-permute-start | bytes 786440 | tf_op jit(solution)/shard_map/ppermute | solution.py:405
  72.9 66.3 %collective-permute-start.7 = (f32[32,8,512]{2,1,0:T(8,128)S(1)}, f32[32,8,512]{2,1,0:T(8,128)S(1)}, u32[]{:S(2)}, u32[]{:S(2)}) collective-permute-start(f32[32,8,512]{2,1,0:T(8,128)S(1)} %pad_maximum_fusion), channel_id=1, source_target_pairs={{0,8},{2,10},{4,12},{6,14},{8,0},{10,2},{12,4},{14,6},{16,24},{18,... | collective-permute-start | bytes 1572872 | tf_op jit(solution)/shard_map/ppermute | solution.py:405
  82.4 71.9 %collective-permute-start.10 = (f32[32,8,512]{2,1,0:T(8,128)S(1)}, f32[32,8,512]{2,1,0:T(8,128)S(1)}, u32[]{:S(2)}, u32[]{:S(2)}) collective-permute-start(f32[32,8,512]{2,1,0:T(8,128)S(1)} %pad_maximum_fusion.2), channel_id=1, source_target_pairs={{0,16},{2,18},{4,20},{6,22},{8,24},{10,26},{12,28},{14,30},{16,0},... | collective-permute-start | bytes 1572872 | tf_op jit(solution)/shard_map/ppermute | solution.py:405
  128.0 34.6 %collective-permute-start.5 = (f32[1,8,128]{2,1,0:T(8,128)}, f32[1,8,128]{2,1,0:T(8,128)S(1)}, u32[]{:S(2)}, u32[]{:S(2)}) collective-permute-start(f32[1,8,128]{2,1,0:T(8,128)} %slice.179), channel_id=1, source_target_pairs={{0,16},{2,18},{4,20},{6,22},{8,24},{10,26},{12,28},{14,30},{16,0},... | collective-permute-start | bytes 12296 | tf_op jit(solution)/shard_map/ppermute | solution.py:405
  128.0 123.1 %all-to-all-start.1 = ((f32[16,2,1,64,512]{4,3,1,2,0:T(8,128)}), f32[16,2,1,64,512]{4,3,1,2,0:T(8,128)}, u32[]{:S(2)}, u32[]{:S(2)}) async-start(f32[16,2,1,64,512]{4,3,1,2,0:T(8,128)} %bitcast.78), calls=%async_computation.1 | async-start | bytes 8388608 | tf_op jit(solution)/shard_map/all_to_all | solution.py:402
  138.1 70.6 %collective-permute-start.4 = (f32[1,8,128]{2,1,0:T(8,128)}, f32[1,8,128]{2,1,0:T(8,128)S(1)}, u32[]{:S(2)}, u32[]{:S(2)}) collective-permute-start(f32[1,8,128]{2,1,0:T(8,128)} %slice.179), channel_id=1, source_target_pairs={{0,8},{2,10},{4,12},{6,14},{8,0},{10,2},{12,4},{14,6},{16,24},{18,... | collective-permute-start | bytes 12296 | tf_op jit(solution)/shard_map/ppermute | solution.py:405
  139.2 15.2 %copy-start.7 = (f32[32,8,512]{2,1,0:T(8,128)}, f32[32,8,512]{2,1,0:T(8,128)S(1)}, u32[]{:S(2)}) copy-start(f32[32,8,512]{2,1,0:T(8,128)S(1)} %collective-permute-done.7.refs_1_) | copy-start | bytes 1572868
  142.5 67.5 %collective-permute-start.8 = (f32[16,64,512]{2,1,0:T(8,128)}, f32[16,64,512]{2,1,0:T(8,128)}, u32[]{:S(2)}, u32[]{:S(2)}) collective-permute-start(f32[16,64,512]{2,1,0:T(8,128)} %slice.146), channel_id=1, source_target_pairs={{0,1},{1,0},{2,3},{3,2},{4,5},{5,4},{6,7},{7,6},{8,9},{9,8},{10,11... | collective-permute-start | bytes 6291464 | tf_op jit(solution)/shard_map/ppermute | solution.py:428
  154.4 0.8 copy-start.8
  160.7 48.7 %copy-start.6 = (s32[3]{0:T(128)S(1)}, s32[3]{0:T(128)}, u32[]{:S(2)}) copy-start(s32[3]{0:T(128)} %pad_add_fusion) | copy-start | bytes 40
  160.7 3.2 %collective-permute-start.12 = (f32[32,8,512]{2,1,0:T(8,128)}, f32[32,8,512]{2,1,0:T(8,128)S(1)}, u32[]{:S(2)}, u32[]{:S(2)}) collective-permute-start(f32[32,8,512]{2,1,0:T(8,128)} %get-tuple-element.41), channel_id=1, source_target_pairs={{0,2},{2,0},{4,6},{6,4},{8,10},{10,8},{12,14},{14,12},{16,18},{18,... | collective-permute-start | bytes 1572872 | tf_op jit(solution)/shard_map/ppermute | solution.py:405
  160.8 27.3 %collective-permute-start.13 = (f32[32,8,512]{2,1,0:T(8,128)}, f32[32,8,512]{2,1,0:T(8,128)S(1)}, u32[]{:S(2)}, u32[]{:S(2)}) collective-permute-start(f32[32,8,512]{2,1,0:T(8,128)} %get-tuple-element.42), channel_id=1, source_target_pairs={{0,4},{2,6},{4,0},{6,2},{8,12},{10,14},{12,8},{14,10},{16,20},{18,... | collective-permute-start | bytes 1572872 | tf_op jit(solution)/shard_map/ppermute | solution.py:405
  162.6 40.8 %collective-permute-start.14 = (f32[32,8,512]{2,1,0:T(8,128)}, f32[32,8,512]{2,1,0:T(8,128)S(1)}, u32[]{:S(2)}, u32[]{:S(2)}) collective-permute-start(f32[32,8,512]{2,1,0:T(8,128)} %get-tuple-element.43), channel_id=1, source_target_pairs={{0,6},{2,4},{4,2},{6,0},{8,14},{10,12},{12,10},{14,8},{16,22},{18,... | collective-permute-start | bytes 1572872 | tf_op jit(solution)/shard_map/ppermute | solution.py:405
  204.1 60.5 %collective-permute-start.15 = (f32[4,1,64,512]{3,2,1,0:T(8,128)S(1)}, f32[4,1,64,512]{3,2,1,0:T(8,128)S(1)}, u32[]{:S(2)}, u32[]{:S(2)}) collective-permute-start(f32[4,1,64,512]{3,2,1,0:T(8,128)S(1)} %pad_maximum_fusion.5), channel_id=1, source_target_pairs={{0,8},{2,10},{4,12},{6,14},{8,0},{10,2},{12,4},{14,6},{16,24},{18,... | collective-permute-start | bytes 1572872 | tf_op jit(solution)/shard_map/ppermute | solution.py:405
  205.9 61.0 %collective-permute-start.16 = (f32[4,1,64,512]{3,2,1,0:T(8,128)}, f32[4,1,64,512]{3,2,1,0:T(8,128)S(1)}, u32[]{:S(2)}, u32[]{:S(2)}) collective-permute-start(f32[4,1,64,512]{3,2,1,0:T(8,128)} %pad_maximum_fusion.6), channel_id=1, source_target_pairs={{0,16},{2,18},{4,20},{6,22},{8,24},{10,26},{12,28},{14,30},{16,0},... | collective-permute-start | bytes 1572872 | tf_op jit(solution)/shard_map/ppermute | solution.py:405
  206.9 68.1 %collective-permute-start.17 = (f32[4,1,64,512]{3,2,1,0:T(8,128)S(1)}, f32[4,1,64,512]{3,2,1,0:T(8,128)S(1)}, u32[]{:S(2)}, u32[]{:S(2)}) collective-permute-start(f32[4,1,64,512]{3,2,1,0:T(8,128)S(1)} %pad_maximum_fusion.7), channel_id=1, source_target_pairs={{0,24},{2,26},{4,28},{6,30},{8,16},{10,18},{12,20},{14,22},{16,8},... | collective-permute-start | bytes 1572872 | tf_op jit(solution)/shard_map/ppermute | solution.py:405
  215.9 11.6 %copy-start.3 = (f32[1,1,64,512]{3,2,1,0:T(8,128)S(1)}, f32[1,1,64,512]{3,2,1,0:T(8,128)}, u32[]{:S(2)}) copy-start(f32[1,1,64,512]{3,2,1,0:T(8,128)} %get-tuple-element.82) | copy-start | bytes 393220
  259.5 2.8 %copy-start.1 = (f32[3,16,64,512]{3,2,1,0:T(8,128)S(1)}, f32[3,16,64,512]{3,2,1,0:T(8,128)}, u32[]{:S(2)}) copy-start(f32[3,16,64,512]{3,2,1,0:T(8,128)} %param.5) | copy-start | bytes 18874372
